TPU v7x, 128 devices: a whole 4x4x4 slice. The times are simulated.
128 devices in a mesh: section: 4 (over y), dp: 32 (over z, x, core).
Axes of the slice: x: 4, y: 4, z: 4, core: 2. Of those that a mesh axis runs over, the one named last changes fastest.
Arguments:
- features: bfloat16 [2, 32768, 512], P(None, 'dp'), may hold values from -6 to 6
- w_self: bfloat16 [4, 512, 512], P('section'), may hold values from -0.25 to 0.25
- w_neigh: bfloat16 [4, 512, 512], P('section'), may hold values from -0.75 to 0.75
- bias: float32 [4, 512], P('section'), may hold values from -3 to 3
- gain: float32 [4, 512], P('section'), may hold values from 0.5 to 1.5
- hubs: int32 [2, 32, 32], P(None, None, 'dp'), may hold values from -1 to 7, as said below
- tile_src: int32 [2, 256, 6], P(None, 'dp'), may hold values from 0 to 39, as said below
- counts: int32 [2, 256, 6, 128, 128], P(None, 'dp'), may hold values from 0 to 2, as said below
Outputs:
- acts: bfloat16 [4, 2, 32768, 512], P('section', None, 'dp')
Inputs may be any that keep to these rules, and one draw needn't show every extreme that they name: hubs[m, r, r] = -1; hubs[m, r, (r + 1) % 32] is never -1; other entries are -1 or a block index of partition q. `tile_src`: a slot 8 + q appears only where hubs[m, p, q] is not -1 for the tile's partition p. `counts`: some vertices have no edges at all.
All inputs are finite; a program needn't handle non-finite values.
Results may differ from a plain program's by a relative error of at most 0.007.
Values may be sent and summed in bfloat16 or wider, within the bound.
No kernel may reach another device: no remote copies, remote signals or barrier semaphores. Data moves between devices by JAX's collectives and lax.ppermute only.
A program may use at most 128 MiB of HBM per device.

v0:
```python
import jax
import jax.numpy as jnp
from jax import lax
from jax.sharding import PartitionSpec as P


def passed_along(value, axis, by):
    devices = lax.axis_size(axis)
    pairs = [(i, i + by) for i in range(devices) if 0 <= i + by < devices]
    return lax.ppermute(value, axis, pairs)


def sage_layer(layer_in, hub_rows, tile_slots, tile_counts, w_self, w_neigh, bias, gain):
    batch = layer_in.shape[0]
    width = layer_in.shape[2]
    block_rows = tile_counts.shape[3]
    n_blocks = tile_slots.shape[1]
    blocks = layer_in.reshape(batch, n_blocks, block_rows, width)
    clipped = jnp.clip(hub_rows, 0, n_blocks - 1)
    picked = jax.vmap(lambda source, chosen: source[chosen])(blocks, clipped)
    outgoing = jnp.where((hub_rows >= 0)[:, :, None, None], picked, jnp.zeros_like(picked))
    received = lax.all_to_all(outgoing, "dp", split_axis=1, concat_axis=1, tiled=True)
    slot_table = jnp.concatenate([blocks, received], axis=1)
    gathered = jax.vmap(lambda source, chosen: source[chosen])(slot_table, tile_slots)
    summed = jnp.einsum(
        "gbjvu,gbjud->gbvd",
        tile_counts.astype(jnp.bfloat16),
        gathered,
        preferred_element_type=jnp.float32,
    )
    degree = jnp.sum(tile_counts, axis=(2, 4)).astype(jnp.float32)
    neighbor_mean = (summed / jnp.maximum(degree, 1.0)[..., None]).astype(jnp.bfloat16)
    neighbor_mean = neighbor_mean.reshape(layer_in.shape)
    pre_norm = jnp.einsum("grd,de->gre", layer_in, w_self[0], preferred_element_type=jnp.float32)
    pre_norm = pre_norm + jnp.einsum(
        "grd,de->gre", neighbor_mean, w_neigh[0], preferred_element_type=jnp.float32
    )
    pre_norm = pre_norm + bias[0]
    row_mean = jnp.mean(pre_norm, axis=-1, keepdims=True)
    row_var = jnp.mean((pre_norm - row_mean) ** 2, axis=-1, keepdims=True)
    normed = (pre_norm - row_mean) * lax.rsqrt(row_var + 1e-05) * gain[0]
    return jnp.maximum(normed, 0.0).astype(jnp.bfloat16)


def body(features, w_self, w_neigh, bias, gain, hubs, tile_src, counts):
    section_idx = lax.axis_index("section")
    n_sections = lax.axis_size("section")
    hub_rows = hubs[:, :, 0]
    results = jnp.zeros_like(features)
    incoming = features
    for turn_idx in range(n_sections):
        layer_in = jnp.where(section_idx == 0, features, incoming)
        layer_out = sage_layer(layer_in, hub_rows, tile_src, counts, w_self, w_neigh, bias, gain)
        results = jnp.where(section_idx == turn_idx, layer_out, results)
        if turn_idx + 1 < n_sections:
            incoming = passed_along(layer_out, "section", 1)
    return results[None]


def solution(mesh):
    placed = (
        P(None, "dp", None),
        P("section", None, None),
        P("section", None, None),
        P("section", None),
        P("section", None),
        P(None, None, "dp"),
        P(None, "dp", None),
        P(None, "dp", None, None, None),
    )
    return jax.shard_map(
        body, mesh=mesh, in_specs=placed, out_specs=P("section", None, "dp", None), check_vma=False
    )
```

profile of v0, /device:TPU:24, one launch (start us, length us, event | category | flops | bytes accessed | tf_op | source)
XLA Modules:
  0.0 775.0 jit_solution(5003515633899818269)
XLA Ops:
  1.6 7.4 gather_fusion
  9.1 7.2 copy_select_fusion.3
  16.3 8.4 %all-to-all-start = ((bf16[2,32,128,512]{3,2,0,1:T(8,128)(2,1)}), bf16[2,32,128,512]{3,2,0,1:T(8,128)(2,1)}, u32[]{:S(2)}, u32[]{:S(2)}) async-start(bf16[2,32,128,512]{3,2,0,1:T(8,128)(2,1)} %copy_select_fusion.3), calls=%async_computation | async-start | bytes 16777216 | tf_op jit(solution)/shard_map/all_to_all | solution.py:22
  24.9 7.5 fusion.26
  35.8 94.8 %all-to-all-done = bf16[2,32,128,512]{3,2,0,1:T(8,128)(2,1)} async-done(((bf16[2,32,128,512]{3,2,0,1:T(8,128)(2,1)}), bf16[2,32,128,512]{3,2,0,1:T(8,128)(2,1)}, u32[]{:S(2)}, u32[]{:S(2)}) %all-to-all-start) | async-done | bytes 8388640 | tf_op jit(solution)/shard_map/all_to_all | solution.py:22
  130.6 8.8 %pad_maximum_fusion = bf16[2,40,128,512]{3,2,1,0:T(8,128)(2,1)} fusion(bf16[2,8,128,512]{3,2,1,0:T(8,128)(2,1)S(1)} %bitcast.110, bf16[2,32,128,512]{3,2,0,1:T(8,128)(2,1)} %all-to-all-done), kind=kLoop, calls=%fused_computation.8 | loop fusion | flops 20971520 | bytes 20971520 | tf_op jit(solution)/shard_map/concatenate | solution.py:23
  139.4 11.2 %gather_fusion.1 = bf16[96,128,512]{2,1,0:T(8,128)(2,1)} fusion(bf16[2,40,128,512]{3,2,1,0:T(8,128)(2,1)} %pad_maximum_fusion, s32[96]{0:T(128)S(1)} %reshape.99), kind=kCustom, calls=%fused_computation.1 | custom fusion | bytes 25166592 | tf_op jit(solution)/shard_map/vmap()/gather | solution.py:24
  150.6 7.6 fusion.3
  166.2 39.9 %collective-permute-done = bf16[2,1024,512]{1,2,0:T(8,128)(2,1)} collective-permute-done((bf16[2,1024,512]{1,2,0:T(8,128)(2,1)}, bf16[2,1024,512]{1,2,0:T(8,128)(2,1)}, u32[]{:S(2)}, u32[]{:S(2)}) %collective-permute-start) | collective-permute-done | bytes 2097184 | tf_op jit(solution)/shard_map/ppermute | solution.py:10
  217.9 7.2 copy_select_fusion.2
  225.1 103.3 %all_to_all.20 = bf16[2,32,128,512]{3,2,0,1:T(8,128)(2,1)S(1)} all-to-all(bf16[2,32,128,512]{3,2,0,1:T(8,128)(2,1)} %copy_select_fusion.2), channel_id=1, replica_groups=mesh['section'=4,'dp'=32] {'dp'}, dimensions={1} | all-to-all | bytes 16777216 | tf_op jit(solution)/shard_map/all_to_all | solution.py:22
  335.1 11.2 %gather_fusion.3 = bf16[96,128,512]{2,1,0:T(8,128)(2,1)} fusion(bf16[2,40,128,512]{3,2,1,0:T(8,128)(2,1)} %pad_maximum_fusion.1, s32[96]{0:T(128)S(1)} %reshape.99), kind=kCustom, calls=%fused_computation.3 | custom fusion | bytes 25166592 | tf_op jit(solution)/shard_map/vmap()/gather | solution.py:24
  346.3 7.4 fusion.2
  360.6 48.0 %collective-permute-done.1 = bf16[2,1024,512]{1,2,0:T(8,128)(2,1)S(1)} collective-permute-done((bf16[2,1024,512]{1,2,0:T(8,128)(2,1)S(1)}, bf16[2,1024,512]{1,2,0:T(8,128)(2,1)S(1)}, u32[]{:S(2)}, u32[]{:S(2)}) %collective-permute-start.1) | collective-permute-done | bytes 2097184 | tf_op jit(solution)/shard_map/ppermute | solution.py:10
  418.8 7.2 copy_select_fusion.1
  426.0 100.6 %all_to_all.21 = bf16[2,32,128,512]{3,2,0,1:T(8,128)(2,1)S(1)} all-to-all(bf16[2,32,128,512]{3,2,0,1:T(8,128)(2,1)} %copy_select_fusion.1), channel_id=1, replica_groups=mesh['section'=4,'dp'=32] {'dp'}, dimensions={1} | all-to-all | bytes 16777216 | tf_op jit(solution)/shard_map/all_to_all | solution.py:22
  533.3 11.2 %gather_fusion.5 = bf16[96,128,512]{2,1,0:T(8,128)(2,1)} fusion(bf16[2,40,128,512]{3,2,1,0:T(8,128)(2,1)} %pad_maximum_fusion.2, s32[96]{0:T(128)S(1)} %reshape.99), kind=kCustom, calls=%fused_computation.5 | custom fusion | bytes 25166592 | tf_op jit(solution)/shard_map/vmap()/gather | solution.py:24
  544.5 7.4 fusion.1
  558.7 48.0 %collective-permute-done.2 = bf16[2,1024,512]{1,2,0:T(8,128)(2,1)S(1)} collective-permute-done((bf16[2,1024,512]{1,2,0:T(8,128)(2,1)S(1)}, bf16[2,1024,512]{1,2,0:T(8,128)(2,1)S(1)}, u32[]{:S(2)}, u32[]{:S(2)}) %collective-permute-start.2) | collective-permute-done | bytes 2097184 | tf_op jit(solution)/shard_map/ppermute | solution.py:10
  616.9 7.2 copy_select_fusion
  629.1 105.9 %all-to-all-done.3 = bf16[2,32,128,512]{3,2,0,1:T(8,128)(2,1)} async-done(((bf16[2,32,128,512]{3,2,0,1:T(8,128)(2,1)}), bf16[2,32,128,512]{3,2,0,1:T(8,128)(2,1)}, u32[]{:S(2)}, u32[]{:S(2)}) %all-to-all-start.3) | async-done | bytes 8388640 | tf_op jit(solution)/shard_map/all_to_all | solution.py:22
  735.0 8.8 %pad_maximum_fusion.3 = bf16[2,40,128,512]{3,2,1,0:T(8,128)(2,1)} fusion(bf16[2,8,128,512]{3,2,1,0:T(8,128)(2,1)S(1)} %bitcast.112, bf16[2,32,128,512]{3,2,0,1:T(8,128)(2,1)} %all-to-all-done.3), kind=kLoop, calls=%fused_computation.11 | loop fusion | flops 20971520 | bytes 20971520 | tf_op jit(solution)/shard_map/concatenate | solution.py:23
  743.8 11.2 %gather_fusion.7 = bf16[96,128,512]{2,1,0:T(8,128)(2,1)} fusion(bf16[2,40,128,512]{3,2,1,0:T(8,128)(2,1)} %pad_maximum_fusion.3, s32[96]{0:T(128)S(1)} %reshape.99), kind=kCustom, calls=%fused_computation.7 | custom fusion | bytes 25166592 | tf_op jit(solution)/shard_map/vmap()/gather | solution.py:24
  754.9 7.4 fusion
  (85 shorter events, 89.4 us)
Async XLA Ops:
  0.0 32.5 %copy-start = (bf16[1,512,512]{2,1,0:T(8,128)(2,1)S(1)}, bf16[1,512,512]{2,1,0:T(8,128)(2,1)}, u32[]{:S(2)}) copy-start(bf16[1,512,512]{2,1,0:T(8,128)(2,1)} %param.9) | copy-start | bytes 1572868
  16.3 8.4 %copy-start.17 = (s32[2,8,6]{1,0,2:T(2,128)S(1)}, s32[2,8,6]{1,0,2:T(2,128)}, u32[]{:S(2)}) copy-start(s32[2,8,6]{1,0,2:T(2,128)} %param.14) | copy-start | bytes 1156
  16.3 114.3 %all-to-all-start = ((bf16[2,32,128,512]{3,2,0,1:T(8,128)(2,1)}), bf16[2,32,128,512]{3,2,0,1:T(8,128)(2,1)}, u32[]{:S(2)}, u32[]{:S(2)}) async-start(bf16[2,32,128,512]{3,2,0,1:T(8,128)(2,1)} %copy_select_fusion.3), calls=%async_computation | async-start | bytes 16777216 | tf_op jit(solution)/shard_map/all_to_all | solution.py:22
  24.9 7.6 copy-start.1
  150.6 7.6 copy-start.13
  150.6 7.6 copy-start.14
  150.6 7.6 copy-start.15
  159.7 2.7 copy-start.2
  159.7 0.7 copy-start.16
  162.4 43.7 %collective-permute-start = (bf16[2,1024,512]{1,2,0:T(8,128)(2,1)}, bf16[2,1024,512]{1,2,0:T(8,128)(2,1)}, u32[]{:S(2)}, u32[]{:S(2)}) collective-permute-start(bf16[2,1024,512]{1,2,0:T(8,128)(2,1)} %maximum_convert_fusion.3), channel_id=1, source_target_pairs={{0,32},{32,64},{64,96},{1,33},{33,65},{65,97},{2,34},{34,66},{66,9... | collective-permute-start | bytes 6291464 | tf_op jit(solution)/shard_map/ppermute | solution.py:10
  353.8 1.6 copy-start.11
  356.9 2.1 copy-start.4
  357.4 51.2 %copy-start.8 = (bf16[2,1024,512]{1,2,0:T(8,128)(2,1)S(1)}, bf16[2,1024,512]{1,2,0:T(8,128)(2,1)}, u32[]{:S(2)}) copy-start(bf16[2,1024,512]{1,2,0:T(8,128)(2,1)} %copy.74) | copy-start | bytes 6291460
  359.0 49.6 %collective-permute-start.1 = (bf16[2,1024,512]{1,2,0:T(8,128)(2,1)S(1)}, bf16[2,1024,512]{1,2,0:T(8,128)(2,1)S(1)}, u32[]{:S(2)}, u32[]{:S(2)}) collective-permute-start(bf16[2,1024,512]{1,2,0:T(8,128)(2,1)S(1)} %maximum_convert_fusion.2), channel_id=1, source_target_pairs={{0,32},{32,64},{64,96},{1,33},{33,65},{65,97},{2,34},{34,66},{66,9... | collective-permute-start | bytes 6291464 | tf_op jit(solution)/shard_map/ppermute | solution.py:10
  551.9 1.6 copy-start.12
  555.1 2.0 copy-start.6
  555.6 51.1 %copy-start.9 = (bf16[2,1024,512]{1,2,0:T(8,128)(2,1)S(1)}, bf16[2,1024,512]{1,2,0:T(8,128)(2,1)}, u32[]{:S(2)}) copy-start(bf16[2,1024,512]{1,2,0:T(8,128)(2,1)} %copy.74) | copy-start | bytes 6291460
  557.0 49.6 %collective-permute-start.2 = (bf16[2,1024,512]{1,2,0:T(8,128)(2,1)S(1)}, bf16[2,1024,512]{1,2,0:T(8,128)(2,1)S(1)}, u32[]{:S(2)}, u32[]{:S(2)}) collective-permute-start(bf16[2,1024,512]{1,2,0:T(8,128)(2,1)S(1)} %maximum_convert_fusion.1), channel_id=1, source_target_pairs={{0,32},{32,64},{64,96},{1,33},{33,65},{65,97},{2,34},{34,66},{66,9... | collective-permute-start | bytes 6291464 | tf_op jit(solution)/shard_map/ppermute | solution.py:10
  624.1 110.8 %all-to-all-start.3 = ((bf16[2,32,128,512]{3,2,0,1:T(8,128)(2,1)}), bf16[2,32,128,512]{3,2,0,1:T(8,128)(2,1)}, u32[]{:S(2)}, u32[]{:S(2)}) async-start(bf16[2,32,128,512]{3,2,0,1:T(8,128)(2,1)} %copy_select_fusion), calls=%async_computation.3 | async-start | bytes 16777216 | tf_op jit(solution)/shard_map/all_to_all | solution.py:22
  762.4 1.6 copy-start.10
  764.0 2.2 copy-start.5
  764.0 3.5 copy-start.7
  765.5 3.4 copy-start.3
where the time goes:
time: 784 us; the launch traced here: 775 us
  waiting for transfers between devices  336 us (43%)
  blocking collectives  204 us (26%)
  local copies, waits for them, and re-layouts  88.7 us (11%)
  other arithmetic  83.7 us (11%)
  matrix products  43.3 us (6%)
  starting transfers between devices  18.1 us (2%)
    all_to_all x2, blocking collectives, sage_layer(): lax.all_to_all(outgoing, 'dp', split_axis=1, concat_axis=1, tiled=True)  204 us
    all_to_all x2, waiting for transfers between devices, sage_layer(): lax.all_to_all(outgoing, 'dp', split_axis=1, concat_axis=1, tiled=True)  201 us
    ppermute x3, waiting for transfers between devices, passed_along(): return lax.ppermute(value, axis, pairs)  136 us
    gather x6, local copies, waits for them, and re-layouts, sage_layer(): source[chosen]  44.8 us
    concatenate x4, other arithmetic, sage_layer(): slot_table = jnp.concatenate([blocks, received], axis=1)  31.1 us
    dot_general x4, matrix products, sage_layer(): jnp.einsum('gbjvu,gbjud->gbvd', tile_counts.astype(jnp.bfloat16), gathere...  29.9 us
    select_n x4, other arithmetic, sage_layer(): jnp.where((hub_rows >= 0)[:, :, None, None], picked, jnp.zeros_like(picked))  28.8 us
    gather x5, local copies, waits for them, and re-layouts, sage_layer(): picked = jax.vmap(lambda source, chosen: source[chosen])(blocks, clipped)  25 us
  transfers between devices with their start and end apart: 5, of which 5 were waited for; matrix products, arithmetic and copies ran while one was open for 2% of the time, Pallas kernels for 0%

commit v1 on v0

v1 whole, which is shorter than its diff:
```python
import functools

import jax
import jax.numpy as jnp
from jax import lax
from jax.experimental import pallas as pl
from jax.experimental.pallas import tpu as pltpu
from jax.sharding import Mesh, PartitionSpec as P

SECTION = ("sm", "se")
PARTS = ("dk", "dc")
VMEM_BYTES = 40 * 1024 * 1024
HBM = pltpu.HBM


def params():
    return pltpu.CompilerParams(vmem_limit_bytes=VMEM_BYTES)


def start_picks(meta, source, outgoing, sems):
    n_dest = outgoing.shape[0]
    half = n_dest // 2
    for j in range(n_dest):
        reader = 2 * (j % half) + j // half
        block = jnp.maximum(meta[reader], 0)
        pltpu.make_async_copy(source.at[block], outgoing.at[j], sems.at[j]).start()


def wait_picks(source, outgoing, sems):
    for j in range(outgoing.shape[0]):
        pltpu.make_async_copy(source.at[0], outgoing.at[j], sems.at[j]).wait()


def pick_kernel(meta, source, outgoing, sems):
    start_picks(meta, source, outgoing, sems)
    wait_picks(source, outgoing, sems)


def pick(meta, own):
    n_dest = meta.shape[0] - 48
    return pl.pallas_call(
        pick_kernel,
        out_shape=jax.ShapeDtypeStruct((n_dest,) + own.shape[1:], own.dtype),
        in_specs=[
            pl.BlockSpec(memory_space=pltpu.SMEM),
            pl.BlockSpec(memory_space=pltpu.VMEM),
        ],
        out_specs=pl.BlockSpec(memory_space=HBM),
        scratch_shapes=[pltpu.SemaphoreType.DMA((n_dest,))],
        compiler_params=params(),
        name="pick",
    )(meta, own)


def aggregate_kernel(n_hubs, meta, own, received, counts, inverse, out, table, held, table_sems, count_sems):
    n_blocks, tiles = own.shape[0], 6
    own_copy = pltpu.make_async_copy(own, table.at[pl.ds(0, n_blocks)], table_sems.at[0])
    hub_copy = pltpu.make_async_copy(received, table.at[pl.ds(n_blocks, n_hubs)], table_sems.at[1])
    hub_copy.start()
    own_copy.start()
    count_copies = [
        pltpu.make_async_copy(counts.at[b], held.at[b], count_sems.at[b]) for b in range(n_blocks)
    ]
    for copy in count_copies:
        copy.start()
    own_copy.wait()
    hub_copy.wait()
    width = out.shape[-1]
    for b in range(n_blocks):
        count_copies[b].wait()
        picked = []
        for j in range(tiles):
            slot = meta[n_hubs + b * tiles + j]
            owner = slot - n_blocks
            place = jnp.where(
                slot < n_blocks, slot, n_blocks + lax.rem(owner, 2) * (n_hubs // 2) + lax.div(owner, 2)
            )
            picked.append(table[place])
        summed = jnp.dot(held[b], jnp.concatenate(picked, axis=0), preferred_element_type=jnp.float32)
        scale = inverse[b]
        scale = jnp.concatenate([scale] * (width // scale.shape[-1]), axis=-1)
        out[b] = (summed * scale).astype(out.dtype)


def aggregate(meta, own, received, counts, inverse):
    n_hubs = received.shape[0]
    n_blocks, rows, width = own.shape
    return pl.pallas_call(
        functools.partial(aggregate_kernel, n_hubs),
        out_shape=jax.ShapeDtypeStruct(own.shape, own.dtype),
        in_specs=[
            pl.BlockSpec(memory_space=pltpu.SMEM),
            pl.BlockSpec(memory_space=HBM),
            pl.BlockSpec(memory_space=HBM),
            pl.BlockSpec(memory_space=HBM),
            pl.BlockSpec(memory_space=pltpu.VMEM),
        ],
        out_specs=pl.BlockSpec(memory_space=pltpu.VMEM),
        scratch_shapes=[
            pltpu.VMEM((n_blocks + n_hubs, rows, width), own.dtype),
            pltpu.VMEM(counts.shape, counts.dtype),
            pltpu.SemaphoreType.DMA((2,)),
            pltpu.SemaphoreType.DMA((n_blocks,)),
        ],
        compiler_params=params(),
        name="aggregate",
    )(meta, own, received, counts, inverse)


def dense_kernel(last, place, meta, h, mean_mine, mean_other, w_mine, w_other, affine, *rest):
    if last:
        h_out, weights, w_sems = rest
    else:
        h_out, own_out, outgoing, weights, w_sems, pick_sems = rest
    rel, core = place[0], place[1]
    width = h.shape[-1]
    half = width // 2
    mine_cols = pl.ds(core * half, half)
    other_cols = pl.ds((1 - core) * half, half)

    def copies(self_source, neigh_source):
        return [
            pltpu.make_async_copy(self_source.at[rel], weights.at[pl.ds(0, width)], w_sems.at[0]),
            pltpu.make_async_copy(
                neigh_source.at[rel, mine_cols], weights.at[pl.ds(width, half)], w_sems.at[1]
            ),
            pltpu.make_async_copy(
                neigh_source.at[rel, other_cols], weights.at[pl.ds(width + half, half)], w_sems.at[2]
            ),
        ]

    @pl.when(core == 0)
    def _():
        for copy in copies(w_mine, w_other):
            copy.start()

    @pl.when(core != 0)
    def _():
        for copy in copies(w_other, w_mine):
            copy.start()

    for copy in copies(w_mine, w_other):
        copy.wait()
    n_blocks, rows = mean_mine.shape[0], mean_mine.shape[1]
    bias, gain = affine[0:1, :], affine[1:2, :]
    for b in range(n_blocks):
        chunk = pl.ds(b * rows, rows)
        pre = jnp.dot(h[chunk, :], weights[0:width], preferred_element_type=jnp.float32)
        means = jnp.concatenate([mean_mine[b], mean_other[b]], axis=-1)
        pre = pre + jnp.dot(means, weights[width : 2 * width], preferred_element_type=jnp.float32)
        pre = pre + bias
        mu = jnp.mean(pre, axis=-1, keepdims=True)
        centred = pre - mu
        var = jnp.mean(centred * centred, axis=-1, keepdims=True)
        normed = centred * lax.rsqrt(var + 1e-05) * gain
        value = jnp.maximum(normed, 0.0).astype(h_out.dtype)
        h_out[chunk, :] = value
        if not last:
            own_out[b] = jnp.where(core == 0, value[:, :half], value[:, half:])
    if not last:
        start_picks(meta, own_out, outgoing, pick_sems)
        wait_picks(own_out, outgoing, pick_sems)


def dense(last, n_hubs, place, meta, h, mean_mine, mean_other, w_mine, w_other, affine):
    rows, width = h.shape
    vmem, smem, hbm = (pl.BlockSpec(memory_space=s) for s in (pltpu.VMEM, pltpu.SMEM, HBM))
    out_shape = [jax.ShapeDtypeStruct(h.shape, h.dtype)]
    out_specs = [vmem]
    scratch = [pltpu.VMEM((2 * width, width), h.dtype), pltpu.SemaphoreType.DMA((3,))]
    if not last:
        out_shape += [
            jax.ShapeDtypeStruct(mean_mine.shape, h.dtype),
            jax.ShapeDtypeStruct((n_hubs,) + mean_mine.shape[1:], h.dtype),
        ]
        out_specs += [vmem, hbm]
        scratch.append(pltpu.SemaphoreType.DMA((n_hubs,)))
    return pl.pallas_call(
        functools.partial(dense_kernel, last),
        out_shape=out_shape,
        in_specs=[smem, smem, vmem, vmem, vmem, hbm, hbm, vmem],
        out_specs=out_specs,
        scratch_shapes=scratch,
        compiler_params=params(),
        name="dense",
    )(place, meta, h, mean_mine, mean_other, w_mine, w_other, affine)


def swap(value):
    return lax.ppermute(value, "dc", [(0, 1), (1, 0)])


def around(value, by):
    n = lax.axis_size("sm") * lax.axis_size("se")
    return lax.ppermute(value, SECTION, [(i, (i + by) % n) for i in range(n)])


def to_layer(value, layer, graph):
    pairs = [((2 * graph + e) * 2 + e, 2 * layer + e) for e in range(2)]
    return lax.ppermute(value, ("sm", "se", "dc"), pairs)


def body(features, w_self, w_neigh, bias, gain, hubs, tile_src, counts):
    graph, parity = lax.axis_index("sm"), lax.axis_index("se")
    core = lax.axis_index("dc")
    section = 2 * graph + parity
    here = core == parity
    n_layers = 4
    n_blocks, tiles, rows = tile_src.shape[1], tile_src.shape[2], counts.shape[3]
    width = features.shape[2]
    half = width // 2
    n_hubs = hubs.shape[1]

    weight = jnp.where(core == 0, w_self[0], w_neigh[0])
    from_prev, from_next = around(weight, 1), around(weight, -1)

    feats = lax.dynamic_index_in_dim(features, graph, 0, keepdims=False)
    mine = lax.dynamic_slice_in_dim(feats, core * half, half, 1)
    for_other = lax.dynamic_slice_in_dim(feats, (1 - core) * half, half, 1)
    meta = jnp.concatenate(
        [
            lax.dynamic_index_in_dim(hubs, graph, 0, keepdims=False).reshape(-1),
            lax.dynamic_index_in_dim(tile_src, graph, 0, keepdims=False).reshape(-1),
        ]
    )
    meta = jnp.where(here, meta, swap(meta))
    own = jnp.where(here, mine, swap(for_other)).reshape(n_blocks, rows, half)
    outgoing = pick(meta, own)

    opposite = jnp.concatenate(
        [around(from_prev[: width // 2], 1), around(from_next[width // 2 :], -1)], axis=0
    )
    w_mine = jnp.stack([weight, from_next, opposite, from_prev])
    w_other = swap(w_mine)
    affine = jnp.concatenate([bias, gain, jnp.zeros((6, width), jnp.float32)], axis=0)
    affine = lax.all_gather(affine, SECTION)

    other = swap(mine)
    own_flat = own.reshape(-1, half)
    relayed = jnp.where(
        core == 0, jnp.concatenate([own_flat, other], axis=1), jnp.concatenate([other, own_flat], axis=1)
    )
    h = jnp.where(here, feats, relayed)

    tile_counts = lax.dynamic_index_in_dim(counts, graph, 0, keepdims=False).astype(jnp.bfloat16)
    tile_counts = tile_counts.transpose(0, 2, 1, 3).reshape(n_blocks, rows, tiles * rows)
    tile_counts = jnp.where(here, tile_counts, swap(tile_counts))
    degree = jnp.sum(tile_counts.astype(jnp.float32), axis=2, keepdims=True)
    inverse = jnp.broadcast_to(1.0 / jnp.maximum(degree, 1.0), (n_blocks, rows, 128))

    results = None
    for layer in range(n_layers):
        received = lax.all_to_all(outgoing, ("se", "dk"), 0, 0, tiled=True)
        mean_mine = aggregate(meta, own, received, tile_counts, inverse)
        mean_other = swap(mean_mine)
        place = jnp.stack([lax.rem(layer - section + n_layers, n_layers), core]).astype(jnp.int32)
        last = layer == n_layers - 1
        outs = dense(
            last, n_hubs, place, meta, h, mean_mine, mean_other, w_mine, w_other, affine[layer]
        )
        if last:
            (h,) = outs
        else:
            h, own, outgoing = outs
        arrived = jnp.stack([to_layer(h, layer, 0), to_layer(h, layer, 1)])
        results = arrived if results is None else jnp.where(section == layer, arrived, results)
    return results[None]


def solution(mesh):
    n_section, n_dp = mesh.shape["section"], mesh.shape["dp"]
    units = Mesh(mesh.devices.reshape(2, n_section // 2, n_dp // 2, 2), SECTION + PARTS)
    placed = (
        P(None, PARTS, None),
        P(SECTION, None, None),
        P(SECTION, None, None),
        P(SECTION, None),
        P(SECTION, None),
        P(None, None, PARTS),
        P(None, PARTS, None),
        P(None, PARTS, None, None, None),
    )
    return jax.shard_map(
        body, mesh=units, in_specs=placed, out_specs=P(SECTION, None, PARTS, None), check_vma=False
    )
```

time: 784 us -> 289 us (0.37)
  waiting for transfers between devices: 336 us -> 85.2 us
  blocking collectives: 204 us -> 79.2 us
  other arithmetic: 83.7 us -> 17 us
  local copies, waits for them, and re-layouts: 88.7 us -> 23.8 us
  Pallas kernels: 0 us -> 48.6 us
  matrix products: 43.3 us -> 0 us
  starting transfers between devices: 18.1 us -> 32.9 us
    all_to_all x2, waiting for transfers between devices: 201 us -> 23.5 us  [body(): received = lax.all_to_all(outgoing, ('se', 'dk'), 0, 0, tiled=True)]
    all_to_all x2, blocking collectives: 204 us -> 67.3 us  [body(): received = lax.all_to_all(outgoing, ('se', 'dk'), 0, 0, tiled=True)]
    ppermute x3 -> x21, waiting for transfers between devices: 136 us -> 61.7 us  [the longest x8 33.8 us: to_layer(): return lax.ppermute(value, ('sm', 'se', 'dc'), pairs)]
    gather x11 -> x0, local copies, waits for them, and re-layouts: 69.8 us -> none  [the longest x6 44.8 us: sage_layer(): source[chosen]]
    pallas_call x0 -> x9, Pallas kernels: none -> 48.6 us  [the longest x4 26.5 us: dense(): pl.pallas_call(functools.partial(dense_kernel, last), out_shape=out_shape...]
    dot_general x12 -> x0, matrix products: 43.3 us -> none  [the longest x4 29.9 us: sage_layer(): jnp.einsum('gbjvu,gbjud->gbvd', tile_counts.astype(jnp.bfloat16), gathere...]
    concatenate x4 -> x2, other arithmetic: 31.1 us -> 0.15 us  [the longest x1 0.08 us: body(): jnp.concatenate([lax.dynamic_index_in_dim(hubs, graph, 0, keepdims=False)...]
    select_n x7 -> x5, other arithmetic: 35 us -> 10.4 us  [the longest x1 3.87 us: body(): jnp.where(section == layer, arrived, results)]
  transfers between devices with their start and end apart: 5 -> 23, of which waited for: 5 -> 8; matrix products, arithmetic and copies ran while one was open for 2% -> 9% of each run, Pallas kernels for 0% -> 6%
where the time goes in v1:
time: 289 us; the launch traced here: 287 us
  waiting for transfers between devices  85.2 us (29%)
  blocking collectives  79.2 us (27%)
  Pallas kernels  48.6 us (17%)
  starting transfers between devices  32.9 us (11%)
  local copies, waits for them, and re-layouts  23.8 us (8%)
  other arithmetic  17 us (6%)
    all_to_all x2, blocking collectives, body(): received = lax.all_to_all(outgoing, ('se', 'dk'), 0, 0, tiled=True)  67.3 us
    ppermute x8, waiting for transfers between devices, to_layer(): return lax.ppermute(value, ('sm', 'se', 'dc'), pairs)  33.8 us
    pallas_call x4, Pallas kernels, dense(): pl.pallas_call(functools.partial(dense_kernel, last), out_shape=out_shape...  26.5 us
    ppermute x4, waiting for transfers between devices, around(): return lax.ppermute(value, SECTION, [(i, (i + by) % n) for i in range(n)])  23.8 us
    all_to_all x2, waiting for transfers between devices, body(): received = lax.all_to_all(outgoing, ('se', 'dk'), 0, 0, tiled=True)  23.5 us
    pallas_call x4, Pallas kernels, aggregate(): pl.pallas_call(functools.partial(aggregate_kernel, n_hubs), out_shape=jax...  20.1 us
    all_to_all x2, starting transfers between devices, body(): received = lax.all_to_all(outgoing, ('se', 'dk'), 0, 0, tiled=True)  14.5 us
    unnamed x33, local copies, waits for them, and re-layouts  12.9 us
  transfers between devices with their start and end apart: 23, of which 8 were waited for; matrix products, arithmetic and copies ran while one was open for 9% of the time, Pallas kernels for 6%

profile of v1, /device:TPU:24, one launch (start us, length us, event | category | flops | bytes accessed | tf_op | source)
XLA Modules:
  0.0 287.0 jit_solution(3387043567398853222)
XLA Ops:
  6.8 3.9 %constant_dynamic-slice_fusion = s32[1,8,6,128,128]{4,3,2,1,0:T(8,128)} fusion(s32[2,8,6,128,128]{4,3,2,1,0:T(8,128)} %param.15, s32[]{:T(128)S(6)} %select_n.115), kind=kLoop, calls=%fused_computation.15 | loop fusion | bytes 6291460 | tf_op jit(solution)/shard_map/jit(dynamic_index_in_dim)/dynamic_slice | solution.py:245
  10.7 2.4 copy.15
  14.6 2.6 copy.14
  17.3 2.5 broadcast_select_fusion.2
  21.9 9.5 %all-to-all-start = ((bf16[32,128,256]{2,1,0:T(8,128)(2,1)}), bf16[32,128,256]{2,1,0:T(8,128)(2,1)}, u32[]{:S(2)}, u32[]{:S(2)}) async-start(bf16[32,128,256]{2,1,0:T(8,128)(2,1)} %pick.1), calls=%async_computation | async-start | bytes 4194304 | tf_op jit(solution)/shard_map/all_to_all | solution.py:253
  33.7 3.0 %collective-permute-start.7 = (bf16[256,512]{1,0:T(8,128)(2,1)S(1)}, bf16[256,512]{1,0:T(8,128)(2,1)S(1)}, u32[]{:S(2)}, u32[]{:S(2)}) collective-permute-start(bf16[256,512]{1,0:T(8,128)(2,1)S(1)} %slice.28), channel_id=1, source_target_pairs={{0,32},{32,64},{64,96},{96,0},{1,33},{33,65},{65,97},{97,1},{2,34}... | collective-permute-start | bytes 786440 | tf_op jit(solution)/shard_map/ppermute | solution.py:195
  36.7 23.0 %collective-permute-done.8 = bf16[256,512]{1,0:T(8,128)(2,1)S(1)} collective-permute-done((bf16[256,512]{1,0:T(8,128)(2,1)S(1)}, bf16[256,512]{1,0:T(8,128)(2,1)S(1)}, u32[]{:S(2)}, u32[]{:S(2)}) %collective-permute-start.8) | collective-permute-done | bytes 262176 | tf_op jit(solution)/shard_map/ppermute | solution.py:195
  62.8 3.0 %convert_reduce_fusion = (f32[8,128]{1,0:T(8,128)S(1)}, bf16[8,128,768]{2,1,0:T(8,128)(2,1)}) fusion(bf16[8,128,768]{2,1,0:T(8,128)(2,1)} %copy.14, bf16[8,128,768]{2,1,0:T(8,128)(2,1)} %collective-permute-done.3, pred[]{:T(512)S(6)} %eq.17), kind=kLoop, calls=%fused_computation | loop fusion | flops 2358272 | bytes 4722689 | tf_op jit(solution)/shard_map/reduce_sum | solution.py:248
  67.5 5.5 %aggregate.4.mean_mine = bf16[8,128,256]{2,1,0:T(8,128)(2,1)} custom-call(s32[80]{0:T(128)S(1)} %broadcast_select_fusion.3.meta, bf16[8,128,256]{2,1,0:T(8,128)(2,1)S(1)} %bitcast.34, bf16[32,128,256]{2,1,0:T(8,128)(2,1)} %all-to-all-done.received, bf16[8,128,768]{2,1,0:T(8,128)(2,1)S(1)} %copy-done.2, f32[8,128,128]{2,1,0:T(8,128)S(1)} %broadcast_in_dim.4.inverse), custom_call_target="tpu_custom_call" | custom-call | tf_op jit(solution)/shard_map/aggregate/pallas_call | solution.py:88
  73.2 11.8 %all-gather = f32[32,512]{1,0:T(8,128)S(1)} all-gather(f32[8,512]{1,0:T(8,128)S(1)} %maximum_maximum_fusion), channel_id=2, replica_groups=mesh['sm'=2,'se'=2,'dk'=16,'dc'=2] {'sm','se'}, dimensions={0}, use_global_device_ids=true | all-gather | bytes 81920 | tf_op jit(solution)/shard_map/all_gather | solution.py:236
  87.1 7.0 %dense.4 = (bf16[1024,512]{1,0:T(8,128)(2,1)S(1)}, bf16[8,128,256]{2,1,0:T(8,128)(2,1)S(1)}, bf16[32,128,256]{2,1,0:T(8,128)(2,1)S(1)}) custom-call(s32[2]{0:T(128)S(1)} %pad_add_fusion.4.place, s32[80]{0:T(128)S(1)} %broadcast_select_fusion.3.meta, bf16[1024,512]{1,0:T(8,128)(2,1)S(1)} %fusion.h, bf16[8,128,256]{2,1,0:T(8,128)(2,1)} %aggregate.4.mean_mine, ...), custom_call_target="tpu_custom_call" | custom-call | tf_op jit(solution)/shard_map/dense/pallas_call | solution.py:178
  95.1 34.6 %all_to_all.20.received = bf16[32,128,256]{2,1,0:T(8,128)(2,1)S(1)} all-to-all(bf16[32,128,256]{2,1,0:T(8,128)(2,1)S(1)} %get-tuple-element.16), channel_id=1, replica_groups=mesh['sm'=2,'se'=2,'dk'=16,'dc'=2] {'se','dk'}, dimensions={0} | all-to-all | bytes 4194304 | tf_op jit(solution)/shard_map/all_to_all | solution.py:253
  129.8 4.9 %aggregate.5.mean_mine = bf16[8,128,256]{2,1,0:T(8,128)(2,1)S(1)} custom-call(s32[80]{0:T(128)S(1)} %broadcast_select_fusion.3.meta, bf16[8,128,256]{2,1,0:T(8,128)(2,1)S(1)} %get-tuple-element.15.own, bf16[32,128,256]{2,1,0:T(8,128)(2,1)S(1)} %all_to_all.20.received, bf16[8,128,768]{2,1,0:T(8,128)(2,1)S(1)} %copy-done.3, ...), custom_call_target="tpu_custom_call" | custom-call | tf_op jit(solution)/shard_map/aggregate/pallas_call | solution.py:88
  138.0 6.8 %dense.5 = (bf16[1024,512]{1,0:T(8,128)(2,1)S(1)}, bf16[8,128,256]{2,1,0:T(8,128)(2,1)S(1)}, bf16[32,128,256]{2,1,0:T(8,128)(2,1)S(1)}) custom-call(s32[2]{0:T(128)S(1)} %pad_add_fusion.3.place, s32[80]{0:T(128)S(1)} %broadcast_select_fusion.3.meta, bf16[1024,512]{1,0:T(8,128)(2,1)S(1)} %copy-done.8, bf16[8,128,256]{2,1,0:T(8,128)(2,1)S(1)} %aggregate.5.mean_mine, ...), custom_call_target="tpu_custom_call" | custom-call | tf_op jit(solution)/shard_map/dense/pallas_call | solution.py:178
  145.9 32.7 %all_to_all.21.received = bf16[32,128,256]{2,1,0:T(8,128)(2,1)S(1)} all-to-all(bf16[32,128,256]{2,1,0:T(8,128)(2,1)S(1)} %get-tuple-element.19), channel_id=1, replica_groups=mesh['sm'=2,'se'=2,'dk'=16,'dc'=2] {'se','dk'}, dimensions={0} | all-to-all | bytes 4194304 | tf_op jit(solution)/shard_map/all_to_all | solution.py:253
  178.6 4.9 %aggregate.6.mean_mine = bf16[8,128,256]{2,1,0:T(8,128)(2,1)S(1)} custom-call(s32[80]{0:T(128)S(1)} %broadcast_select_fusion.3.meta, bf16[8,128,256]{2,1,0:T(8,128)(2,1)S(1)} %get-tuple-element.18.own, bf16[32,128,256]{2,1,0:T(8,128)(2,1)S(1)} %all_to_all.21.received, bf16[8,128,768]{2,1,0:T(8,128)(2,1)S(1)} %copy-done.4, ...), custom_call_target="tpu_custom_call" | custom-call | tf_op jit(solution)/shard_map/aggregate/pallas_call | solution.py:88
  186.9 7.8 %dense.6 = (bf16[1024,512]{1,0:T(8,128)(2,1)}, bf16[8,128,256]{2,1,0:T(8,128)(2,1)S(1)}, bf16[32,128,256]{2,1,0:T(8,128)(2,1)S(1)}) custom-call(s32[2]{0:T(128)S(1)} %pad_add_fusion.2.place, s32[80]{0:T(128)S(1)} %broadcast_select_fusion.3.meta, bf16[1024,512]{1,0:T(8,128)(2,1)S(1)} %copy-done.10, bf16[8,128,256]{2,1,0:T(8,128)(2,1)S(1)} %aggregate.6.mean_mine, ...), custom_call_target="tpu_custom_call" | custom-call | tf_op jit(solution)/shard_map/dense/pallas_call | solution.py:178
  196.8 5.0 %all-to-all-start.3 = ((bf16[32,128,256]{2,1,0:T(8,128)(2,1)}), bf16[32,128,256]{2,1,0:T(8,128)(2,1)}, u32[]{:S(2)}, u32[]{:S(2)}) async-start(bf16[32,128,256]{2,1,0:T(8,128)(2,1)} %copy-done.6), calls=%async_computation.3 | async-start | bytes 4194304 | tf_op jit(solution)/shard_map/all_to_all | solution.py:253
  206.8 23.5 %all-to-all-done.3.received = bf16[32,128,256]{2,1,0:T(8,128)(2,1)} async-done(((bf16[32,128,256]{2,1,0:T(8,128)(2,1)}), bf16[32,128,256]{2,1,0:T(8,128)(2,1)}, u32[]{:S(2)}, u32[]{:S(2)}) %all-to-all-start.3) | async-done | bytes 2097184 | tf_op jit(solution)/shard_map/all_to_all | solution.py:253
  232.7 4.7 %aggregate.7.mean_mine = bf16[8,128,256]{2,1,0:T(8,128)(2,1)S(1)} custom-call(s32[80]{0:T(128)S(1)} %broadcast_select_fusion.3.meta, bf16[8,128,256]{2,1,0:T(8,128)(2,1)S(1)} %copy-done.12, bf16[32,128,256]{2,1,0:T(8,128)(2,1)} %all-to-all-done.3.received, bf16[8,128,768]{2,1,0:T(8,128)(2,1)S(1)} %copy-done.5, f32[8,128,128]{2,1,0:T(8,128)S(1)} %broadcast_in_dim.4.inverse), custom_call_target="tpu_custom_call" | custom-call | tf_op jit(solution)/shard_map/aggregate/pallas_call | solution.py:88
  241.1 4.8 %dense.7 = bf16[1024,512]{1,0:T(8,128)(2,1)} custom-call(s32[2]{0:T(128)S(1)} %pad_add_fusion.place, s32[80]{0:T(128)S(1)} %broadcast_select_fusion.3.meta, bf16[1024,512]{1,0:T(8,128)(2,1)} %get-tuple-element.20.h, bf16[8,128,256]{2,1,0:T(8,128)(2,1)S(1)} %aggregate.7.mean_mine, bf16[8,128,256]{2,1,0:T(8,128)(2,1)S(1)} %collective-permute-done.12.mean_other, ...), custom_call_target="tpu_custom_call" | custom-call | tf_op jit(solution)/shard_map/dense/pallas_call | solution.py:178
  249.3 21.0 %collective-permute-done.14 = bf16[1024,512]{1,0:T(8,128)(2,1)S(1)} collective-permute-done((bf16[1024,512]{1,0:T(8,128)(2,1)}, bf16[1024,512]{1,0:T(8,128)(2,1)S(1)}, u32[]{:S(2)}, u32[]{:S(2)}) %collective-permute-start.14) | collective-permute-done | bytes 1048608 | tf_op jit(solution)/shard_map/ppermute | solution.py:200
  270.3 12.9 %collective-permute-done.13 = bf16[1024,512]{1,0:T(8,128)(2,1)S(1)} collective-permute-done((bf16[1024,512]{1,0:T(8,128)(2,1)}, bf16[1024,512]{1,0:T(8,128)(2,1)S(1)}, u32[]{:S(2)}, u32[]{:S(2)}) %collective-permute-start.13) | collective-permute-done | bytes 1048608 | tf_op jit(solution)/shard_map/ppermute | solution.py:200
  283.2 3.9 %maximum_select_fusion = bf16[1,2,1024,512]{3,2,1,0:T(8,128)(2,1)} fusion(bf16[1,1,1024,512]{3,2,1,0:T(8,128)(2,1)S(1)} %bitcast.37, bf16[1,1,1024,512]{3,2,1,0:T(8,128)(2,1)S(1)} %bitcast.38, bf16[1,1,1024,512]{3,2,1,0:T(8,128)(2,1)} %bitcast.20, bf16[1,1,1024,512]{3,2,1,0:T(8,128)(2,1)S(1)} %bitcast.36, bf16[1,1,1024,512]{3,2,1,0:T(8,128)(2,1)} %bitcast.22, ...), kind=kLoop, calls=%fused_computation.2 | loop fusion | flops 7340032 | bytes 10485763 | tf_op jit(solution)/shard_map/jit(_where)/select_n | solution.py:266
  (96 shorter events, 45.0 us)
Async XLA Ops:
  2.0 30.8 %collective-permute-start.6 = (bf16[512,512]{1,0:T(8,128)(2,1)}, bf16[512,512]{1,0:T(8,128)(2,1)}, u32[]{:S(2)}, u32[]{:S(2)}) collective-permute-start(bf16[512,512]{1,0:T(8,128)(2,1)} %bitcast.13), channel_id=1, source_target_pairs={{0,32},{32,64},{64,96},{96,0},{1,33},{33,65},{65,97},{97,1},{2,34}... | collective-permute-start | bytes 1572872 | tf_op jit(solution)/shard_map/ppermute | solution.py:195
  2.1 29.3 %collective-permute-start.5 = (bf16[512,512]{1,0:T(8,128)(2,1)}, bf16[512,512]{1,0:T(8,128)(2,1)}, u32[]{:S(2)}, u32[]{:S(2)}) collective-permute-start(bf16[512,512]{1,0:T(8,128)(2,1)} %bitcast.13), channel_id=1, source_target_pairs={{0,96},{32,0},{64,32},{96,64},{1,97},{33,1},{65,33},{97,65},{2,98}... | collective-permute-start | bytes 1572872 | tf_op jit(solution)/shard_map/ppermute | solution.py:195
  6.0 11.2 %collective-permute-start.1 = (bf16[1024,256]{1,0:T(8,128)(2,1)}, bf16[1024,256]{1,0:T(8,128)(2,1)}, u32[]{:S(2)}, u32[]{:S(2)}) collective-permute-start(bf16[1024,256]{1,0:T(8,128)(2,1)} %dynamic-slice_bitcast_fusion), channel_id=1, source_target_pairs={{0,1},{1,0},{2,3},{3,2},{4,5},{5,4},{6,7},{7,6},{8,9},{9,8},{10,11... | collective-permute-start | bytes 1572872 | tf_op jit(solution)/shard_map/ppermute | solution.py:190
  6.3 10.9 %collective-permute-start = (s32[80]{0:T(128)S(1)}, s32[80]{0:T(128)S(1)}, u32[]{:S(2)}, u32[]{:S(2)}) collective-permute-start(s32[80]{0:T(128)S(1)} %pad_add_fusion.1), channel_id=1, source_target_pairs={{0,1},{1,0},{2,3},{3,2},{4,5},{5,4},{6,7},{7,6},{8,9},{9,8},{10,11... | collective-permute-start | bytes 968 | tf_op jit(solution)/shard_map/ppermute | solution.py:190
  17.2 45.6 %collective-permute-start.3 = (bf16[8,128,768]{2,1,0:T(8,128)(2,1)}, bf16[8,128,768]{2,1,0:T(8,128)(2,1)}, u32[]{:S(2)}, u32[]{:S(2)}) collective-permute-start(bf16[8,128,768]{2,1,0:T(8,128)(2,1)} %copy.14), channel_id=1, source_target_pairs={{0,1},{1,0},{2,3},{3,2},{4,5},{5,4},{6,7},{7,6},{8,9},{9,8},{10,11... | collective-permute-start | bytes 4718600 | tf_op jit(solution)/shard_map/ppermute | solution.py:190
  21.9 43.9 %all-to-all-start = ((bf16[32,128,256]{2,1,0:T(8,128)(2,1)}), bf16[32,128,256]{2,1,0:T(8,128)(2,1)}, u32[]{:S(2)}, u32[]{:S(2)}) async-start(bf16[32,128,256]{2,1,0:T(8,128)(2,1)} %pick.1), calls=%async_computation | async-start | bytes 4194304 | tf_op jit(solution)/shard_map/all_to_all | solution.py:253
  32.3 27.4 %collective-permute-start.8 = (bf16[256,512]{1,0:T(8,128)(2,1)S(1)}, bf16[256,512]{1,0:T(8,128)(2,1)S(1)}, u32[]{:S(2)}, u32[]{:S(2)}) collective-permute-start(bf16[256,512]{1,0:T(8,128)(2,1)S(1)} %slice.29), channel_id=1, source_target_pairs={{0,96},{32,0},{64,32},{96,64},{1,97},{33,1},{65,33},{97,65},{2,98}... | collective-permute-start | bytes 786440 | tf_op jit(solution)/shard_map/ppermute | solution.py:195
  33.7 26.8 %collective-permute-start.7 = (bf16[256,512]{1,0:T(8,128)(2,1)S(1)}, bf16[256,512]{1,0:T(8,128)(2,1)S(1)}, u32[]{:S(2)}, u32[]{:S(2)}) collective-permute-start(bf16[256,512]{1,0:T(8,128)(2,1)S(1)} %slice.28), channel_id=1, source_target_pairs={{0,32},{32,64},{64,96},{96,0},{1,33},{33,65},{65,97},{97,1},{2,34}... | collective-permute-start | bytes 786440 | tf_op jit(solution)/shard_map/ppermute | solution.py:195
  62.1 25.0 %collective-permute-start.9 = (bf16[4,512,512]{2,1,0:T(8,128)(2,1)S(1)}, bf16[4,512,512]{2,1,0:T(8,128)(2,1)}, u32[]{:S(2)}, u32[]{:S(2)}) collective-permute-start(bf16[4,512,512]{2,1,0:T(8,128)(2,1)S(1)} %pad_maximum_fusion.w_mine), channel_id=1, source_target_pairs={{0,1},{1,0},{2,3},{3,2},{4,5},{5,4},{6,7},{7,6},{8,9},{9,8},{10,11... | collective-permute-start | bytes 6291464 | tf_op jit(solution)/shard_map/ppermute | solution.py:190
  62.3 22.8 %collective-permute-start.2 = (bf16[1024,256]{1,0:T(8,128)(2,1)}, bf16[1024,256]{1,0:T(8,128)(2,1)}, u32[]{:S(2)}, u32[]{:S(2)}) collective-permute-start(bf16[1024,256]{1,0:T(8,128)(2,1)} %get-tuple-element.26), channel_id=1, source_target_pairs={{0,1},{1,0},{2,3},{3,2},{4,5},{5,4},{6,7},{7,6},{8,9},{9,8},{10,11... | collective-permute-start | bytes 1572872 | tf_op jit(solution)/shard_map/ppermute | solution.py:190
  73.0 14.1 %collective-permute-start.4 = (bf16[8,128,256]{2,1,0:T(8,128)(2,1)}, bf16[8,128,256]{2,1,0:T(8,128)(2,1)}, u32[]{:S(2)}, u32[]{:S(2)}) collective-permute-start(bf16[8,128,256]{2,1,0:T(8,128)(2,1)} %aggregate.4.mean_mine), channel_id=1, source_target_pairs={{0,1},{1,0},{2,3},{3,2},{4,5},{5,4},{6,7},{7,6},{8,9},{9,8},{10,11... | collective-permute-start | bytes 1572872 | tf_op jit(solution)/shard_map/ppermute | solution.py:190
  95.1 34.6 %copy-start.3 = (bf16[8,128,768]{2,1,0:T(8,128)(2,1)S(1)}, bf16[8,128,768]{2,1,0:T(8,128)(2,1)}, u32[]{:S(2)}) copy-start(bf16[8,128,768]{2,1,0:T(8,128)(2,1)} %get-tuple-element.24.counts) | copy-start | bytes 4718596
  134.7 2.1 collective-permute-start.10
  183.5 2.1 collective-permute-start.11
  196.8 33.5 %all-to-all-start.3 = ((bf16[32,128,256]{2,1,0:T(8,128)(2,1)}), bf16[32,128,256]{2,1,0:T(8,128)(2,1)}, u32[]{:S(2)}, u32[]{:S(2)}) async-start(bf16[32,128,256]{2,1,0:T(8,128)(2,1)} %copy-done.6), calls=%async_computation.3 | async-start | bytes 4194304 | tf_op jit(solution)/shard_map/all_to_all | solution.py:253
  201.8 44.1 %collective-permute-start.20 = (bf16[1024,512]{1,0:T(8,128)(2,1)}, bf16[1024,512]{1,0:T(8,128)(2,1)}, u32[]{:S(2)}, u32[]{:S(2)}) collective-permute-start(bf16[1024,512]{1,0:T(8,128)(2,1)} %copy-done.7), channel_id=1, source_target_pairs={{64,0},{97,1},{66,2},{99,3},{68,4},{101,5},{70,6},{103,7},{72,8},{... | collective-permute-start | bytes 3145736 | tf_op jit(solution)/shard_map/ppermute | solution.py:200
  203.5 43.2 %collective-permute-start.19 = (bf16[1024,512]{1,0:T(8,128)(2,1)}, bf16[1024,512]{1,0:T(8,128)(2,1)}, u32[]{:S(2)}, u32[]{:S(2)}) collective-permute-start(bf16[1024,512]{1,0:T(8,128)(2,1)} %copy-done.7), channel_id=1, source_target_pairs={{0,0},{33,1},{2,2},{35,3},{4,4},{37,5},{6,6},{39,7},{8,8},{41,9},{... | collective-permute-start | bytes 3145736 | tf_op jit(solution)/shard_map/ppermute | solution.py:200
  205.2 42.8 %collective-permute-start.18 = (bf16[1024,512]{1,0:T(8,128)(2,1)}, bf16[1024,512]{1,0:T(8,128)(2,1)}, u32[]{:S(2)}, u32[]{:S(2)}) collective-permute-start(bf16[1024,512]{1,0:T(8,128)(2,1)} %copy-done.9), channel_id=1, source_target_pairs={{64,32},{97,33},{66,34},{99,35},{68,36},{101,37},{70,38},{103,39},... | collective-permute-start | bytes 3145736 | tf_op jit(solution)/shard_map/ppermute | solution.py:200
  237.5 2.0 collective-permute-start.12
  237.7 11.6 %collective-permute-start.17 = (bf16[1024,512]{1,0:T(8,128)(2,1)}, bf16[1024,512]{1,0:T(8,128)(2,1)}, u32[]{:S(2)}, u32[]{:S(2)}) collective-permute-start(bf16[1024,512]{1,0:T(8,128)(2,1)} %copy-done.9), channel_id=1, source_target_pairs={{0,32},{33,33},{2,34},{35,35},{4,36},{37,37},{6,38},{39,39},{8,40}... | collective-permute-start | bytes 3145736 | tf_op jit(solution)/shard_map/ppermute | solution.py:200
  239.5 9.8 %collective-permute-start.16 = (bf16[1024,512]{1,0:T(8,128)(2,1)}, bf16[1024,512]{1,0:T(8,128)(2,1)}, u32[]{:S(2)}, u32[]{:S(2)}) collective-permute-start(bf16[1024,512]{1,0:T(8,128)(2,1)} %get-tuple-element.20.h), channel_id=1, source_target_pairs={{64,64},{97,65},{66,66},{99,67},{68,68},{101,69},{70,70},{103,71},... | collective-permute-start | bytes 3145736 | tf_op jit(solution)/shard_map/ppermute | solution.py:200
  245.9 3.4 %collective-permute-start.15 = (bf16[1024,512]{1,0:T(8,128)(2,1)}, bf16[1024,512]{1,0:T(8,128)(2,1)S(1)}, u32[]{:S(2)}, u32[]{:S(2)}) collective-permute-start(bf16[1024,512]{1,0:T(8,128)(2,1)} %get-tuple-element.20.h), channel_id=1, source_target_pairs={{0,64},{33,65},{2,66},{35,67},{4,68},{37,69},{6,70},{39,71},{8,72}... | collective-permute-start | bytes 3145736 | tf_op jit(solution)/shard_map/ppermute | solution.py:200
  246.7 23.6 %collective-permute-start.14 = (bf16[1024,512]{1,0:T(8,128)(2,1)}, bf16[1024,512]{1,0:T(8,128)(2,1)S(1)}, u32[]{:S(2)}, u32[]{:S(2)}) collective-permute-start(bf16[1024,512]{1,0:T(8,128)(2,1)} %dense.7), channel_id=1, source_target_pairs={{64,96},{97,97},{66,98},{99,99},{68,100},{101,101},{70,102},{103,1... | collective-permute-start | bytes 3145736 | tf_op jit(solution)/shard_map/ppermute | solution.py:200
  248.0 35.2 %collective-permute-start.13 = (bf16[1024,512]{1,0:T(8,128)(2,1)}, bf16[1024,512]{1,0:T(8,128)(2,1)S(1)}, u32[]{:S(2)}, u32[]{:S(2)}) collective-permute-start(bf16[1024,512]{1,0:T(8,128)(2,1)} %dense.7), channel_id=1, source_target_pairs={{0,96},{33,97},{2,98},{35,99},{4,100},{37,101},{6,102},{39,103},{8... | collective-permute-start | bytes 3145736 | tf_op jit(solution)/shard_map/ppermute | solution.py:200
  (15 other events, 70.7 us)

commit v2 on v0

v2 whole, which is shorter than its diff:
```python
import functools

import jax
import jax.numpy as jnp
from jax import lax
from jax.experimental import pallas as pl
from jax.experimental.pallas import tpu as pltpu
from jax.sharding import Mesh, PartitionSpec as P

SECTION = ("sm", "se")
PARTS = ("dz", "dx", "dc")
CHIPS, CORES = ("dx", "se", "dz"), ("dx", "dc", "dz")
SIDE = 4
ROWS = 128
CHUNK = 256
N_LAYERS = 4
SPLIT_ROWS = 16
VMEM, SMEM, HBM = pltpu.VMEM, pltpu.SMEM, pltpu.HBM


MIB = 1024 * 1024


def params(mib=24):
    return pltpu.CompilerParams(vmem_limit_bytes=mib * MIB)


def call(kernel, name, in_spaces, out_shape, out_spaces, scratch=(), mib=24, **kwargs):
    return pl.pallas_call(
        kernel,
        out_shape=out_shape,
        in_specs=[pl.BlockSpec(memory_space=s) for s in in_spaces],
        out_specs=[pl.BlockSpec(memory_space=s) for s in out_spaces],
        scratch_shapes=list(scratch),
        compiler_params=params(mib),
        name=name,
        **kwargs,
    )


def like(array, shape=None):
    return jax.ShapeDtypeStruct(shape or array.shape, array.dtype)


def part(index, size):
    return pl.ds(pl.multiple_of(index * size, size), size)


def block_rows(block):
    return part(block, ROWS)


def run_copies(pieces, sems):
    copies = [pltpu.make_async_copy(s, d, sems.at[i]) for i, (s, d) in enumerate(pieces)]
    for copy in copies:
        copy.start()
    for copy in copies:
        copy.wait()


def reader_of(j):
    x, e, z = j // (2 * SIDE), j // SIDE % 2, j % SIDE
    return 2 * (z * SIDE + x) + e


def place_of(partition):
    chip, e = lax.div(partition, 2), lax.rem(partition, 2)
    z, x = lax.div(chip, SIDE), lax.rem(chip, SIDE)
    return x * (2 * SIDE) + e * SIDE + z


def front_kernel(hubs, features, w_self, w_neigh, bias, gain, outgoing, packed, held, load_sem, w_sem, sems):
    graph, parity, core = lax.axis_index("sm"), lax.axis_index("se"), lax.axis_index("dc")
    width = packed.shape[1]
    load = pltpu.make_async_copy(features.at[graph], held, load_sem)
    load.start()
    for index, source in enumerate((w_self, w_neigh)):

        @pl.when(core == index)
        def _(source=source):
            pltpu.make_async_copy(source.at[0], packed.at[pl.ds(0, width)], w_sem).start()

    values = jnp.concatenate([bias[...], gain[...]], axis=0)
    parts = []
    for _ in range(3):
        part = values.astype(packed.dtype).astype(jnp.float32)
        parts.append(part)
        values = values - part
    parts.append(jnp.zeros((SPLIT_ROWS - 6, width), jnp.float32))
    packed[width : width + SPLIT_ROWS, :] = jnp.concatenate(parts, axis=0).astype(packed.dtype)
    load.wait()
    half = outgoing.shape[2]
    copies = []
    for j in range(outgoing.shape[0]):
        reader = reader_of(j)
        block = jnp.maximum(hubs[graph, reader - reader % 2 + parity], 0)
        source = held.at[block_rows(block), pl.ds((reader % 2) * half, half)]
        copies.append(pltpu.make_async_copy(source, outgoing.at[j], sems.at[j]))
        copies[-1].start()
    pltpu.make_async_copy(w_self.at[0], packed.at[pl.ds(0, width)], w_sem).wait()
    for copy in copies:
        copy.wait()


def front(hubs, features, w_self, w_neigh, bias, gain):
    n_hubs, (_, rows, width) = hubs.shape[1], features.shape
    return call(
        front_kernel,
        "front",
        (SMEM, HBM, HBM, HBM, VMEM, VMEM),
        [like(features, (n_hubs, ROWS, width // 2)), like(w_self, (width + SPLIT_ROWS, width))],
        (HBM, VMEM),
        [
            pltpu.VMEM((rows, width), features.dtype),
            pltpu.SemaphoreType.DMA,
            pltpu.SemaphoreType.DMA,
            pltpu.SemaphoreType.DMA((n_hubs,)),
        ],
        mib=56,
    )(hubs, features, w_self, w_neigh, bias, gain)


def ready_kernel(place, *refs):
    sources, (h, counts, inverse, sems) = refs[:6], refs[6:]
    here = place[1] == place[2]
    for held, want in enumerate((jnp.logical_not(here), here)):

        @pl.when(want)
        def _(held=held):
            feats, tile_counts, inverses = sources[3 * (1 - held) : 3 * (1 - held) + 3]
            feats = feats.at[place[0]]
            run_copies([(feats, h), (tile_counts, counts), (inverses, inverse)], sems)


def ready(place, feats, counts, inverse, feats_swapped, counts_swapped, inverse_swapped):
    _, rows, width = feats.shape
    return call(
        ready_kernel,
        "ready",
        (SMEM,) + (HBM,) * 6,
        [like(feats, (rows, width)), like(counts), like(inverse)],
        (VMEM,) * 3,
        [pltpu.SemaphoreType.DMA((3,))],
    )(place, feats, counts, inverse, feats_swapped, counts_swapped, inverse_swapped)


def tally_kernel(place, counts, out, inverse):
    tiles = counts.shape[2]
    total = jnp.zeros((ROWS, ROWS), jnp.float32)
    for j in range(tiles):
        tile = counts[0, 0, j].astype(jnp.float32)
        total = total + tile
        out[0, :, j * ROWS : (j + 1) * ROWS] = tile.astype(out.dtype)
    degree = jnp.sum(total, axis=1, keepdims=True)
    inverse[0] = jnp.broadcast_to(1.0 / jnp.maximum(degree, 1.0), (ROWS, ROWS))


def tally(place, counts):
    n_blocks, tiles = counts.shape[1], counts.shape[2]
    return pl.pallas_call(
        tally_kernel,
        out_shape=[
            jax.ShapeDtypeStruct((n_blocks, ROWS, tiles * ROWS), jnp.bfloat16),
            jax.ShapeDtypeStruct((n_blocks, ROWS, ROWS), jnp.float32),
        ],
        grid_spec=pltpu.PrefetchScalarGridSpec(
            num_scalar_prefetch=1,
            grid=(n_blocks,),
            in_specs=[pl.BlockSpec((1, 1, tiles, ROWS, ROWS), lambda b, place: (place[0], b, 0, 0, 0))],
            out_specs=[
                pl.BlockSpec((1, ROWS, tiles * ROWS), lambda b, place: (b, 0, 0)),
                pl.BlockSpec((1, ROWS, ROWS), lambda b, place: (b, 0, 0)),
            ],
        ),
        compiler_params=params(),
        name="tally",
    )(place, counts)


def aggregate_kernel(core_ref, tile_src, h, received, counts, inverse, out):
    n_blocks = counts.shape[0]
    tiles = counts.shape[2] // ROWS
    cols = part(core_ref[0], out.shape[1])
    for b in range(n_blocks):
        picked = []
        for j in range(tiles):
            slot = tile_src[b * tiles + j]
            near = h[block_rows(jnp.minimum(slot, n_blocks - 1)), cols]
            sender = place_of(jnp.maximum(slot - n_blocks, 0))
            picked.append(lax.select(slot < n_blocks, near, received[sender]))
        summed = jnp.dot(counts[b], jnp.concatenate(picked, axis=0), preferred_element_type=jnp.float32)
        scale = inverse[b]
        scale = jnp.concatenate([scale] * (out.shape[1] // ROWS), axis=1)
        out[b * ROWS : (b + 1) * ROWS, :] = (summed * scale).astype(out.dtype)


def aggregate(core, tile_src, h, received, counts, inverse):
    rows, width = h.shape
    (out,) = call(
        aggregate_kernel,
        "aggregate",
        (SMEM, SMEM, VMEM, VMEM, VMEM, VMEM),
        [like(h, (rows, width // 2))],
        (VMEM,),
    )(core, tile_src, h, received, counts, inverse)
    return out


def layer_rows(layer, core, rows, h, mean_mine, mean_other, gathered, pre):
    width = h.shape[1]
    half = width // 2
    parts = gathered[2 * layer, width : width + SPLIT_ROWS, :].astype(jnp.float32)
    affine = (parts[4:6] + parts[2:4]) + parts[0:2]
    bias, gain = affine[0:1], affine[1:2]
    left = jnp.concatenate([h[rows, :], mean_mine[rows, :], mean_other[rows, :]], axis=1)
    right = jnp.concatenate(
        [
            gathered[2 * layer, 0:width, :],
            gathered[2 * layer + 1, part(core, half), :],
            gathered[2 * layer + 1, part(1 - core, half), :],
        ],
        axis=0,
    )
    pre[...] = jnp.dot(left, right, preferred_element_type=jnp.float32)
    for begin in range(0, CHUNK, 64):
        x = pre[begin : begin + 64, :] + bias
        mu = jnp.mean(x, axis=1, keepdims=True)
        centred = x - mu
        var = jnp.mean(centred * centred, axis=1, keepdims=True)
        yield begin, jnp.maximum(centred * lax.rsqrt(var + 1e-05) * gain, 0.0).astype(h.dtype)


def dense_kernel(layer, core_ref, blocks, h, mean_mine, mean_other, gathered, h_out, outgoing, pre):
    core = core_ref[0]
    for c in range(h.shape[0] // CHUNK):
        rows = pl.ds(c * CHUNK, CHUNK)
        for begin, value in layer_rows(layer, core, rows, h, mean_mine, mean_other, gathered, pre.at[c]):
            begin = c * CHUNK + begin
            h_out[begin : begin + 64, :] = value
    for j in range(outgoing.shape[0]):
        outgoing[j] = h_out[block_rows(blocks[reader_of(j)]), part(core, outgoing.shape[2])]


def dense(layer, core, blocks, h, mean_mine, mean_other, gathered):
    rows, width = h.shape
    return call(
        functools.partial(dense_kernel, layer),
        "dense",
        (SMEM, SMEM) + (VMEM,) * 4,
        [like(h), like(h, (blocks.shape[0], ROWS, width // 2))],
        (VMEM, VMEM),
        [pltpu.VMEM((rows // CHUNK, CHUNK, width), jnp.float32)],
    )(core, blocks, h, mean_mine, mean_other, gathered)


def last_dense_kernel(core_ref, h, mean_mine, mean_other, gathered, *rest):
    *kept, leaving, pre, sems = rest
    core, last = core_ref[0], N_LAYERS - 1
    half_rows = leaving.shape[1]
    copies = [
        pltpu.make_async_copy(source.at[part(core, half_rows)], leaving.at[layer], sems.at[layer])
        for layer, source in enumerate([*kept, h])
    ]
    for copy in copies:
        copy.start()
    n_chunks = half_rows // CHUNK
    for c in range(n_chunks):
        rows = part(core * n_chunks + c, CHUNK)
        for begin, value in layer_rows(last, core, rows, h, mean_mine, mean_other, gathered, pre.at[c]):
            begin = c * CHUNK + begin
            leaving[last, begin : begin + 64, :] = value
    for copy in copies:
        copy.wait()


def last_dense(core, h, mean_mine, mean_other, gathered, kept):
    rows, width = h.shape
    (out,) = call(
        last_dense_kernel,
        "last_dense",
        (SMEM,) + (VMEM,) * 4 + (HBM,) * len(kept),
        [like(h, (N_LAYERS, rows // 2, width))],
        (VMEM,),
        [
            pltpu.VMEM((rows // 2 // CHUNK, CHUNK, width), jnp.float32),
            pltpu.SemaphoreType.DMA((N_LAYERS - 1,)),
        ],
    )(core, h, mean_mine, mean_other, gathered, *kept)
    return out


def finish_kernel(core_ref, straight, crossed, out, sems):
    core, chunk = core_ref[0], straight.shape[1]
    pieces = []
    for g in range(2):
        pieces.append((straight.at[2 * g + core], out.at[g, part(core, chunk)]))
        pieces.append((crossed.at[g], out.at[g, part(1 - core, chunk)]))
    run_copies(pieces, sems)


def finish(core, straight, crossed):
    _, chunk, width = straight.shape
    (out,) = call(
        finish_kernel,
        "finish",
        (SMEM, VMEM, VMEM),
        [like(straight, (2, 2 * chunk, width))],
        (HBM,),
        [pltpu.SemaphoreType.DMA((4,))],
    )(core, straight, crossed)
    return out


def swap(value):
    return lax.ppermute(value, "dc", [(0, 1), (1, 0)])


def scalars(*values):
    return jnp.stack([jnp.asarray(v).astype(jnp.int32) for v in values])


def body(features, w_self, w_neigh, bias, gain, hubs, tile_src, counts):
    graph, parity = lax.axis_index("sm"), lax.axis_index("se")
    core = lax.axis_index("dc")
    section = 2 * graph + parity
    here = core == parity
    n_hubs = hubs.shape[1]
    place = scalars(graph, parity, core)

    outgoing, packed = front(hubs[:, :, 0], features, w_self, w_neigh, bias, gain)
    gathered = lax.all_gather(packed, SECTION + ("dc",))
    received = lax.all_to_all(outgoing, CORES, 0, 0, tiled=True)

    blocks = jnp.maximum(lax.dynamic_index_in_dim(hubs, graph, 0, keepdims=False).reshape(-1), 0)
    lists = jnp.concatenate(
        [blocks, lax.dynamic_index_in_dim(tile_src, graph, 0, keepdims=False).reshape(-1)]
    )
    lists = jnp.where(here, lists, swap(lists))
    blocks, tiles = lists[:n_hubs], lists[n_hubs:]
    counts, outgoing = lax.optimization_barrier((counts, outgoing))
    tile_counts, inverse = tally(place, counts)
    h, tile_counts, inverse = ready(
        place, features, tile_counts, inverse, swap(features), swap(tile_counts), swap(inverse)
    )
    core_ref, kept = scalars(core), []
    for layer in range(N_LAYERS):
        if layer > 0:
            received = lax.all_to_all(outgoing, CHIPS, 0, 0, tiled=True)
        else:
            received, gathered = lax.optimization_barrier((received, gathered))
        mean_mine = aggregate(core_ref, tiles, h, received, tile_counts, inverse)
        mean_other = swap(mean_mine)
        if layer < N_LAYERS - 1:
            h, outgoing = dense(layer, core_ref, blocks, h, mean_mine, mean_other, gathered)
            kept.append(h)
        else:
            leaving = last_dense(core_ref, h, mean_mine, mean_other, gathered, kept[:-1])
    straight = lax.all_to_all(leaving, SECTION, 0, 0, tiled=True)
    theirs = [lax.dynamic_index_in_dim(straight, 2 * g + 1 - core, 0, keepdims=False) for g in range(2)]
    results = finish(core_ref, straight, swap(jnp.stack(theirs)))
    return results[None]


def solution(mesh):
    n_section, n_dp = mesh.shape["section"], mesh.shape["dp"]
    units = Mesh(mesh.devices.reshape(2, n_section // 2, n_dp // 2 // SIDE, SIDE, 2), SECTION + PARTS)
    placed = (
        P(None, PARTS, None),
        P(SECTION, None, None),
        P(SECTION, None, None),
        P(SECTION, None),
        P(SECTION, None),
        P(None, None, PARTS),
        P(None, PARTS, None),
        P(None, PARTS, None, None, None),
    )
    return jax.shard_map(
        body, mesh=units, in_specs=placed, out_specs=P(SECTION, None, PARTS, None), check_vma=False
    )
```

time: 784 us -> 213 us (0.27)
  waiting for transfers between devices: 336 us -> 47.6 us
  blocking collectives: 204 us -> 98.4 us
  other arithmetic: 83.7 us -> 0.33 us
  local copies, waits for them, and re-layouts: 88.7 us -> 9.93 us
  matrix products: 43.3 us -> 0 us
  Pallas kernels: 0 us -> 25.4 us
  between operations: 0.81 us -> 13.6 us
    all_to_all x2, waiting for transfers between devices: 201 us -> 34.8 us  [the longest x1 24.6 us: body(): straight = lax.all_to_all(leaving, SECTION, 0, 0, tiled=True)]
    ppermute x3 -> x9, waiting for transfers between devices: 136 us -> 12.8 us  [swap(): return lax.ppermute(value, 'dc', [(0, 1), (1, 0)])]
    all_to_all x2 -> x3, blocking collectives: 204 us -> 98.4 us  [body(): received = lax.all_to_all(outgoing, CHIPS, 0, 0, tiled=True)]
    gather x11 -> x0, local copies, waits for them, and re-layouts: 69.8 us -> none  [the longest x6 44.8 us: sage_layer(): source[chosen]]
    dot_general x12 -> x0, matrix products: 43.3 us -> none  [the longest x4 29.9 us: sage_layer(): jnp.einsum('gbjvu,gbjud->gbvd', tile_counts.astype(jnp.bfloat16), gathere...]
    select_n x7 -> x1, other arithmetic: 35 us -> 0.08 us  [body(): lists = jnp.where(here, lists, swap(lists))]
    concatenate x4 -> x1, other arithmetic: 31.1 us -> 0.08 us  [body(): jnp.concatenate([blocks, lax.dynamic_index_in_dim(tile_src, graph, 0, kee...]
    pallas_call x0 -> x12, Pallas kernels: none -> 25.4 us  [the longest x3 6.4 us: dense(): call(functools.partial(dense_kernel, layer), 'dense', (SMEM, SMEM) + (VME...]
  transfers between devices with their start and end apart: 5 -> 12, of which waited for: 5 -> 8; matrix products, arithmetic and copies ran while one was open for 2% -> 0% of each run, Pallas kernels for 0% -> 3%
where the time goes in v2:
time: 213 us; the launch traced here: 209 us
  blocking collectives  98.4 us (46%)
  waiting for transfers between devices  47.6 us (22%)
  Pallas kernels  25.4 us (12%)
  starting transfers between devices  14.2 us (7%)
  between operations  13.6 us (6%)
  local copies, waits for them, and re-layouts  9.93 us (5%)
    all_to_all x3, blocking collectives, body(): received = lax.all_to_all(outgoing, CHIPS, 0, 0, tiled=True)  98.4 us
    all_to_all x1, waiting for transfers between devices, body(): straight = lax.all_to_all(leaving, SECTION, 0, 0, tiled=True)  24.6 us
    ppermute x9, waiting for transfers between devices, swap(): return lax.ppermute(value, 'dc', [(0, 1), (1, 0)])  12.8 us
    all_to_all x1, waiting for transfers between devices, body(): received = lax.all_to_all(outgoing, CORES, 0, 0, tiled=True)  10.2 us
    unnamed x22, local copies, waits for them, and re-layouts  9.62 us
    all_to_all x1, starting transfers between devices, body(): received = lax.all_to_all(outgoing, CORES, 0, 0, tiled=True)  8.39 us
    pallas_call x3, Pallas kernels, dense(): call(functools.partial(dense_kernel, layer), 'dense', (SMEM, SMEM) + (VME...  6.4 us
    pallas_call x4, Pallas kernels, aggregate(): call(aggregate_kernel, 'aggregate', (SMEM, SMEM, VMEM, VMEM, VMEM, VMEM),...  5.99 us
  transfers between devices with their start and end apart: 12, of which 8 were waited for; matrix products, arithmetic and copies ran while one was open for 0% of the time, Pallas kernels for 3%

profile of v2, /device:TPU:24, one launch (start us, length us, event | category | flops | bytes accessed | tf_op | source)
XLA Modules:
  0.0 209.5 jit_solution(7734493677977839291)
XLA Ops:
  6.5 4.7 %front.1 = (bf16[32,128,256]{2,1,0:T(8,128)(2,1)}, bf16[528,512]{1,0:T(8,128)(2,1)}) custom-call(s32[2,32]{1,0:T(2,128)} %bitcast.16, bf16[2,1024,512]{2,1,0:T(8,128)(2,1)} %refs_0_.1, bf16[1,512,512]{2,1,0:T(8,128)(2,1)} %w_self.1, bf16[1,512,512]{2,1,0:T(8,128)(2,1)} %w_neigh.1, f32[1,512]{1,0:T(1,128)} %bias.1, f32[1,512]{1,0:T(1,128)} %gain.1), custom_call_target="tpu_custom_call" | custom-call | tf_op jit(solution)/shard_map/front/pallas_call | solution.py:107
  11.3 8.4 %all-to-all-start = ((bf16[32,128,256]{2,1,0:T(8,128)(2,1)}), bf16[32,128,256]{2,1,0:T(8,128)(2,1)}, u32[]{:S(2)}, u32[]{:S(2)}) async-start(bf16[32,128,256]{2,1,0:T(8,128)(2,1)} %get-tuple-element.21), calls=%async_computation | async-start | bytes 4194304 | tf_op jit(solution)/shard_map/all_to_all | solution.py:332
  19.8 2.9 %copy-done.5 = s32[2,8,6,128,128]{4,3,2,1,0:T(8,128)S(1)} copy-done((s32[2,8,6,128,128]{4,3,2,1,0:T(8,128)S(1)}, s32[2,8,6,128,128]{4,3,2,1,0:T(8,128)}, u32[]{:S(2)}) %copy-start.5) | copy-done | bytes 6291480
  22.7 3.6 %tally.1 = (bf16[8,128,768]{2,1,0:T(8,128)(2,1)}, f32[8,128,128]{2,1,0:T(8,128)S(1)}) custom-call(s32[3]{0:T(128)S(1)} %pad_add_fusion.1.place, s32[2,8,6,128,128]{4,3,2,1,0:T(8,128)S(1)} %copy-done.5), custom_call_target="tpu_custom_call" | custom-call | tf_op jit(solution)/shard_map/tally/pallas_call | solution.py:160
  28.1 2.6 %collective-permute-done = s32[80]{0:T(128)S(1)} collective-permute-done((s32[80]{0:T(128)S(1)}, s32[80]{0:T(128)S(1)}, u32[]{:S(2)}, u32[]{:S(2)}) %collective-permute-start) | collective-permute-done | bytes 352 | tf_op jit(solution)/shard_map/ppermute | solution.py:315
  31.7 1.7 copy-done.3
  35.4 2.4 %ready.1 = (bf16[1024,512]{1,0:T(8,128)(2,1)S(1)}, bf16[8,128,768]{2,1,0:T(8,128)(2,1)S(1)}, f32[8,128,128]{2,1,0:T(8,128)S(1)}) custom-call(s32[3]{0:T(128)S(1)} %pad_add_fusion.1.place, bf16[2,1024,512]{2,1,0:T(8,128)(2,1)S(1)} %copy-done.3, bf16[8,128,768]{2,1,0:T(8,128)(2,1)} %get-tuple-element.23.refs_1_, f32[8,128,128]{2,1,0:T(8,128)S(1)} %copy-done.7, ...), custom_call_target="tpu_custom_call" | custom-call | tf_op jit(solution)/shard_map/ready/pallas_call | solution.py:137
  37.8 10.2 %all-to-all-done.received = bf16[32,128,256]{2,1,0:T(8,128)(2,1)} async-done(((bf16[32,128,256]{2,1,0:T(8,128)(2,1)}), bf16[32,128,256]{2,1,0:T(8,128)(2,1)}, u32[]{:S(2)}, u32[]{:S(2)}) %all-to-all-start) | async-done | bytes 2097184 | tf_op jit(solution)/shard_map/all_to_all | solution.py:332
  48.0 2.5 %aggregate.4.mean_mine = bf16[1024,256]{1,0:T(8,128)(2,1)S(1)} custom-call(s32[1]{0:T(128)} %bitcast.core_ref, s32[48]{0:T(128)S(1)} %slice.7.tile_src, bf16[1024,512]{1,0:T(8,128)(2,1)S(1)} %get-tuple-element.25.h, bf16[32,128,256]{2,1,0:T(8,128)(2,1)} %all-to-all-done.received, bf16[8,128,768]{2,1,0:T(8,128)(2,1)S(1)} %get-tuple-element.28.counts, ...), custom_call_target="tpu_custom_call" | custom-call | tf_op jit(solution)/shard_map/aggregate/pallas_call | solution.py:199
  50.6 1.9 collective-permute-done.4.mean_other
  52.5 2.1 %dense.3 = (bf16[1024,512]{1,0:T(8,128)(2,1)S(1)}, bf16[32,128,256]{2,1,0:T(8,128)(2,1)S(1)}) custom-call(s32[1]{0:T(128)} %bitcast.core_ref, s32[32]{0:T(128)S(1)} %bitcast.13, bf16[1024,512]{1,0:T(8,128)(2,1)S(1)} %get-tuple-element.25.h, bf16[1024,256]{1,0:T(8,128)(2,1)S(1)} %aggregate.4.mean_mine, ...), custom_call_target="tpu_custom_call" | custom-call | tf_op jit(solution)/shard_map/dense/pallas_call | solution.py:246
  54.7 33.0 %all_to_all.25.received = bf16[32,128,256]{2,1,0:T(8,128)(2,1)S(1)} all-to-all(bf16[32,128,256]{2,1,0:T(8,128)(2,1)S(1)} %get-tuple-element.32), channel_id=1, replica_groups=mesh['sm'=2,'se'=2,'dz'=4,'dx'=4,'dc'=2] {'dx','se','dz'}, dimensions={0} | all-to-all | bytes 4194304 | tf_op jit(solution)/shard_map/all_to_all | solution.py:348
  88.9 1.9 collective-permute-done.5.mean_other
  90.8 2.1 %dense.4 = (bf16[1024,512]{1,0:T(8,128)(2,1)S(1)}, bf16[32,128,256]{2,1,0:T(8,128)(2,1)S(1)}) custom-call(s32[1]{0:T(128)} %bitcast.core_ref, s32[32]{0:T(128)S(1)} %bitcast.14, bf16[1024,512]{1,0:T(8,128)(2,1)S(1)} %get-tuple-element.31.h.rest_0_, bf16[1024,256]{1,0:T(8,128)(2,1)S(1)} %aggregate.5.mean_mine, ...), custom_call_target="tpu_custom_call" | custom-call | tf_op jit(solution)/shard_map/dense/pallas_call | solution.py:246
  92.9 32.7 %all_to_all.26.received = bf16[32,128,256]{2,1,0:T(8,128)(2,1)S(1)} all-to-all(bf16[32,128,256]{2,1,0:T(8,128)(2,1)S(1)} %get-tuple-element.34), channel_id=1, replica_groups=mesh['sm'=2,'se'=2,'dz'=4,'dx'=4,'dc'=2] {'dx','se','dz'}, dimensions={0} | all-to-all | bytes 4194304 | tf_op jit(solution)/shard_map/all_to_all | solution.py:348
  126.9 1.9 collective-permute-done.6.mean_other
  128.8 2.1 %dense.5 = (bf16[1024,512]{1,0:T(8,128)(2,1)S(1)}, bf16[32,128,256]{2,1,0:T(8,128)(2,1)S(1)}) custom-call(s32[1]{0:T(128)} %bitcast.core_ref, s32[32]{0:T(128)S(1)} %bitcast.15, bf16[1024,512]{1,0:T(8,128)(2,1)S(1)} %get-tuple-element.33.h.rest_1_, bf16[1024,256]{1,0:T(8,128)(2,1)S(1)} %aggregate.6.mean_mine, ...), custom_call_target="tpu_custom_call" | custom-call | tf_op jit(solution)/shard_map/dense/pallas_call | solution.py:246
  130.9 32.7 %all_to_all.27.received = bf16[32,128,256]{2,1,0:T(8,128)(2,1)S(1)} all-to-all(bf16[32,128,256]{2,1,0:T(8,128)(2,1)S(1)} %get-tuple-element.36), channel_id=1, replica_groups=mesh['sm'=2,'se'=2,'dz'=4,'dx'=4,'dc'=2] {'dx','se','dz'}, dimensions={0} | all-to-all | bytes 4194304 | tf_op jit(solution)/shard_map/all_to_all | solution.py:348
  164.9 1.9 collective-permute-done.7.mean_other
  167.9 1.3 copy-done.4
  169.2 4.6 %all-to-all-start.4 = ((bf16[4,512,512]{2,1,0:T(8,128)(2,1)}), bf16[4,512,512]{2,1,0:T(8,128)(2,1)S(1)}, u32[]{:S(2)}, u32[]{:S(2)}) async-start(bf16[4,512,512]{2,1,0:T(8,128)(2,1)} %copy-done.4), calls=%async_computation.4 | async-start | bytes 4194304 | tf_op jit(solution)/shard_map/all_to_all | solution.py:358
  173.8 24.6 %all-to-all-done.4.straight = bf16[4,512,512]{2,1,0:T(8,128)(2,1)S(1)} async-done(((bf16[4,512,512]{2,1,0:T(8,128)(2,1)}), bf16[4,512,512]{2,1,0:T(8,128)(2,1)S(1)}, u32[]{:S(2)}, u32[]{:S(2)}) %all-to-all-start.4) | async-done | bytes 2097184 | tf_op jit(solution)/shard_map/all_to_all | solution.py:358
  198.6 2.6 %collective-permute-done.8.crossed = bf16[2,512,512]{2,1,0:T(8,128)(2,1)S(1)} collective-permute-done((bf16[2,512,512]{2,1,0:T(8,128)(2,1)S(1)}, bf16[2,512,512]{2,1,0:T(8,128)(2,1)S(1)}, u32[]{:S(2)}, u32[]{:S(2)}) %collective-permute-start.8) | collective-permute-done | bytes 1048608 | tf_op jit(solution)/shard_map/ppermute | solution.py:315
  201.3 1.3 finish.1
  (48 shorter events, 10.2 us)
Async XLA Ops:
  6.5 21.1 %copy-start = (s32[2,8,6]{1,0,2:T(2,128)S(1)}, s32[2,8,6]{1,0,2:T(2,128)}, u32[]{:S(2)}) copy-start(s32[2,8,6]{1,0,2:T(2,128)} %param.14) | copy-start | bytes 1156
  6.5 4.7 %copy-start.2 = (bf16[2,1024,512]{2,1,0:T(8,128)(2,1)S(1)}, bf16[2,1024,512]{2,1,0:T(8,128)(2,1)}, u32[]{:S(2)}) copy-start(bf16[2,1024,512]{2,1,0:T(8,128)(2,1)} %refs_0_.1) | copy-start | bytes 6291460
  6.5 41.5 %all-gather.3.cloned.1.call-start = ((), (), s32[]{:S(2)}) async-start(), calls=%async_computation.5 | async-start | bytes 4866048 | tf_op jit(solution)/shard_map/all_gather | solution.py:331
  11.2 20.4 %collective-permute-start.1 = (bf16[2,1024,512]{2,1,0:T(8,128)(2,1)S(1)}, bf16[2,1024,512]{2,1,0:T(8,128)(2,1)}, u32[]{:S(2)}, u32[]{:S(2)}) collective-permute-start(bf16[2,1024,512]{2,1,0:T(8,128)(2,1)S(1)} %copy-done.2), channel_id=1, source_target_pairs={{0,1},{1,0},{2,3},{3,2},{4,5},{5,4},{6,7},{7,6},{8,9},{9,8},{10,11... | collective-permute-start | bytes 6291464 | tf_op jit(solution)/shard_map/ppermute | solution.py:315
  11.3 36.7 %all-to-all-start = ((bf16[32,128,256]{2,1,0:T(8,128)(2,1)}), bf16[32,128,256]{2,1,0:T(8,128)(2,1)}, u32[]{:S(2)}, u32[]{:S(2)}) async-start(bf16[32,128,256]{2,1,0:T(8,128)(2,1)} %get-tuple-element.21), calls=%async_computation | async-start | bytes 4194304 | tf_op jit(solution)/shard_map/all_to_all | solution.py:332
  19.8 2.9 %copy-start.5 = (s32[2,8,6,128,128]{4,3,2,1,0:T(8,128)S(1)}, s32[2,8,6,128,128]{4,3,2,1,0:T(8,128)}, u32[]{:S(2)}) copy-start(s32[2,8,6,128,128]{4,3,2,1,0:T(8,128)} %counts) | copy-start | bytes 18874372
  22.7 5.1 %copy-start.10 = (s32[2,32,1]{1,2,0:T(1,128)S(1)}, s32[2,32,1]{1,2,0:T(1,128)}, u32[]{:S(2)}) copy-start(s32[2,32,1]{1,2,0:T(1,128)} %param.13) | copy-start | bytes 772
  26.3 5.4 %collective-permute-start.2 = (bf16[8,128,768]{2,1,0:T(8,128)(2,1)}, bf16[8,128,768]{2,1,0:T(8,128)(2,1)}, u32[]{:S(2)}, u32[]{:S(2)}) collective-permute-start(bf16[8,128,768]{2,1,0:T(8,128)(2,1)} %get-tuple-element.23.refs_1_), channel_id=1, source_target_pairs={{0,1},{1,0},{2,3},{3,2},{4,5},{5,4},{6,7},{7,6},{8,9},{9,8},{10,11... | collective-permute-start | bytes 4718600 | tf_op jit(solution)/shard_map/ppermute | solution.py:315
  26.5 4.3 %collective-permute-start.3 = (f32[8,128,128]{2,1,0:T(8,128)S(1)}, f32[8,128,128]{2,1,0:T(8,128)S(1)}, u32[]{:S(2)}, u32[]{:S(2)}) collective-permute-start(f32[8,128,128]{2,1,0:T(8,128)S(1)} %get-tuple-element.24.refs_2_), channel_id=1, source_target_pairs={{0,1},{1,0},{2,3},{3,2},{4,5},{5,4},{6,7},{7,6},{8,9},{9,8},{10,11... | collective-permute-start | bytes 1572872 | tf_op jit(solution)/shard_map/ppermute | solution.py:315
  26.8 0.8 copy-start.6
  27.9 2.8 %collective-permute-start = (s32[80]{0:T(128)S(1)}, s32[80]{0:T(128)S(1)}, u32[]{:S(2)}, u32[]{:S(2)}) collective-permute-start(s32[80]{0:T(128)S(1)} %pad_add_fusion), channel_id=1, source_target_pairs={{0,1},{1,0},{2,3},{3,2},{4,5},{5,4},{6,7},{7,6},{8,9},{9,8},{10,11... | collective-permute-start | bytes 968 | tf_op jit(solution)/shard_map/ppermute | solution.py:315
  30.8 0.8 copy-start.8
  31.7 1.7 copy-start.3
  33.3 1.1 copy-start.7
  34.4 1.0 copy-start.9
  48.0 4.5 %copy-start.1 = (bf16[4224,512]{1,0:T(8,128)(2,1)S(1)}, bf16[4224,512]{1,0:T(8,128)(2,1)}, u32[]{:S(2)}) copy-start(bf16[4224,512]{1,0:T(8,128)(2,1)} %all-gather.3.cloned.1.call-done) | copy-start | bytes 12976132
  50.5 2.0 collective-permute-start.4
  88.8 2.0 collective-permute-start.5
  126.8 2.0 collective-permute-start.6
  164.8 2.0 collective-permute-start.7
  167.9 1.3 copy-start.4
  169.2 29.2 %all-to-all-start.4 = ((bf16[4,512,512]{2,1,0:T(8,128)(2,1)}), bf16[4,512,512]{2,1,0:T(8,128)(2,1)S(1)}, u32[]{:S(2)}, u32[]{:S(2)}) async-start(bf16[4,512,512]{2,1,0:T(8,128)(2,1)} %copy-done.4), calls=%async_computation.4 | async-start | bytes 4194304 | tf_op jit(solution)/shard_map/all_to_all | solution.py:358
  198.5 2.7 %collective-permute-start.8 = (bf16[2,512,512]{2,1,0:T(8,128)(2,1)S(1)}, bf16[2,512,512]{2,1,0:T(8,128)(2,1)S(1)}, u32[]{:S(2)}, u32[]{:S(2)}) collective-permute-start(bf16[2,512,512]{2,1,0:T(8,128)(2,1)S(1)} %pad_maximum_fusion), channel_id=1, source_target_pairs={{0,1},{1,0},{2,3},{3,2},{4,5},{5,4},{6,7},{7,6},{8,9},{9,8},{10,11... | collective-permute-start | bytes 3145736 | tf_op jit(solution)/shard_map/ppermute | solution.py:315
Sparse Core Ops, SparseCore 0:
  11.3 32.8 all-gather.2

commit v3 on v2

--- a/solution.py
+++ b/solution.py
@@ -311,6 +311,23 @@
     return out
 
 
+def theirs_kernel(core_ref, straight, out, sems):
+    core = core_ref[0]
+    run_copies([(straight.at[2 * g + 1 - core], out.at[g]) for g in range(2)], sems)
+
+
+def theirs(core, straight):
+    (out,) = call(
+        theirs_kernel,
+        "theirs",
+        (SMEM, VMEM),
+        [like(straight, (2,) + straight.shape[1:])],
+        (VMEM,),
+        [pltpu.SemaphoreType.DMA((2,))],
+    )(core, straight)
+    return out
+
+
 def swap(value):
     return lax.ppermute(value, "dc", [(0, 1), (1, 0)])
 
@@ -356,8 +373,7 @@
         else:
             leaving = last_dense(core_ref, h, mean_mine, mean_other, gathered, kept[:-1])
     straight = lax.all_to_all(leaving, SECTION, 0, 0, tiled=True)
-    theirs = [lax.dynamic_index_in_dim(straight, 2 * g + 1 - core, 0, keepdims=False) for g in range(2)]
-    results = finish(core_ref, straight, swap(jnp.stack(theirs)))
+    results = finish(core_ref, straight, swap(theirs(core_ref, straight)))
     return results[None]
 
 

time: 213 us -> 211 us (level)
  blocking collectives: 98.4 us -> 127 us
  waiting for transfers between devices: 47.6 us -> 23.1 us
  starting transfers between devices: 14.2 us -> 9.64 us
    all_to_all x0 -> x1, blocking collectives: none -> 29 us  [body(): straight = lax.all_to_all(leaving, SECTION, 0, 0, tiled=True)]
    all_to_all x1 -> x0, waiting for transfers between devices: 24.6 us -> none  [body(): straight = lax.all_to_all(leaving, SECTION, 0, 0, tiled=True)]
    all_to_all x1 -> x0, starting transfers between devices: 4.59 us -> none  [body(): straight = lax.all_to_all(leaving, SECTION, 0, 0, tiled=True)]
    unnamed x22 -> x20, local copies, waits for them, and re-layouts: 9.62 us -> 8.29 us
  transfers between devices with their start and end apart: 12 -> 11, of which waited for: 8 -> 7; matrix products, arithmetic and copies ran while one was open for 0% -> 0% of each run, Pallas kernels for 3% -> 3%
where the time goes in v3:
time: 211 us; the launch traced here: 208 us
  blocking collectives  127 us (60%)
  Pallas kernels  25.5 us (12%)
  waiting for transfers between devices  23.1 us (11%)
  between operations  13.6 us (6%)
  starting transfers between devices  9.64 us (5%)
  local copies, waits for them, and re-layouts  8.53 us (4%)
    all_to_all x3, blocking collectives, body(): received = lax.all_to_all(outgoing, CHIPS, 0, 0, tiled=True)  98.4 us
    all_to_all x1, blocking collectives, body(): straight = lax.all_to_all(leaving, SECTION, 0, 0, tiled=True)  29 us
    ppermute x9, waiting for transfers between devices, swap(): return lax.ppermute(value, 'dc', [(0, 1), (1, 0)])  12.8 us
    all_to_all x1, waiting for transfers between devices, body(): received = lax.all_to_all(outgoing, CORES, 0, 0, tiled=True)  10.2 us
    all_to_all x1, starting transfers between devices, body(): received = lax.all_to_all(outgoing, CORES, 0, 0, tiled=True)  8.39 us
    unnamed x20, local copies, waits for them, and re-layouts  8.29 us
    pallas_call x3, Pallas kernels, dense(): call(functools.partial(dense_kernel, layer), 'dense', (SMEM, SMEM) + (VME...  6.4 us
    pallas_call x4, Pallas kernels, aggregate(): call(aggregate_kernel, 'aggregate', (SMEM, SMEM, VMEM, VMEM, VMEM, VMEM),...  5.99 us
  transfers between devices with their start and end apart: 11, of which 7 were waited for; matrix products, arithmetic and copies ran while one was open for 0% of the time, Pallas kernels for 3%

profile of v3, /device:TPU:24, one launch (start us, length us, event | category | flops | bytes accessed | tf_op | source)
XLA Modules:
  0.0 207.9 jit_solution(76815423334426524)
XLA Ops:
  6.5 4.7 %front.1 = (bf16[32,128,256]{2,1,0:T(8,128)(2,1)}, bf16[528,512]{1,0:T(8,128)(2,1)}) custom-call(s32[2,32]{1,0:T(2,128)} %bitcast.16, bf16[2,1024,512]{2,1,0:T(8,128)(2,1)} %refs_0_.1, bf16[1,512,512]{2,1,0:T(8,128)(2,1)} %w_self.1, bf16[1,512,512]{2,1,0:T(8,128)(2,1)} %w_neigh.1, f32[1,512]{1,0:T(1,128)} %bias.1, f32[1,512]{1,0:T(1,128)} %gain.1), custom_call_target="tpu_custom_call" | custom-call | tf_op jit(solution)/shard_map/front/pallas_call | solution.py:107
  11.3 8.4 %all-to-all-start = ((bf16[32,128,256]{2,1,0:T(8,128)(2,1)}), bf16[32,128,256]{2,1,0:T(8,128)(2,1)}, u32[]{:S(2)}, u32[]{:S(2)}) async-start(bf16[32,128,256]{2,1,0:T(8,128)(2,1)} %get-tuple-element.21), calls=%async_computation | async-start | bytes 4194304 | tf_op jit(solution)/shard_map/all_to_all | solution.py:349
  19.8 2.9 %copy-done.4 = s32[2,8,6,128,128]{4,3,2,1,0:T(8,128)S(1)} copy-done((s32[2,8,6,128,128]{4,3,2,1,0:T(8,128)S(1)}, s32[2,8,6,128,128]{4,3,2,1,0:T(8,128)}, u32[]{:S(2)}) %copy-start.4) | copy-done | bytes 6291480
  22.7 3.6 %tally.1 = (bf16[8,128,768]{2,1,0:T(8,128)(2,1)}, f32[8,128,128]{2,1,0:T(8,128)S(1)}) custom-call(s32[3]{0:T(128)S(1)} %pad_add_fusion.1.place, s32[2,8,6,128,128]{4,3,2,1,0:T(8,128)S(1)} %copy-done.4), custom_call_target="tpu_custom_call" | custom-call | tf_op jit(solution)/shard_map/tally/pallas_call | solution.py:160
  28.1 2.6 %collective-permute-done = s32[80]{0:T(128)S(1)} collective-permute-done((s32[80]{0:T(128)S(1)}, s32[80]{0:T(128)S(1)}, u32[]{:S(2)}, u32[]{:S(2)}) %collective-permute-start) | collective-permute-done | bytes 352 | tf_op jit(solution)/shard_map/ppermute | solution.py:332
  31.6 1.7 copy-done.3
  35.4 2.4 %ready.1 = (bf16[1024,512]{1,0:T(8,128)(2,1)S(1)}, bf16[8,128,768]{2,1,0:T(8,128)(2,1)S(1)}, f32[8,128,128]{2,1,0:T(8,128)S(1)}) custom-call(s32[3]{0:T(128)S(1)} %pad_add_fusion.1.place, bf16[2,1024,512]{2,1,0:T(8,128)(2,1)S(1)} %copy-done.3, bf16[8,128,768]{2,1,0:T(8,128)(2,1)} %get-tuple-element.23.refs_1_, f32[8,128,128]{2,1,0:T(8,128)S(1)} %copy-done.6, ...), custom_call_target="tpu_custom_call" | custom-call | tf_op jit(solution)/shard_map/ready/pallas_call | solution.py:137
  37.8 10.2 %all-to-all-done.received = bf16[32,128,256]{2,1,0:T(8,128)(2,1)} async-done(((bf16[32,128,256]{2,1,0:T(8,128)(2,1)}), bf16[32,128,256]{2,1,0:T(8,128)(2,1)}, u32[]{:S(2)}, u32[]{:S(2)}) %all-to-all-start) | async-done | bytes 2097184 | tf_op jit(solution)/shard_map/all_to_all | solution.py:349
  48.0 2.5 %aggregate.4.mean_mine = bf16[1024,256]{1,0:T(8,128)(2,1)S(1)} custom-call(s32[1]{0:T(128)} %bitcast.core_ref, s32[48]{0:T(128)S(1)} %slice.7.tile_src, bf16[1024,512]{1,0:T(8,128)(2,1)S(1)} %get-tuple-element.25.h, bf16[32,128,256]{2,1,0:T(8,128)(2,1)} %all-to-all-done.received, bf16[8,128,768]{2,1,0:T(8,128)(2,1)S(1)} %get-tuple-element.28.counts, ...), custom_call_target="tpu_custom_call" | custom-call | tf_op jit(solution)/shard_map/aggregate/pallas_call | solution.py:199
  50.6 1.9 collective-permute-done.4.mean_other
  52.5 2.1 %dense.3 = (bf16[1024,512]{1,0:T(8,128)(2,1)S(1)}, bf16[32,128,256]{2,1,0:T(8,128)(2,1)S(1)}) custom-call(s32[1]{0:T(128)} %bitcast.core_ref, s32[32]{0:T(128)S(1)} %bitcast.13, bf16[1024,512]{1,0:T(8,128)(2,1)S(1)} %get-tuple-element.25.h, bf16[1024,256]{1,0:T(8,128)(2,1)S(1)} %aggregate.4.mean_mine, ...), custom_call_target="tpu_custom_call" | custom-call | tf_op jit(solution)/shard_map/dense/pallas_call | solution.py:246
  54.7 33.0 %all_to_all.25.received = bf16[32,128,256]{2,1,0:T(8,128)(2,1)S(1)} all-to-all(bf16[32,128,256]{2,1,0:T(8,128)(2,1)S(1)} %get-tuple-element.32), channel_id=1, replica_groups=mesh['sm'=2,'se'=2,'dz'=4,'dx'=4,'dc'=2] {'dx','se','dz'}, dimensions={0} | all-to-all | bytes 4194304 | tf_op jit(solution)/shard_map/all_to_all | solution.py:365
  87.7 1.2 aggregate.5.mean_mine
  88.9 1.9 collective-permute-done.5.mean_other
  90.8 2.1 %dense.4 = (bf16[1024,512]{1,0:T(8,128)(2,1)S(1)}, bf16[32,128,256]{2,1,0:T(8,128)(2,1)S(1)}) custom-call(s32[1]{0:T(128)} %bitcast.core_ref, s32[32]{0:T(128)S(1)} %bitcast.14, bf16[1024,512]{1,0:T(8,128)(2,1)S(1)} %get-tuple-element.31.h.rest_0_, bf16[1024,256]{1,0:T(8,128)(2,1)S(1)} %aggregate.5.mean_mine, ...), custom_call_target="tpu_custom_call" | custom-call | tf_op jit(solution)/shard_map/dense/pallas_call | solution.py:246
  93.0 32.7 %all_to_all.26.received = bf16[32,128,256]{2,1,0:T(8,128)(2,1)S(1)} all-to-all(bf16[32,128,256]{2,1,0:T(8,128)(2,1)S(1)} %get-tuple-element.34), channel_id=1, replica_groups=mesh['sm'=2,'se'=2,'dz'=4,'dx'=4,'dc'=2] {'dx','se','dz'}, dimensions={0} | all-to-all | bytes 4194304 | tf_op jit(solution)/shard_map/all_to_all | solution.py:365
  125.6 1.2 aggregate.6.mean_mine
  126.9 1.9 collective-permute-done.6.mean_other
  128.8 2.1 %dense.5 = (bf16[1024,512]{1,0:T(8,128)(2,1)S(1)}, bf16[32,128,256]{2,1,0:T(8,128)(2,1)S(1)}) custom-call(s32[1]{0:T(128)} %bitcast.core_ref, s32[32]{0:T(128)S(1)} %bitcast.15, bf16[1024,512]{1,0:T(8,128)(2,1)S(1)} %get-tuple-element.33.h.rest_1_, bf16[1024,256]{1,0:T(8,128)(2,1)S(1)} %aggregate.6.mean_mine, ...), custom_call_target="tpu_custom_call" | custom-call | tf_op jit(solution)/shard_map/dense/pallas_call | solution.py:246
  130.9 32.7 %all_to_all.27.received = bf16[32,128,256]{2,1,0:T(8,128)(2,1)S(1)} all-to-all(bf16[32,128,256]{2,1,0:T(8,128)(2,1)S(1)} %get-tuple-element.36), channel_id=1, replica_groups=mesh['sm'=2,'se'=2,'dz'=4,'dx'=4,'dc'=2] {'dx','se','dz'}, dimensions={0} | all-to-all | bytes 4194304 | tf_op jit(solution)/shard_map/all_to_all | solution.py:365
  164.9 1.9 collective-permute-done.7.mean_other
  167.9 29.0 %all_to_all.28.straight = bf16[4,512,512]{2,1,0:T(8,128)(2,1)S(1)} all-to-all(bf16[4,512,512]{2,1,0:T(8,128)(2,1)S(1)} %last_dense.1), channel_id=1, replica_groups=mesh['sm'=2,'se'=2,'dz'=4,'dx'=4,'dc'=2] {'sm','se'}, dimensions={0} | all-to-all | bytes 4194304 | tf_op jit(solution)/shard_map/all_to_all | solution.py:375
  197.0 2.6 %collective-permute-done.8.crossed = bf16[2,512,512]{2,1,0:T(8,128)(2,1)S(1)} collective-permute-done((bf16[2,512,512]{2,1,0:T(8,128)(2,1)S(1)}, bf16[2,512,512]{2,1,0:T(8,128)(2,1)S(1)}, u32[]{:S(2)}, u32[]{:S(2)}) %collective-permute-start.8) | collective-permute-done | bytes 1048608 | tf_op jit(solution)/shard_map/ppermute | solution.py:332
  199.7 1.3 finish.1
  (44 shorter events, 7.8 us)
Async XLA Ops:
  6.5 21.1 %copy-start = (s32[2,8,6]{1,0,2:T(2,128)S(1)}, s32[2,8,6]{1,0,2:T(2,128)}, u32[]{:S(2)}) copy-start(s32[2,8,6]{1,0,2:T(2,128)} %param.14) | copy-start | bytes 1156
  6.5 4.7 %copy-start.2 = (bf16[2,1024,512]{2,1,0:T(8,128)(2,1)S(1)}, bf16[2,1024,512]{2,1,0:T(8,128)(2,1)}, u32[]{:S(2)}) copy-start(bf16[2,1024,512]{2,1,0:T(8,128)(2,1)} %refs_0_.1) | copy-start | bytes 6291460
  6.5 41.5 %all-gather.3.cloned.1.call-start = ((), (), s32[]{:S(2)}) async-start(), calls=%async_computation.5 | async-start | bytes 4866048 | tf_op jit(solution)/shard_map/all_gather | solution.py:348
  11.2 20.4 %collective-permute-start.1 = (bf16[2,1024,512]{2,1,0:T(8,128)(2,1)S(1)}, bf16[2,1024,512]{2,1,0:T(8,128)(2,1)}, u32[]{:S(2)}, u32[]{:S(2)}) collective-permute-start(bf16[2,1024,512]{2,1,0:T(8,128)(2,1)S(1)} %copy-done.2), channel_id=1, source_target_pairs={{0,1},{1,0},{2,3},{3,2},{4,5},{5,4},{6,7},{7,6},{8,9},{9,8},{10,11... | collective-permute-start | bytes 6291464 | tf_op jit(solution)/shard_map/ppermute | solution.py:332
  11.3 36.7 %all-to-all-start = ((bf16[32,128,256]{2,1,0:T(8,128)(2,1)}), bf16[32,128,256]{2,1,0:T(8,128)(2,1)}, u32[]{:S(2)}, u32[]{:S(2)}) async-start(bf16[32,128,256]{2,1,0:T(8,128)(2,1)} %get-tuple-element.21), calls=%async_computation | async-start | bytes 4194304 | tf_op jit(solution)/shard_map/all_to_all | solution.py:349
  19.8 2.9 %copy-start.4 = (s32[2,8,6,128,128]{4,3,2,1,0:T(8,128)S(1)}, s32[2,8,6,128,128]{4,3,2,1,0:T(8,128)}, u32[]{:S(2)}) copy-start(s32[2,8,6,128,128]{4,3,2,1,0:T(8,128)} %counts) | copy-start | bytes 18874372
  22.7 5.1 %copy-start.9 = (s32[2,32,1]{1,2,0:T(1,128)S(1)}, s32[2,32,1]{1,2,0:T(1,128)}, u32[]{:S(2)}) copy-start(s32[2,32,1]{1,2,0:T(1,128)} %param.13) | copy-start | bytes 772
  26.3 5.4 %collective-permute-start.2 = (bf16[8,128,768]{2,1,0:T(8,128)(2,1)}, bf16[8,128,768]{2,1,0:T(8,128)(2,1)}, u32[]{:S(2)}, u32[]{:S(2)}) collective-permute-start(bf16[8,128,768]{2,1,0:T(8,128)(2,1)} %get-tuple-element.23.refs_1_), channel_id=1, source_target_pairs={{0,1},{1,0},{2,3},{3,2},{4,5},{5,4},{6,7},{7,6},{8,9},{9,8},{10,11... | collective-permute-start | bytes 4718600 | tf_op jit(solution)/shard_map/ppermute | solution.py:332
  26.5 4.3 %collective-permute-start.3 = (f32[8,128,128]{2,1,0:T(8,128)S(1)}, f32[8,128,128]{2,1,0:T(8,128)S(1)}, u32[]{:S(2)}, u32[]{:S(2)}) collective-permute-start(f32[8,128,128]{2,1,0:T(8,128)S(1)} %get-tuple-element.24.refs_2_), channel_id=1, source_target_pairs={{0,1},{1,0},{2,3},{3,2},{4,5},{5,4},{6,7},{7,6},{8,9},{9,8},{10,11... | collective-permute-start | bytes 1572872 | tf_op jit(solution)/shard_map/ppermute | solution.py:332
  26.8 0.8 copy-start.5
  27.9 2.8 %collective-permute-start = (s32[80]{0:T(128)S(1)}, s32[80]{0:T(128)S(1)}, u32[]{:S(2)}, u32[]{:S(2)}) collective-permute-start(s32[80]{0:T(128)S(1)} %pad_add_fusion), channel_id=1, source_target_pairs={{0,1},{1,0},{2,3},{3,2},{4,5},{5,4},{6,7},{7,6},{8,9},{9,8},{10,11... | collective-permute-start | bytes 968 | tf_op jit(solution)/shard_map/ppermute | solution.py:332
  30.8 0.8 copy-start.7
  31.6 1.7 copy-start.3
  33.3 1.1 copy-start.6
  34.4 1.0 copy-start.8
  48.0 4.5 %copy-start.1 = (bf16[4224,512]{1,0:T(8,128)(2,1)S(1)}, bf16[4224,512]{1,0:T(8,128)(2,1)}, u32[]{:S(2)}) copy-start(bf16[4224,512]{1,0:T(8,128)(2,1)} %all-gather.3.cloned.1.call-done) | copy-start | bytes 12976132
  50.5 2.0 collective-permute-start.4
  88.8 2.0 collective-permute-start.5
  126.8 2.0 collective-permute-start.6
  164.8 2.0 collective-permute-start.7
  196.9 2.7 %collective-permute-start.8 = (bf16[2,512,512]{2,1,0:T(8,128)(2,1)S(1)}, bf16[2,512,512]{2,1,0:T(8,128)(2,1)S(1)}, u32[]{:S(2)}, u32[]{:S(2)}) collective-permute-start(bf16[2,512,512]{2,1,0:T(8,128)(2,1)S(1)} %theirs.1), channel_id=1, source_target_pairs={{0,1},{1,0},{2,3},{3,2},{4,5},{5,4},{6,7},{7,6},{8,9},{9,8},{10,11... | collective-permute-start | bytes 3145736 | tf_op jit(solution)/shard_map/ppermute | solution.py:332
Sparse Core Ops, SparseCore 0:
  11.3 32.8 all-gather.2

commit v4 on v3

--- a/solution.py
+++ b/solution.py
@@ -177,11 +177,13 @@
     )(place, counts)
 
 
-def aggregate_kernel(core_ref, tile_src, h, received, counts, inverse, out):
+def aggregate_kernel(last, core_ref, tile_src, h, received, counts, inverse, *outs):
     n_blocks = counts.shape[0]
     tiles = counts.shape[2] // ROWS
-    cols = part(core_ref[0], out.shape[1])
-    for b in range(n_blocks):
+    core, width = core_ref[0], outs[0].shape[1]
+    cols = part(core, width)
+    for i in range(n_blocks):
+        b = lax.rem(n_blocks // 2 * (1 - core) + i, n_blocks) if last else i
         picked = []
         for j in range(tiles):
             slot = tile_src[b * tiles + j]
@@ -190,124 +192,143 @@
             picked.append(lax.select(slot < n_blocks, near, received[sender]))
         summed = jnp.dot(counts[b], jnp.concatenate(picked, axis=0), preferred_element_type=jnp.float32)
         scale = inverse[b]
-        scale = jnp.concatenate([scale] * (out.shape[1] // ROWS), axis=1)
-        out[b * ROWS : (b + 1) * ROWS, :] = (summed * scale).astype(out.dtype)
-
-
-def aggregate(core, tile_src, h, received, counts, inverse):
+        scale = jnp.concatenate([scale] * (width // ROWS), axis=1)
+        per_out = n_blocks // len(outs)
+        begin = i % per_out * ROWS
+        outs[i // per_out][begin : begin + ROWS, :] = (summed * scale).astype(h.dtype)
+
+
+def aggregate(last, core, tile_src, h, received, counts, inverse):
     rows, width = h.shape
-    (out,) = call(
-        aggregate_kernel,
+    n_outs = 2 if last else 1
+    outs = call(
+        functools.partial(aggregate_kernel, last),
         "aggregate",
         (SMEM, SMEM, VMEM, VMEM, VMEM, VMEM),
-        [like(h, (rows, width // 2))],
+        [like(h, (rows // n_outs, width // 2))] * n_outs,
+        (VMEM,) * n_outs,
+    )(core, tile_src, h, received, counts, inverse)
+    return outs[0], outs[-1]
+
+
+def own_products_kernel(layer, core_ref, h, mean_mine, gathered, pre):
+    core, width = core_ref[0], h.shape[1]
+    parts = gathered[2 * layer, width : width + SPLIT_ROWS, :].astype(jnp.float32)
+    bias = ((parts[4:6] + parts[2:4]) + parts[0:2])[0:1]
+    right = jnp.concatenate(
+        [gathered[2 * layer, 0:width, :], gathered[2 * layer + 1, part(core, width // 2), :]], axis=0
+    )
+    n_chunks = pre.shape[0] // CHUNK
+    for c in range(n_chunks):
+        rows = pl.ds(c * CHUNK, CHUNK)
+        h_rows = rows if pre.shape[0] == h.shape[0] else part(core * n_chunks + c, CHUNK)
+        left = jnp.concatenate([h[h_rows, :], mean_mine[rows, :]], axis=1)
+        pre[rows, :] = jnp.dot(left, right, preferred_element_type=jnp.float32) + bias
+
+
+def own_products(layer, core, h, mean_mine, gathered):
+    (out,) = call(
+        functools.partial(own_products_kernel, layer),
+        "own_products",
+        (SMEM, VMEM, VMEM, VMEM),
+        [jax.ShapeDtypeStruct((mean_mine.shape[0], h.shape[1]), jnp.float32)],
         (VMEM,),
-    )(core, tile_src, h, received, counts, inverse)
+    )(core, h, mean_mine, gathered)
     return out
 
 
-def layer_rows(layer, core, rows, h, mean_mine, mean_other, gathered, pre):
-    width = h.shape[1]
-    half = width // 2
+def layer_rows(layer, core, c, pre, mean_other, gathered, summed):
+    width = pre.shape[1]
     parts = gathered[2 * layer, width : width + SPLIT_ROWS, :].astype(jnp.float32)
-    affine = (parts[4:6] + parts[2:4]) + parts[0:2]
-    bias, gain = affine[0:1], affine[1:2]
-    left = jnp.concatenate([h[rows, :], mean_mine[rows, :], mean_other[rows, :]], axis=1)
-    right = jnp.concatenate(
-        [
-            gathered[2 * layer, 0:width, :],
-            gathered[2 * layer + 1, part(core, half), :],
-            gathered[2 * layer + 1, part(1 - core, half), :],
-        ],
-        axis=0,
-    )
-    pre[...] = jnp.dot(left, right, preferred_element_type=jnp.float32)
+    gain = ((parts[4:6] + parts[2:4]) + parts[0:2])[1:2]
+    right = gathered[2 * layer + 1, part(1 - core, width // 2), :]
+    rows = pl.ds(c * CHUNK, CHUNK)
+    summed[...] = pre[rows, :] + jnp.dot(mean_other[rows, :], right, preferred_element_type=jnp.float32)
     for begin in range(0, CHUNK, 64):
-        x = pre[begin : begin + 64, :] + bias
+        x = summed[begin : begin + 64, :]
         mu = jnp.mean(x, axis=1, keepdims=True)
         centred = x - mu
         var = jnp.mean(centred * centred, axis=1, keepdims=True)
-        yield begin, jnp.maximum(centred * lax.rsqrt(var + 1e-05) * gain, 0.0).astype(h.dtype)
-
-
-def dense_kernel(layer, core_ref, blocks, h, mean_mine, mean_other, gathered, h_out, outgoing, pre):
+        value = jnp.maximum(centred * lax.rsqrt(var + 1e-05) * gain, 0.0)
+        yield c * CHUNK + begin, value.astype(mean_other.dtype)
+
+
+def dense_kernel(layer, core_ref, blocks, pre, mean_other, gathered, h_out, outgoing, summed):
     core = core_ref[0]
-    for c in range(h.shape[0] // CHUNK):
-        rows = pl.ds(c * CHUNK, CHUNK)
-        for begin, value in layer_rows(layer, core, rows, h, mean_mine, mean_other, gathered, pre.at[c]):
-            begin = c * CHUNK + begin
+    for c in range(pre.shape[0] // CHUNK):
+        for begin, value in layer_rows(layer, core, c, pre, mean_other, gathered, summed.at[c]):
             h_out[begin : begin + 64, :] = value
     for j in range(outgoing.shape[0]):
         outgoing[j] = h_out[block_rows(blocks[reader_of(j)]), part(core, outgoing.shape[2])]
 
 
-def dense(layer, core, blocks, h, mean_mine, mean_other, gathered):
-    rows, width = h.shape
+def dense(layer, core, blocks, pre, mean_other, gathered):
+    rows, width = pre.shape
     return call(
         functools.partial(dense_kernel, layer),
         "dense",
-        (SMEM, SMEM) + (VMEM,) * 4,
-        [like(h), like(h, (blocks.shape[0], ROWS, width // 2))],
+        (SMEM, SMEM) + (VMEM,) * 3,
+        [like(mean_other, pre.shape), like(mean_other, (blocks.shape[0], ROWS, width // 2))],
         (VMEM, VMEM),
         [pltpu.VMEM((rows // CHUNK, CHUNK, width), jnp.float32)],
-    )(core, blocks, h, mean_mine, mean_other, gathered)
-
-
-def last_dense_kernel(core_ref, h, mean_mine, mean_other, gathered, *rest):
-    *kept, leaving, pre, sems = rest
+    )(core, blocks, pre, mean_other, gathered)
+
+
+def last_dense_kernel(core_ref, pre, mean_other, gathered, *rest):
+    *kept, leaving, summed, sems = rest
     core, last = core_ref[0], N_LAYERS - 1
     half_rows = leaving.shape[1]
     copies = [
         pltpu.make_async_copy(source.at[part(core, half_rows)], leaving.at[layer], sems.at[layer])
-        for layer, source in enumerate([*kept, h])
+        for layer, source in enumerate(kept)
     ]
     for copy in copies:
         copy.start()
-    n_chunks = half_rows // CHUNK
-    for c in range(n_chunks):
-        rows = part(core * n_chunks + c, CHUNK)
-        for begin, value in layer_rows(last, core, rows, h, mean_mine, mean_other, gathered, pre.at[c]):
-            begin = c * CHUNK + begin
+    for c in range(half_rows // CHUNK):
+        for begin, value in layer_rows(last, core, c, pre, mean_other, gathered, summed.at[c]):
             leaving[last, begin : begin + 64, :] = value
     for copy in copies:
         copy.wait()
 
 
-def last_dense(core, h, mean_mine, mean_other, gathered, kept):
-    rows, width = h.shape
+def last_dense(core, pre, mean_other, gathered, kept):
+    half_rows, width = pre.shape
     (out,) = call(
         last_dense_kernel,
         "last_dense",
-        (SMEM,) + (VMEM,) * 4 + (HBM,) * len(kept),
-        [like(h, (N_LAYERS, rows // 2, width))],
+        (SMEM,) + (VMEM,) * 3 + (HBM,) * len(kept),
+        [like(mean_other, (N_LAYERS, half_rows, width))],
         (VMEM,),
         [
-            pltpu.VMEM((rows // 2 // CHUNK, CHUNK, width), jnp.float32),
+            pltpu.VMEM((half_rows // CHUNK, CHUNK, width), jnp.float32),
             pltpu.SemaphoreType.DMA((N_LAYERS - 1,)),
         ],
-    )(core, h, mean_mine, mean_other, gathered, *kept)
+    )(core, pre, mean_other, gathered, *kept)
     return out
 
 
-def finish_kernel(core_ref, straight, crossed, out, sems):
-    core, chunk = core_ref[0], straight.shape[1]
+def finish_kernel(crossing, core_ref, source, *rest):
+    out, sems = rest[-2:]
+    core, chunk = core_ref[0], source.shape[1]
+    half = 1 - core if crossing else core
     pieces = []
     for g in range(2):
-        pieces.append((straight.at[2 * g + core], out.at[g, part(core, chunk)]))
-        pieces.append((crossed.at[g], out.at[g, part(1 - core, chunk)]))
+        piece = source.at[g] if crossing else source.at[2 * g + core]
+        pieces.append((piece, out.at[g, part(half, chunk)]))
     run_copies(pieces, sems)
 
 
-def finish(core, straight, crossed):
-    _, chunk, width = straight.shape
+def finish(crossing, core, source, *results):
+    _, chunk, width = source.shape
     (out,) = call(
-        finish_kernel,
+        functools.partial(finish_kernel, crossing),
         "finish",
-        (SMEM, VMEM, VMEM),
-        [like(straight, (2, 2 * chunk, width))],
+        (SMEM, VMEM) + (HBM,) * len(results),
+        [like(source, (2, 2 * chunk, width))],
         (HBM,),
-        [pltpu.SemaphoreType.DMA((4,))],
-    )(core, straight, crossed)
+        [pltpu.SemaphoreType.DMA((2,))],
+        input_output_aliases={2: 0} if crossing else {},
+    )(core, source, *results)
     return out
 
 
@@ -365,15 +386,18 @@
             received = lax.all_to_all(outgoing, CHIPS, 0, 0, tiled=True)
         else:
             received, gathered = lax.optimization_barrier((received, gathered))
-        mean_mine = aggregate(core_ref, tiles, h, received, tile_counts, inverse)
-        mean_other = swap(mean_mine)
-        if layer < N_LAYERS - 1:
-            h, outgoing = dense(layer, core_ref, blocks, h, mean_mine, mean_other, gathered)
+        last = layer == N_LAYERS - 1
+        theirs_too, mean_mine = aggregate(last, core_ref, tiles, h, received, tile_counts, inverse)
+        mean_other = swap(theirs_too)
+        pre = own_products(layer, core_ref, h, mean_mine, gathered)
+        if last:
+            leaving = last_dense(core_ref, pre, mean_other, gathered, kept)
+        else:
+            h, outgoing = dense(layer, core_ref, blocks, pre, mean_other, gathered)
             kept.append(h)
-        else:
-            leaving = last_dense(core_ref, h, mean_mine, mean_other, gathered, kept[:-1])
     straight = lax.all_to_all(leaving, SECTION, 0, 0, tiled=True)
-    results = finish(core_ref, straight, swap(theirs(core_ref, straight)))
+    crossed = swap(theirs(core_ref, straight))
+    results = finish(True, core_ref, crossed, finish(False, core_ref, straight))
     return results[None]
 
 

time: 211 us -> 209 us (level)
  waiting for transfers between devices: 23.1 us -> 17.9 us
  Pallas kernels: 25.5 us -> 27.8 us
    ppermute x9, waiting for transfers between devices: 12.8 us -> 7.62 us  [swap(): return lax.ppermute(value, 'dc', [(0, 1), (1, 0)])]
    pallas_call x6 -> x11, Pallas kernels: 8.37 us -> 12.2 us  [the longest x4 6.02 us: aggregate(): call(functools.partial(aggregate_kernel, last), 'aggregate', (SMEM, SMEM,...]
  transfers between devices with their start and end apart: 11 -> 11, of which waited for: 7 -> 7; matrix products, arithmetic and copies ran while one was open for 0% -> 0% of each run, Pallas kernels for 3% -> 5%
where the time goes in v4:
time: 209 us; the launch traced here: 205 us
  blocking collectives  127 us (61%)
  Pallas kernels  27.8 us (13%)
  waiting for transfers between devices  17.9 us (9%)
  between operations  13.6 us (7%)
  starting transfers between devices  9.64 us (5%)
  local copies, waits for them, and re-layouts  8.81 us (4%)
    all_to_all x3, blocking collectives, body(): received = lax.all_to_all(outgoing, CHIPS, 0, 0, tiled=True)  98.3 us
    all_to_all x1, blocking collectives, body(): straight = lax.all_to_all(leaving, SECTION, 0, 0, tiled=True)  29 us
    all_to_all x1, waiting for transfers between devices, body(): received = lax.all_to_all(outgoing, CORES, 0, 0, tiled=True)  10.2 us
    unnamed x20, local copies, waits for them, and re-layouts  8.57 us
    all_to_all x1, starting transfers between devices, body(): received = lax.all_to_all(outgoing, CORES, 0, 0, tiled=True)  8.39 us
    ppermute x9, waiting for transfers between devices, swap(): return lax.ppermute(value, 'dc', [(0, 1), (1, 0)])  7.62 us
    pallas_call x4, Pallas kernels, aggregate(): call(functools.partial(aggregate_kernel, last), 'aggregate', (SMEM, SMEM,...  6.02 us
    pallas_call x3, Pallas kernels, dense(): call(functools.partial(dense_kernel, layer), 'dense', (SMEM, SMEM) + (VME...  4.84 us
  transfers between devices with their start and end apart: 11, of which 7 were waited for; matrix products, arithmetic and copies ran while one was open for 0% of the time, Pallas kernels for 5%

profile of v4, /device:TPU:24, one launch (start us, length us, event | category | flops | bytes accessed | tf_op | source)
XLA Modules:
  0.0 205.2 jit_solution(15960903258749613016)
XLA Ops:
  6.5 4.6 %front.1 = (bf16[32,128,256]{2,1,0:T(8,128)(2,1)}, bf16[528,512]{1,0:T(8,128)(2,1)}) custom-call(s32[2,32]{1,0:T(2,128)} %bitcast.20, bf16[2,1024,512]{2,1,0:T(8,128)(2,1)} %refs_0_.1, bf16[1,512,512]{2,1,0:T(8,128)(2,1)} %w_self.1, bf16[1,512,512]{2,1,0:T(8,128)(2,1)} %w_neigh.1, f32[1,512]{1,0:T(1,128)} %bias.1, f32[1,512]{1,0:T(1,128)} %gain.1), custom_call_target="tpu_custom_call" | custom-call | tf_op jit(solution)/shard_map/front/pallas_call | solution.py:107
  11.3 8.4 %all-to-all-start = ((bf16[32,128,256]{2,1,0:T(8,128)(2,1)}), bf16[32,128,256]{2,1,0:T(8,128)(2,1)}, u32[]{:S(2)}, u32[]{:S(2)}) async-start(bf16[32,128,256]{2,1,0:T(8,128)(2,1)} %get-tuple-element.23), calls=%async_computation | async-start | bytes 4194304 | tf_op jit(solution)/shard_map/all_to_all | solution.py:370
  19.8 2.9 %copy-done.4 = s32[2,8,6,128,128]{4,3,2,1,0:T(8,128)S(1)} copy-done((s32[2,8,6,128,128]{4,3,2,1,0:T(8,128)S(1)}, s32[2,8,6,128,128]{4,3,2,1,0:T(8,128)}, u32[]{:S(2)}) %copy-start.4) | copy-done | bytes 6291480
  22.7 3.6 %tally.1 = (bf16[8,128,768]{2,1,0:T(8,128)(2,1)}, f32[8,128,128]{2,1,0:T(8,128)S(1)}) custom-call(s32[3]{0:T(128)S(1)} %pad_add_fusion.1.place, s32[2,8,6,128,128]{4,3,2,1,0:T(8,128)S(1)} %copy-done.4), custom_call_target="tpu_custom_call" | custom-call | tf_op jit(solution)/shard_map/tally/pallas_call | solution.py:160
  28.1 2.6 %collective-permute-done = s32[80]{0:T(128)S(1)} collective-permute-done((s32[80]{0:T(128)S(1)}, s32[80]{0:T(128)S(1)}, u32[]{:S(2)}, u32[]{:S(2)}) %collective-permute-start) | collective-permute-done | bytes 352 | tf_op jit(solution)/shard_map/ppermute | solution.py:353
  31.7 1.7 copy-done.3
  33.3 1.1 copy-done.6
  34.4 1.0 copy-done.8
  35.4 2.4 %ready.1 = (bf16[1024,512]{1,0:T(8,128)(2,1)S(1)}, bf16[8,128,768]{2,1,0:T(8,128)(2,1)S(1)}, f32[8,128,128]{2,1,0:T(8,128)S(1)}) custom-call(s32[3]{0:T(128)S(1)} %pad_add_fusion.1.place, bf16[2,1024,512]{2,1,0:T(8,128)(2,1)S(1)} %copy-done.3, bf16[8,128,768]{2,1,0:T(8,128)(2,1)} %get-tuple-element.25.refs_1_, f32[8,128,128]{2,1,0:T(8,128)S(1)} %copy-done.6, ...), custom_call_target="tpu_custom_call" | custom-call | tf_op jit(solution)/shard_map/ready/pallas_call | solution.py:137
  37.8 10.2 %all-to-all-done.received = bf16[32,128,256]{2,1,0:T(8,128)(2,1)} async-done(((bf16[32,128,256]{2,1,0:T(8,128)(2,1)}), bf16[32,128,256]{2,1,0:T(8,128)(2,1)}, u32[]{:S(2)}, u32[]{:S(2)}) %all-to-all-start) | async-done | bytes 2097184 | tf_op jit(solution)/shard_map/all_to_all | solution.py:370
  48.0 2.5 %aggregate.4.mean_mine = bf16[1024,256]{1,0:T(8,128)(2,1)S(1)} custom-call(s32[1]{0:T(128)} %bitcast.core_ref, s32[48]{0:T(128)S(1)} %slice.7.tile_src, bf16[1024,512]{1,0:T(8,128)(2,1)S(1)} %get-tuple-element.27.h, bf16[32,128,256]{2,1,0:T(8,128)(2,1)} %all-to-all-done.received, bf16[8,128,768]{2,1,0:T(8,128)(2,1)S(1)} %get-tuple-element.30.counts, ...), custom_call_target="tpu_custom_call" | custom-call | tf_op jit(solution)/shard_map/aggregate/pallas_call | solution.py:204
  52.5 1.6 dense.3
  54.1 33.0 %all_to_all.25.received = bf16[32,128,256]{2,1,0:T(8,128)(2,1)S(1)} all-to-all(bf16[32,128,256]{2,1,0:T(8,128)(2,1)S(1)} %get-tuple-element.34), channel_id=1, replica_groups=mesh['sm'=2,'se'=2,'dz'=4,'dx'=4,'dc'=2] {'dx','se','dz'}, dimensions={0} | all-to-all | bytes 4194304 | tf_op jit(solution)/shard_map/all_to_all | solution.py:386
  87.1 1.2 aggregate.5.mean_mine
  90.3 1.6 dense.4
  91.9 32.7 %all_to_all.26.received = bf16[32,128,256]{2,1,0:T(8,128)(2,1)S(1)} all-to-all(bf16[32,128,256]{2,1,0:T(8,128)(2,1)S(1)} %get-tuple-element.36), channel_id=1, replica_groups=mesh['sm'=2,'se'=2,'dz'=4,'dx'=4,'dc'=2] {'dx','se','dz'}, dimensions={0} | all-to-all | bytes 4194304 | tf_op jit(solution)/shard_map/all_to_all | solution.py:386
  124.6 1.2 aggregate.6.mean_mine
  127.8 1.6 dense.5
  129.4 32.7 %all_to_all.27.received = bf16[32,128,256]{2,1,0:T(8,128)(2,1)S(1)} all-to-all(bf16[32,128,256]{2,1,0:T(8,128)(2,1)S(1)} %get-tuple-element.38), channel_id=1, replica_groups=mesh['sm'=2,'se'=2,'dz'=4,'dx'=4,'dc'=2] {'dx','se','dz'}, dimensions={0} | all-to-all | bytes 4194304 | tf_op jit(solution)/shard_map/all_to_all | solution.py:386
  162.1 1.2 aggregate.7
  165.6 29.0 %all_to_all.28.straight.source = bf16[4,512,512]{2,1,0:T(8,128)(2,1)S(1)} all-to-all(bf16[4,512,512]{2,1,0:T(8,128)(2,1)S(1)} %last_dense.1), channel_id=1, replica_groups=mesh['sm'=2,'se'=2,'dz'=4,'dx'=4,'dc'=2] {'sm','se'}, dimensions={0} | all-to-all | bytes 4194304 | tf_op jit(solution)/shard_map/all_to_all | solution.py:398
  194.8 1.0 finish.2.rest_0_
  195.7 1.7 collective-permute-done.8.source
  197.4 1.0 finish.3
  (49 shorter events, 11.4 us)
Async XLA Ops:
  6.5 21.1 %copy-start = (s32[2,8,6]{1,0,2:T(2,128)S(1)}, s32[2,8,6]{1,0,2:T(2,128)}, u32[]{:S(2)}) copy-start(s32[2,8,6]{1,0,2:T(2,128)} %param.14) | copy-start | bytes 1156
  6.5 4.7 %copy-start.2 = (bf16[2,1024,512]{2,1,0:T(8,128)(2,1)S(1)}, bf16[2,1024,512]{2,1,0:T(8,128)(2,1)}, u32[]{:S(2)}) copy-start(bf16[2,1024,512]{2,1,0:T(8,128)(2,1)} %refs_0_.1) | copy-start | bytes 6291460
  6.5 41.5 %all-gather.3.cloned.1.call-start = ((), (), s32[]{:S(2)}) async-start(), calls=%async_computation.5 | async-start | bytes 4866048 | tf_op jit(solution)/shard_map/all_gather | solution.py:369
  11.2 20.4 %collective-permute-start.1 = (bf16[2,1024,512]{2,1,0:T(8,128)(2,1)S(1)}, bf16[2,1024,512]{2,1,0:T(8,128)(2,1)}, u32[]{:S(2)}, u32[]{:S(2)}) collective-permute-start(bf16[2,1024,512]{2,1,0:T(8,128)(2,1)S(1)} %copy-done.2), channel_id=1, source_target_pairs={{0,1},{1,0},{2,3},{3,2},{4,5},{5,4},{6,7},{7,6},{8,9},{9,8},{10,11... | collective-permute-start | bytes 6291464 | tf_op jit(solution)/shard_map/ppermute | solution.py:353
  11.3 36.7 %all-to-all-start = ((bf16[32,128,256]{2,1,0:T(8,128)(2,1)}), bf16[32,128,256]{2,1,0:T(8,128)(2,1)}, u32[]{:S(2)}, u32[]{:S(2)}) async-start(bf16[32,128,256]{2,1,0:T(8,128)(2,1)} %get-tuple-element.23), calls=%async_computation | async-start | bytes 4194304 | tf_op jit(solution)/shard_map/all_to_all | solution.py:370
  19.8 2.9 %copy-start.4 = (s32[2,8,6,128,128]{4,3,2,1,0:T(8,128)S(1)}, s32[2,8,6,128,128]{4,3,2,1,0:T(8,128)}, u32[]{:S(2)}) copy-start(s32[2,8,6,128,128]{4,3,2,1,0:T(8,128)} %counts) | copy-start | bytes 18874372
  22.7 5.1 %copy-start.9 = (s32[2,32,1]{1,2,0:T(1,128)S(1)}, s32[2,32,1]{1,2,0:T(1,128)}, u32[]{:S(2)}) copy-start(s32[2,32,1]{1,2,0:T(1,128)} %param.13) | copy-start | bytes 772
  26.3 5.4 %collective-permute-start.2 = (bf16[8,128,768]{2,1,0:T(8,128)(2,1)}, bf16[8,128,768]{2,1,0:T(8,128)(2,1)}, u32[]{:S(2)}, u32[]{:S(2)}) collective-permute-start(bf16[8,128,768]{2,1,0:T(8,128)(2,1)} %get-tuple-element.25.refs_1_), channel_id=1, source_target_pairs={{0,1},{1,0},{2,3},{3,2},{4,5},{5,4},{6,7},{7,6},{8,9},{9,8},{10,11... | collective-permute-start | bytes 4718600 | tf_op jit(solution)/shard_map/ppermute | solution.py:353
  26.5 4.3 %collective-permute-start.3 = (f32[8,128,128]{2,1,0:T(8,128)S(1)}, f32[8,128,128]{2,1,0:T(8,128)S(1)}, u32[]{:S(2)}, u32[]{:S(2)}) collective-permute-start(f32[8,128,128]{2,1,0:T(8,128)S(1)} %get-tuple-element.26.refs_2_), channel_id=1, source_target_pairs={{0,1},{1,0},{2,3},{3,2},{4,5},{5,4},{6,7},{7,6},{8,9},{9,8},{10,11... | collective-permute-start | bytes 1572872 | tf_op jit(solution)/shard_map/ppermute | solution.py:353
  26.8 0.8 copy-start.5
  27.9 2.8 %collective-permute-start = (s32[80]{0:T(128)S(1)}, s32[80]{0:T(128)S(1)}, u32[]{:S(2)}, u32[]{:S(2)}) collective-permute-start(s32[80]{0:T(128)S(1)} %pad_add_fusion), channel_id=1, source_target_pairs={{0,1},{1,0},{2,3},{3,2},{4,5},{5,4},{6,7},{7,6},{8,9},{9,8},{10,11... | collective-permute-start | bytes 968 | tf_op jit(solution)/shard_map/ppermute | solution.py:353
  30.8 0.8 copy-start.7
  31.7 1.7 copy-start.3
  33.3 1.1 copy-start.6
  34.4 1.0 copy-start.8
  48.0 2.9 %copy-start.1 = (bf16[4224,512]{1,0:T(8,128)(2,1)S(1)}, bf16[4224,512]{1,0:T(8,128)(2,1)}, u32[]{:S(2)}) copy-start(bf16[4224,512]{1,0:T(8,128)(2,1)} %all-gather.3.cloned.1.call-done) | copy-start | bytes 12976132
  50.5 2.0 collective-permute-start.4
  88.3 2.0 collective-permute-start.5
  125.8 2.0 collective-permute-start.6
  163.3 1.6 collective-permute-start.7
  194.7 2.7 %collective-permute-start.8 = (bf16[2,512,512]{2,1,0:T(8,128)(2,1)S(1)}, bf16[2,512,512]{2,1,0:T(8,128)(2,1)S(1)}, u32[]{:S(2)}, u32[]{:S(2)}) collective-permute-start(bf16[2,512,512]{2,1,0:T(8,128)(2,1)S(1)} %theirs.1), channel_id=1, source_target_pairs={{0,1},{1,0},{2,3},{3,2},{4,5},{5,4},{6,7},{7,6},{8,9},{9,8},{10,11... | collective-permute-start | bytes 3145736 | tf_op jit(solution)/shard_map/ppermute | solution.py:353
Sparse Core Ops, SparseCore 0:
  11.3 32.8 all-gather.2

commit v5 on v4

--- a/solution.py
+++ b/solution.py
@@ -69,7 +69,9 @@
     return x * (2 * SIDE) + e * SIDE + z
 
 
-def front_kernel(hubs, features, w_self, w_neigh, bias, gain, outgoing, packed, held, load_sem, w_sem, sems):
+def front_kernel(
+    hubs, features, w_self, w_neigh, bias, gain, outgoing, packed_out, held, packed, load_sem, w_sem, out_sem, sems
+):
     graph, parity, core = lax.axis_index("sm"), lax.axis_index("se"), lax.axis_index("dc")
     width = packed.shape[1]
     load = pltpu.make_async_copy(features.at[graph], held, load_sem)
@@ -98,6 +100,8 @@
         copies.append(pltpu.make_async_copy(source, outgoing.at[j], sems.at[j]))
         copies[-1].start()
     pltpu.make_async_copy(w_self.at[0], packed.at[pl.ds(0, width)], w_sem).wait()
+    copies.append(pltpu.make_async_copy(packed, packed_out, out_sem))
+    copies[-1].start()
     for copy in copies:
         copy.wait()
 
@@ -109,9 +113,11 @@
         "front",
         (SMEM, HBM, HBM, HBM, VMEM, VMEM),
         [like(features, (n_hubs, ROWS, width // 2)), like(w_self, (width + SPLIT_ROWS, width))],
-        (HBM, VMEM),
+        (HBM, HBM),
         [
             pltpu.VMEM((rows, width), features.dtype),
+            pltpu.VMEM((width + SPLIT_ROWS, width), w_self.dtype),
+            pltpu.SemaphoreType.DMA,
             pltpu.SemaphoreType.DMA,
             pltpu.SemaphoreType.DMA,
             pltpu.SemaphoreType.DMA((n_hubs,)),

time: 209 us -> 208 us (level)
  no operation moved by 1% of the time
where the time goes in v5:
time: 208 us; the launch traced here: 205 us
  blocking collectives  127 us (61%)
  Pallas kernels  27.2 us (13%)
  waiting for transfers between devices  17.9 us (9%)
  between operations  13.6 us (7%)
  starting transfers between devices  9.64 us (5%)
  local copies, waits for them, and re-layouts  8.81 us (4%)
    all_to_all x3, blocking collectives, body(): received = lax.all_to_all(outgoing, CHIPS, 0, 0, tiled=True)  98.3 us
    all_to_all x1, blocking collectives, body(): straight = lax.all_to_all(leaving, SECTION, 0, 0, tiled=True)  29 us
    all_to_all x1, waiting for transfers between devices, body(): received = lax.all_to_all(outgoing, CORES, 0, 0, tiled=True)  10.2 us
    unnamed x20, local copies, waits for them, and re-layouts  8.57 us
    all_to_all x1, starting transfers between devices, body(): received = lax.all_to_all(outgoing, CORES, 0, 0, tiled=True)  8.39 us
    ppermute x9, waiting for transfers between devices, swap(): return lax.ppermute(value, 'dc', [(0, 1), (1, 0)])  7.62 us
    pallas_call x4, Pallas kernels, aggregate(): call(functools.partial(aggregate_kernel, last), 'aggregate', (SMEM, SMEM,...  6.03 us
    pallas_call x3, Pallas kernels, dense(): call(functools.partial(dense_kernel, layer), 'dense', (SMEM, SMEM) + (VME...  4.84 us
  transfers between devices with their start and end apart: 11, of which 7 were waited for; matrix products, arithmetic and copies ran while one was open for 0% of the time, Pallas kernels for 5%

profile of v5, /device:TPU:24, one launch (start us, length us, event | category | flops | bytes accessed | tf_op | source)
XLA Modules:
  0.0 204.7 jit_solution(18105752132003812016)
XLA Ops:
  6.5 4.0 %front.1 = (bf16[32,128,256]{2,1,0:T(8,128)(2,1)}, bf16[528,512]{1,0:T(8,128)(2,1)}) custom-call(s32[2,32]{1,0:T(2,128)} %bitcast.20, bf16[2,1024,512]{2,1,0:T(8,128)(2,1)} %refs_0_.1, bf16[1,512,512]{2,1,0:T(8,128)(2,1)} %w_self.1, bf16[1,512,512]{2,1,0:T(8,128)(2,1)} %w_neigh.1, f32[1,512]{1,0:T(1,128)} %bias.1, f32[1,512]{1,0:T(1,128)} %gain.1), custom_call_target="tpu_custom_call" | custom-call | tf_op jit(solution)/shard_map/front/pallas_call | solution.py:111
  10.7 8.4 %all-to-all-start = ((bf16[32,128,256]{2,1,0:T(8,128)(2,1)}), bf16[32,128,256]{2,1,0:T(8,128)(2,1)}, u32[]{:S(2)}, u32[]{:S(2)}) async-start(bf16[32,128,256]{2,1,0:T(8,128)(2,1)} %get-tuple-element.23), calls=%async_computation | async-start | bytes 4194304 | tf_op jit(solution)/shard_map/all_to_all | solution.py:376
  19.2 2.9 %copy-done.4 = s32[2,8,6,128,128]{4,3,2,1,0:T(8,128)S(1)} copy-done((s32[2,8,6,128,128]{4,3,2,1,0:T(8,128)S(1)}, s32[2,8,6,128,128]{4,3,2,1,0:T(8,128)}, u32[]{:S(2)}) %copy-start.4) | copy-done | bytes 6291480
  22.1 3.6 %tally.1 = (bf16[8,128,768]{2,1,0:T(8,128)(2,1)}, f32[8,128,128]{2,1,0:T(8,128)S(1)}) custom-call(s32[3]{0:T(128)S(1)} %pad_add_fusion.1.place, s32[2,8,6,128,128]{4,3,2,1,0:T(8,128)S(1)} %copy-done.4), custom_call_target="tpu_custom_call" | custom-call | tf_op jit(solution)/shard_map/tally/pallas_call | solution.py:166
  27.5 2.6 %collective-permute-done = s32[80]{0:T(128)S(1)} collective-permute-done((s32[80]{0:T(128)S(1)}, s32[80]{0:T(128)S(1)}, u32[]{:S(2)}, u32[]{:S(2)}) %collective-permute-start) | collective-permute-done | bytes 352 | tf_op jit(solution)/shard_map/ppermute | solution.py:359
  31.1 1.7 copy-done.3
  32.7 1.1 copy-done.6
  33.8 1.0 copy-done.8
  34.8 2.4 %ready.1 = (bf16[1024,512]{1,0:T(8,128)(2,1)S(1)}, bf16[8,128,768]{2,1,0:T(8,128)(2,1)S(1)}, f32[8,128,128]{2,1,0:T(8,128)S(1)}) custom-call(s32[3]{0:T(128)S(1)} %pad_add_fusion.1.place, bf16[2,1024,512]{2,1,0:T(8,128)(2,1)S(1)} %copy-done.3, bf16[8,128,768]{2,1,0:T(8,128)(2,1)} %get-tuple-element.25.refs_1_, f32[8,128,128]{2,1,0:T(8,128)S(1)} %copy-done.6, ...), custom_call_target="tpu_custom_call" | custom-call | tf_op jit(solution)/shard_map/ready/pallas_call | solution.py:143
  37.2 10.2 %all-to-all-done.received = bf16[32,128,256]{2,1,0:T(8,128)(2,1)} async-done(((bf16[32,128,256]{2,1,0:T(8,128)(2,1)}), bf16[32,128,256]{2,1,0:T(8,128)(2,1)}, u32[]{:S(2)}, u32[]{:S(2)}) %all-to-all-start) | async-done | bytes 2097184 | tf_op jit(solution)/shard_map/all_to_all | solution.py:376
  47.4 2.5 %aggregate.4.mean_mine = bf16[1024,256]{1,0:T(8,128)(2,1)S(1)} custom-call(s32[1]{0:T(128)} %bitcast.core_ref, s32[48]{0:T(128)S(1)} %slice.7.tile_src, bf16[1024,512]{1,0:T(8,128)(2,1)S(1)} %get-tuple-element.27.h, bf16[32,128,256]{2,1,0:T(8,128)(2,1)} %all-to-all-done.received, bf16[8,128,768]{2,1,0:T(8,128)(2,1)S(1)} %get-tuple-element.30.counts, ...), custom_call_target="tpu_custom_call" | custom-call | tf_op jit(solution)/shard_map/aggregate/pallas_call | solution.py:210
  51.9 1.6 dense.3
  53.6 33.0 %all_to_all.25.received = bf16[32,128,256]{2,1,0:T(8,128)(2,1)S(1)} all-to-all(bf16[32,128,256]{2,1,0:T(8,128)(2,1)S(1)} %get-tuple-element.34), channel_id=1, replica_groups=mesh['sm'=2,'se'=2,'dz'=4,'dx'=4,'dc'=2] {'dx','se','dz'}, dimensions={0} | all-to-all | bytes 4194304 | tf_op jit(solution)/shard_map/all_to_all | solution.py:392
  86.5 1.2 aggregate.5.mean_mine
  89.7 1.6 dense.4
  91.3 32.7 %all_to_all.26.received = bf16[32,128,256]{2,1,0:T(8,128)(2,1)S(1)} all-to-all(bf16[32,128,256]{2,1,0:T(8,128)(2,1)S(1)} %get-tuple-element.36), channel_id=1, replica_groups=mesh['sm'=2,'se'=2,'dz'=4,'dx'=4,'dc'=2] {'dx','se','dz'}, dimensions={0} | all-to-all | bytes 4194304 | tf_op jit(solution)/shard_map/all_to_all | solution.py:392
  124.0 1.2 aggregate.6.mean_mine
  127.2 1.6 dense.5
  128.8 32.7 %all_to_all.27.received = bf16[32,128,256]{2,1,0:T(8,128)(2,1)S(1)} all-to-all(bf16[32,128,256]{2,1,0:T(8,128)(2,1)S(1)} %get-tuple-element.38), channel_id=1, replica_groups=mesh['sm'=2,'se'=2,'dz'=4,'dx'=4,'dc'=2] {'dx','se','dz'}, dimensions={0} | all-to-all | bytes 4194304 | tf_op jit(solution)/shard_map/all_to_all | solution.py:392
  161.5 1.2 aggregate.7
  165.0 29.0 %all_to_all.28.straight.source = bf16[4,512,512]{2,1,0:T(8,128)(2,1)S(1)} all-to-all(bf16[4,512,512]{2,1,0:T(8,128)(2,1)S(1)} %last_dense.1), channel_id=1, replica_groups=mesh['sm'=2,'se'=2,'dz'=4,'dx'=4,'dc'=2] {'sm','se'}, dimensions={0} | all-to-all | bytes 4194304 | tf_op jit(solution)/shard_map/all_to_all | solution.py:404
  194.2 1.0 finish.2.rest_0_
  195.2 1.7 collective-permute-done.8.source
  196.8 1.0 finish.3
  (49 shorter events, 11.4 us)
Async XLA Ops:
  6.5 20.5 %copy-start = (s32[2,8,6]{1,0,2:T(2,128)S(1)}, s32[2,8,6]{1,0,2:T(2,128)}, u32[]{:S(2)}) copy-start(s32[2,8,6]{1,0,2:T(2,128)} %param.14) | copy-start | bytes 1156
  6.5 4.1 %copy-start.2 = (bf16[2,1024,512]{2,1,0:T(8,128)(2,1)S(1)}, bf16[2,1024,512]{2,1,0:T(8,128)(2,1)}, u32[]{:S(2)}) copy-start(bf16[2,1024,512]{2,1,0:T(8,128)(2,1)} %refs_0_.1) | copy-start | bytes 6291460
  6.5 40.9 %all-gather.3.cloned.1.call-start = ((), (), s32[]{:S(2)}) async-start(), calls=%async_computation.5 | async-start | bytes 4866048 | tf_op jit(solution)/shard_map/all_gather | solution.py:375
  10.6 20.4 %collective-permute-start.1 = (bf16[2,1024,512]{2,1,0:T(8,128)(2,1)S(1)}, bf16[2,1024,512]{2,1,0:T(8,128)(2,1)}, u32[]{:S(2)}, u32[]{:S(2)}) collective-permute-start(bf16[2,1024,512]{2,1,0:T(8,128)(2,1)S(1)} %copy-done.2), channel_id=1, source_target_pairs={{0,1},{1,0},{2,3},{3,2},{4,5},{5,4},{6,7},{7,6},{8,9},{9,8},{10,11... | collective-permute-start | bytes 6291464 | tf_op jit(solution)/shard_map/ppermute | solution.py:359
  10.7 36.7 %all-to-all-start = ((bf16[32,128,256]{2,1,0:T(8,128)(2,1)}), bf16[32,128,256]{2,1,0:T(8,128)(2,1)}, u32[]{:S(2)}, u32[]{:S(2)}) async-start(bf16[32,128,256]{2,1,0:T(8,128)(2,1)} %get-tuple-element.23), calls=%async_computation | async-start | bytes 4194304 | tf_op jit(solution)/shard_map/all_to_all | solution.py:376
  19.2 2.9 %copy-start.4 = (s32[2,8,6,128,128]{4,3,2,1,0:T(8,128)S(1)}, s32[2,8,6,128,128]{4,3,2,1,0:T(8,128)}, u32[]{:S(2)}) copy-start(s32[2,8,6,128,128]{4,3,2,1,0:T(8,128)} %counts) | copy-start | bytes 18874372
  22.1 5.1 %copy-start.9 = (s32[2,32,1]{1,2,0:T(1,128)S(1)}, s32[2,32,1]{1,2,0:T(1,128)}, u32[]{:S(2)}) copy-start(s32[2,32,1]{1,2,0:T(1,128)} %param.13) | copy-start | bytes 772
  25.7 5.4 %collective-permute-start.2 = (bf16[8,128,768]{2,1,0:T(8,128)(2,1)}, bf16[8,128,768]{2,1,0:T(8,128)(2,1)}, u32[]{:S(2)}, u32[]{:S(2)}) collective-permute-start(bf16[8,128,768]{2,1,0:T(8,128)(2,1)} %get-tuple-element.25.refs_1_), channel_id=1, source_target_pairs={{0,1},{1,0},{2,3},{3,2},{4,5},{5,4},{6,7},{7,6},{8,9},{9,8},{10,11... | collective-permute-start | bytes 4718600 | tf_op jit(solution)/shard_map/ppermute | solution.py:359
  25.9 4.3 %collective-permute-start.3 = (f32[8,128,128]{2,1,0:T(8,128)S(1)}, f32[8,128,128]{2,1,0:T(8,128)S(1)}, u32[]{:S(2)}, u32[]{:S(2)}) collective-permute-start(f32[8,128,128]{2,1,0:T(8,128)S(1)} %get-tuple-element.26.refs_2_), channel_id=1, source_target_pairs={{0,1},{1,0},{2,3},{3,2},{4,5},{5,4},{6,7},{7,6},{8,9},{9,8},{10,11... | collective-permute-start | bytes 1572872 | tf_op jit(solution)/shard_map/ppermute | solution.py:359
  26.2 0.8 copy-start.5
  27.3 2.8 %collective-permute-start = (s32[80]{0:T(128)S(1)}, s32[80]{0:T(128)S(1)}, u32[]{:S(2)}, u32[]{:S(2)}) collective-permute-start(s32[80]{0:T(128)S(1)} %pad_add_fusion), channel_id=1, source_target_pairs={{0,1},{1,0},{2,3},{3,2},{4,5},{5,4},{6,7},{7,6},{8,9},{9,8},{10,11... | collective-permute-start | bytes 968 | tf_op jit(solution)/shard_map/ppermute | solution.py:359
  30.2 0.8 copy-start.7
  31.1 1.7 copy-start.3
  32.7 1.1 copy-start.6
  33.8 1.0 copy-start.8
  47.4 2.9 %copy-start.1 = (bf16[4224,512]{1,0:T(8,128)(2,1)S(1)}, bf16[4224,512]{1,0:T(8,128)(2,1)}, u32[]{:S(2)}) copy-start(bf16[4224,512]{1,0:T(8,128)(2,1)} %all-gather.3.cloned.1.call-done) | copy-start | bytes 12976132
  49.9 2.0 collective-permute-start.4
  87.7 2.0 collective-permute-start.5
  125.2 2.0 collective-permute-start.6
  162.7 1.6 collective-permute-start.7
  194.1 2.7 %collective-permute-start.8 = (bf16[2,512,512]{2,1,0:T(8,128)(2,1)S(1)}, bf16[2,512,512]{2,1,0:T(8,128)(2,1)S(1)}, u32[]{:S(2)}, u32[]{:S(2)}) collective-permute-start(bf16[2,512,512]{2,1,0:T(8,128)(2,1)S(1)} %theirs.1), channel_id=1, source_target_pairs={{0,1},{1,0},{2,3},{3,2},{4,5},{5,4},{6,7},{7,6},{8,9},{9,8},{10,11... | collective-permute-start | bytes 3145736 | tf_op jit(solution)/shard_map/ppermute | solution.py:359
Sparse Core Ops, SparseCore 0:
  10.7 32.8 all-gather.2

commit v6 on v5

--- a/solution.py
+++ b/solution.py
@@ -183,10 +183,10 @@
     )(place, counts)
 
 
-def aggregate_kernel(last, core_ref, tile_src, h, received, counts, inverse, *outs):
+def aggregate_kernel(last, tile_src, h, received, counts, inverse, *outs):
     n_blocks = counts.shape[0]
     tiles = counts.shape[2] // ROWS
-    core, width = core_ref[0], outs[0].shape[1]
+    core, width = lax.axis_index("dc"), outs[0].shape[1]
     cols = part(core, width)
     for i in range(n_blocks):
         b = lax.rem(n_blocks // 2 * (1 - core) + i, n_blocks) if last else i
@@ -204,21 +204,21 @@
         outs[i // per_out][begin : begin + ROWS, :] = (summed * scale).astype(h.dtype)
 
 
-def aggregate(last, core, tile_src, h, received, counts, inverse):
+def aggregate(last, tile_src, h, received, counts, inverse):
     rows, width = h.shape
     n_outs = 2 if last else 1
     outs = call(
         functools.partial(aggregate_kernel, last),
         "aggregate",
-        (SMEM, SMEM, VMEM, VMEM, VMEM, VMEM),
+        (SMEM, VMEM, VMEM, VMEM, VMEM),
         [like(h, (rows // n_outs, width // 2))] * n_outs,
         (VMEM,) * n_outs,
-    )(core, tile_src, h, received, counts, inverse)
+    )(tile_src, h, received, counts, inverse)
     return outs[0], outs[-1]
 
 
-def own_products_kernel(layer, core_ref, h, mean_mine, gathered, pre):
-    core, width = core_ref[0], h.shape[1]
+def own_products_kernel(layer, h, mean_mine, gathered, pre):
+    core, width = lax.axis_index("dc"), h.shape[1]
     parts = gathered[2 * layer, width : width + SPLIT_ROWS, :].astype(jnp.float32)
     bias = ((parts[4:6] + parts[2:4]) + parts[0:2])[0:1]
     right = jnp.concatenate(
@@ -232,14 +232,14 @@
         pre[rows, :] = jnp.dot(left, right, preferred_element_type=jnp.float32) + bias
 
 
-def own_products(layer, core, h, mean_mine, gathered):
+def own_products(layer, h, mean_mine, gathered):
     (out,) = call(
         functools.partial(own_products_kernel, layer),
         "own_products",
-        (SMEM, VMEM, VMEM, VMEM),
+        (VMEM, VMEM, VMEM),
         [jax.ShapeDtypeStruct((mean_mine.shape[0], h.shape[1]), jnp.float32)],
         (VMEM,),
-    )(core, h, mean_mine, gathered)
+    )(h, mean_mine, gathered)
     return out
 
 
@@ -250,8 +250,8 @@
     right = gathered[2 * layer + 1, part(1 - core, width // 2), :]
     rows = pl.ds(c * CHUNK, CHUNK)
     summed[...] = pre[rows, :] + jnp.dot(mean_other[rows, :], right, preferred_element_type=jnp.float32)
-    for begin in range(0, CHUNK, 64):
-        x = summed[begin : begin + 64, :]
+    for begin in range(0, CHUNK, 128):
+        x = summed[begin : begin + 128, :]
         mu = jnp.mean(x, axis=1, keepdims=True)
         centred = x - mu
         var = jnp.mean(centred * centred, axis=1, keepdims=True)
@@ -259,99 +259,103 @@
         yield c * CHUNK + begin, value.astype(mean_other.dtype)
 
 
-def dense_kernel(layer, core_ref, blocks, pre, mean_other, gathered, h_out, outgoing, summed):
-    core = core_ref[0]
+def dense_kernel(layer, blocks, pre, mean_other, gathered, h_out, outgoing, summed):
+    core = lax.axis_index("dc")
     for c in range(pre.shape[0] // CHUNK):
         for begin, value in layer_rows(layer, core, c, pre, mean_other, gathered, summed.at[c]):
-            h_out[begin : begin + 64, :] = value
+            h_out[begin : begin + 128, :] = value
     for j in range(outgoing.shape[0]):
         outgoing[j] = h_out[block_rows(blocks[reader_of(j)]), part(core, outgoing.shape[2])]
 
 
-def dense(layer, core, blocks, pre, mean_other, gathered):
+def dense(layer, blocks, pre, mean_other, gathered):
     rows, width = pre.shape
     return call(
         functools.partial(dense_kernel, layer),
         "dense",
-        (SMEM, SMEM) + (VMEM,) * 3,
+        (SMEM,) + (VMEM,) * 3,
         [like(mean_other, pre.shape), like(mean_other, (blocks.shape[0], ROWS, width // 2))],
         (VMEM, VMEM),
         [pltpu.VMEM((rows // CHUNK, CHUNK, width), jnp.float32)],
-    )(core, blocks, pre, mean_other, gathered)
-
-
-def last_dense_kernel(core_ref, pre, mean_other, gathered, *rest):
+    )(blocks, pre, mean_other, gathered)
+
+
+def last_dense_kernel(pre, mean_other, gathered, *rest):
     *kept, leaving, summed, sems = rest
-    core, last = core_ref[0], N_LAYERS - 1
+    core, last = lax.axis_index("dc"), N_LAYERS - 1
     half_rows = leaving.shape[1]
     copies = [
-        pltpu.make_async_copy(source.at[part(core, half_rows)], leaving.at[layer], sems.at[layer])
+        pltpu.make_async_copy(source.at[part(core, half_rows)], leaving.at[ring_place(layer)], sems.at[layer])
         for layer, source in enumerate(kept)
     ]
     for copy in copies:
         copy.start()
     for c in range(half_rows // CHUNK):
         for begin, value in layer_rows(last, core, c, pre, mean_other, gathered, summed.at[c]):
-            leaving[last, begin : begin + 64, :] = value
+            leaving[ring_place(last), begin : begin + 128, :] = value
     for copy in copies:
         copy.wait()
 
 
-def last_dense(core, pre, mean_other, gathered, kept):
+def last_dense(pre, mean_other, gathered, kept):
     half_rows, width = pre.shape
     (out,) = call(
         last_dense_kernel,
         "last_dense",
-        (SMEM,) + (VMEM,) * 3 + (HBM,) * len(kept),
+        (VMEM,) * 3 + (HBM,) * len(kept),
         [like(mean_other, (N_LAYERS, half_rows, width))],
         (VMEM,),
         [
             pltpu.VMEM((half_rows // CHUNK, CHUNK, width), jnp.float32),
             pltpu.SemaphoreType.DMA((N_LAYERS - 1,)),
         ],
-    )(core, pre, mean_other, gathered, *kept)
+    )(pre, mean_other, gathered, *kept)
     return out
 
 
-def finish_kernel(crossing, core_ref, source, *rest):
+def finish_kernel(crossing, source, *rest):
     out, sems = rest[-2:]
-    core, chunk = core_ref[0], source.shape[1]
+    core, chunk = lax.axis_index("dc"), source.shape[1]
     half = 1 - core if crossing else core
     pieces = []
     for g in range(2):
-        piece = source.at[g] if crossing else source.at[2 * g + core]
+        piece = source.at[g] if crossing else source.at[2 * core + g]
         pieces.append((piece, out.at[g, part(half, chunk)]))
     run_copies(pieces, sems)
 
 
-def finish(crossing, core, source, *results):
+def finish(crossing, source, *results):
     _, chunk, width = source.shape
     (out,) = call(
         functools.partial(finish_kernel, crossing),
         "finish",
-        (SMEM, VMEM) + (HBM,) * len(results),
+        (VMEM,) + (HBM,) * len(results),
         [like(source, (2, 2 * chunk, width))],
         (HBM,),
         [pltpu.SemaphoreType.DMA((2,))],
-        input_output_aliases={2: 0} if crossing else {},
-    )(core, source, *results)
+        input_output_aliases={1: 0} if crossing else {},
+    )(source, *results)
     return out
 
 
-def theirs_kernel(core_ref, straight, out, sems):
-    core = core_ref[0]
-    run_copies([(straight.at[2 * g + 1 - core], out.at[g]) for g in range(2)], sems)
-
-
-def theirs(core, straight):
+def ring_place(section):
+    return section % 2 * 2 + section // 2
+
+
+def theirs_kernel(straight, out, sems):
+    core = lax.axis_index("dc")
+    run_copies([(straight.at[pl.ds(2 * (1 - core), 2)], out)], sems)
+
+
+def theirs(straight):
     (out,) = call(
         theirs_kernel,
         "theirs",
-        (SMEM, VMEM),
+        (VMEM,),
         [like(straight, (2,) + straight.shape[1:])],
         (VMEM,),
         [pltpu.SemaphoreType.DMA((2,))],
-    )(core, straight)
+    )(straight)
     return out
 
 
@@ -386,24 +390,24 @@
     h, tile_counts, inverse = ready(
         place, features, tile_counts, inverse, swap(features), swap(tile_counts), swap(inverse)
     )
-    core_ref, kept = scalars(core), []
+    kept = []
     for layer in range(N_LAYERS):
         if layer > 0:
             received = lax.all_to_all(outgoing, CHIPS, 0, 0, tiled=True)
         else:
             received, gathered = lax.optimization_barrier((received, gathered))
         last = layer == N_LAYERS - 1
-        theirs_too, mean_mine = aggregate(last, core_ref, tiles, h, received, tile_counts, inverse)
+        theirs_too, mean_mine = aggregate(last, tiles, h, received, tile_counts, inverse)
         mean_other = swap(theirs_too)
-        pre = own_products(layer, core_ref, h, mean_mine, gathered)
+        pre = own_products(layer, h, mean_mine, gathered)
         if last:
-            leaving = last_dense(core_ref, pre, mean_other, gathered, kept)
+            leaving = last_dense(pre, mean_other, gathered, kept)
         else:
-            h, outgoing = dense(layer, core_ref, blocks, pre, mean_other, gathered)
+            h, outgoing = dense(layer, blocks, pre, mean_other, gathered)
             kept.append(h)
-    straight = lax.all_to_all(leaving, SECTION, 0, 0, tiled=True)
-    crossed = swap(theirs(core_ref, straight))
-    results = finish(True, core_ref, crossed, finish(False, core_ref, straight))
+    straight = lax.all_to_all(leaving, ("se", "sm"), 0, 0, tiled=True)
+    crossed = swap(theirs(straight))
+    results = finish(True, crossed, finish(False, straight))
     return results[None]
 
 

time: 208 us -> 208 us (level)
  no operation moved by 1% of the time
where the time goes in v6:
time: 208 us; the launch traced here: 204 us
  blocking collectives  127 us (61%)
  Pallas kernels  27.2 us (13%)
  waiting for transfers between devices  17.9 us (9%)
  between operations  13.6 us (7%)
  starting transfers between devices  9.64 us (5%)
  local copies, waits for them, and re-layouts  8.8 us (4%)
    all_to_all x3, blocking collectives, body(): received = lax.all_to_all(outgoing, CHIPS, 0, 0, tiled=True)  98.4 us
    all_to_all x1, blocking collectives, body(): straight = lax.all_to_all(leaving, ('se', 'sm'), 0, 0, tiled=True)  28.6 us
    all_to_all x1, waiting for transfers between devices, body(): received = lax.all_to_all(outgoing, CORES, 0, 0, tiled=True)  10.2 us
    unnamed x20, local copies, waits for them, and re-layouts  8.56 us
    all_to_all x1, starting transfers between devices, body(): received = lax.all_to_all(outgoing, CORES, 0, 0, tiled=True)  8.39 us
    ppermute x9, waiting for transfers between devices, swap(): return lax.ppermute(value, 'dc', [(0, 1), (1, 0)])  7.63 us
    pallas_call x4, Pallas kernels, aggregate(): call(functools.partial(aggregate_kernel, last), 'aggregate', (SMEM, VMEM,...  6.04 us
    pallas_call x3, Pallas kernels, dense(): call(functools.partial(dense_kernel, layer), 'dense', (SMEM,) + (VMEM,) *...  4.86 us
  transfers between devices with their start and end apart: 11, of which 7 were waited for; matrix products, arithmetic and copies ran while one was open for 0% of the time, Pallas kernels for 5%

profile of v6, /device:TPU:24, one launch (start us, length us, event | category | flops | bytes accessed | tf_op | source)
XLA Modules:
  0.0 204.3 jit_solution(4734116442194604185)
XLA Ops:
  6.5 4.0 %front.1 = (bf16[32,128,256]{2,1,0:T(8,128)(2,1)}, bf16[528,512]{1,0:T(8,128)(2,1)}) custom-call(s32[2,32]{1,0:T(2,128)} %bitcast.20, bf16[2,1024,512]{2,1,0:T(8,128)(2,1)} %refs_0_.1, bf16[1,512,512]{2,1,0:T(8,128)(2,1)} %w_self.1, bf16[1,512,512]{2,1,0:T(8,128)(2,1)} %w_neigh.1, f32[1,512]{1,0:T(1,128)} %bias.1, f32[1,512]{1,0:T(1,128)} %gain.1), custom_call_target="tpu_custom_call" | custom-call | tf_op jit(solution)/shard_map/front/pallas_call | solution.py:111
  10.7 8.4 %all-to-all-start = ((bf16[32,128,256]{2,1,0:T(8,128)(2,1)}), bf16[32,128,256]{2,1,0:T(8,128)(2,1)}, u32[]{:S(2)}, u32[]{:S(2)}) async-start(bf16[32,128,256]{2,1,0:T(8,128)(2,1)} %get-tuple-element.23), calls=%async_computation | async-start | bytes 4194304 | tf_op jit(solution)/shard_map/all_to_all | solution.py:380
  19.2 2.9 %copy-done.4 = s32[2,8,6,128,128]{4,3,2,1,0:T(8,128)S(1)} copy-done((s32[2,8,6,128,128]{4,3,2,1,0:T(8,128)S(1)}, s32[2,8,6,128,128]{4,3,2,1,0:T(8,128)}, u32[]{:S(2)}) %copy-start.4) | copy-done | bytes 6291480
  22.1 3.6 %tally.1 = (bf16[8,128,768]{2,1,0:T(8,128)(2,1)}, f32[8,128,128]{2,1,0:T(8,128)S(1)}) custom-call(s32[3]{0:T(128)S(1)} %pad_add_fusion.1.place, s32[2,8,6,128,128]{4,3,2,1,0:T(8,128)S(1)} %copy-done.4), custom_call_target="tpu_custom_call" | custom-call | tf_op jit(solution)/shard_map/tally/pallas_call | solution.py:166
  27.5 2.6 %collective-permute-done = s32[80]{0:T(128)S(1)} collective-permute-done((s32[80]{0:T(128)S(1)}, s32[80]{0:T(128)S(1)}, u32[]{:S(2)}, u32[]{:S(2)}) %collective-permute-start) | collective-permute-done | bytes 352 | tf_op jit(solution)/shard_map/ppermute | solution.py:363
  31.1 1.7 copy-done.3
  32.7 1.1 copy-done.6
  33.8 1.0 copy-done.8
  34.8 2.4 %ready.1 = (bf16[1024,512]{1,0:T(8,128)(2,1)S(1)}, bf16[8,128,768]{2,1,0:T(8,128)(2,1)S(1)}, f32[8,128,128]{2,1,0:T(8,128)S(1)}) custom-call(s32[3]{0:T(128)S(1)} %pad_add_fusion.1.place, bf16[2,1024,512]{2,1,0:T(8,128)(2,1)S(1)} %copy-done.3, bf16[8,128,768]{2,1,0:T(8,128)(2,1)} %get-tuple-element.25.refs_1_, f32[8,128,128]{2,1,0:T(8,128)S(1)} %copy-done.6, ...), custom_call_target="tpu_custom_call" | custom-call | tf_op jit(solution)/shard_map/ready/pallas_call | solution.py:143
  37.2 10.2 %all-to-all-done.received = bf16[32,128,256]{2,1,0:T(8,128)(2,1)} async-done(((bf16[32,128,256]{2,1,0:T(8,128)(2,1)}), bf16[32,128,256]{2,1,0:T(8,128)(2,1)}, u32[]{:S(2)}, u32[]{:S(2)}) %all-to-all-start) | async-done | bytes 2097184 | tf_op jit(solution)/shard_map/all_to_all | solution.py:380
  47.4 2.5 %aggregate.4.mean_mine = bf16[1024,256]{1,0:T(8,128)(2,1)S(1)} custom-call(s32[48]{0:T(128)S(1)} %slice.7.tile_src, bf16[1024,512]{1,0:T(8,128)(2,1)S(1)} %get-tuple-element.27.h, bf16[32,128,256]{2,1,0:T(8,128)(2,1)} %all-to-all-done.received, bf16[8,128,768]{2,1,0:T(8,128)(2,1)S(1)} %get-tuple-element.30.counts, f32[8,128,128]{2,1,0:T(8,128)S(1)} %get-tuple-element.31.inverse), custom_call_target="tpu_custom_call" | custom-call | tf_op jit(solution)/shard_map/aggregate/pallas_call | solution.py:210
  51.9 1.6 dense.3
  53.6 33.0 %all_to_all.25.received = bf16[32,128,256]{2,1,0:T(8,128)(2,1)S(1)} all-to-all(bf16[32,128,256]{2,1,0:T(8,128)(2,1)S(1)} %get-tuple-element.34), channel_id=1, replica_groups=mesh['sm'=2,'se'=2,'dz'=4,'dx'=4,'dc'=2] {'dx','se','dz'}, dimensions={0} | all-to-all | bytes 4194304 | tf_op jit(solution)/shard_map/all_to_all | solution.py:396
  86.5 1.2 aggregate.5.mean_mine
  89.7 1.6 dense.4
  91.3 32.7 %all_to_all.26.received = bf16[32,128,256]{2,1,0:T(8,128)(2,1)S(1)} all-to-all(bf16[32,128,256]{2,1,0:T(8,128)(2,1)S(1)} %get-tuple-element.36), channel_id=1, replica_groups=mesh['sm'=2,'se'=2,'dz'=4,'dx'=4,'dc'=2] {'dx','se','dz'}, dimensions={0} | all-to-all | bytes 4194304 | tf_op jit(solution)/shard_map/all_to_all | solution.py:396
  124.0 1.2 aggregate.6.mean_mine
  127.2 1.6 dense.5
  128.8 32.7 %all_to_all.27.received = bf16[32,128,256]{2,1,0:T(8,128)(2,1)S(1)} all-to-all(bf16[32,128,256]{2,1,0:T(8,128)(2,1)S(1)} %get-tuple-element.38), channel_id=1, replica_groups=mesh['sm'=2,'se'=2,'dz'=4,'dx'=4,'dc'=2] {'dx','se','dz'}, dimensions={0} | all-to-all | bytes 4194304 | tf_op jit(solution)/shard_map/all_to_all | solution.py:396
  161.5 1.2 aggregate.7
  165.0 28.6 %all_to_all.28.straight.source = bf16[4,512,512]{2,1,0:T(8,128)(2,1)S(1)} all-to-all(bf16[4,512,512]{2,1,0:T(8,128)(2,1)S(1)} %last_dense.1), channel_id=1, replica_groups=mesh['sm'=2,'se'=2,'dz'=4,'dx'=4,'dc'=2] {'se','sm'}, dimensions={0} | all-to-all | bytes 4194304 | tf_op jit(solution)/shard_map/all_to_all | solution.py:408
  193.8 1.0 finish.2.rest_0_
  194.8 1.6 collective-permute-done.8.source
  196.5 1.0 finish.3
  (49 shorter events, 11.4 us)
Async XLA Ops:
  6.5 20.5 %copy-start = (s32[2,8,6]{1,0,2:T(2,128)S(1)}, s32[2,8,6]{1,0,2:T(2,128)}, u32[]{:S(2)}) copy-start(s32[2,8,6]{1,0,2:T(2,128)} %param.14) | copy-start | bytes 1156
  6.5 4.1 %copy-start.2 = (bf16[2,1024,512]{2,1,0:T(8,128)(2,1)S(1)}, bf16[2,1024,512]{2,1,0:T(8,128)(2,1)}, u32[]{:S(2)}) copy-start(bf16[2,1024,512]{2,1,0:T(8,128)(2,1)} %refs_0_.1) | copy-start | bytes 6291460
  6.5 40.9 %all-gather.3.cloned.1.call-start = ((), (), s32[]{:S(2)}) async-start(), calls=%async_computation.5 | async-start | bytes 4866048 | tf_op jit(solution)/shard_map/all_gather | solution.py:379
  10.6 20.4 %collective-permute-start.1 = (bf16[2,1024,512]{2,1,0:T(8,128)(2,1)S(1)}, bf16[2,1024,512]{2,1,0:T(8,128)(2,1)}, u32[]{:S(2)}, u32[]{:S(2)}) collective-permute-start(bf16[2,1024,512]{2,1,0:T(8,128)(2,1)S(1)} %copy-done.2), channel_id=1, source_target_pairs={{0,1},{1,0},{2,3},{3,2},{4,5},{5,4},{6,7},{7,6},{8,9},{9,8},{10,11... | collective-permute-start | bytes 6291464 | tf_op jit(solution)/shard_map/ppermute | solution.py:363
  10.7 36.7 %all-to-all-start = ((bf16[32,128,256]{2,1,0:T(8,128)(2,1)}), bf16[32,128,256]{2,1,0:T(8,128)(2,1)}, u32[]{:S(2)}, u32[]{:S(2)}) async-start(bf16[32,128,256]{2,1,0:T(8,128)(2,1)} %get-tuple-element.23), calls=%async_computation | async-start | bytes 4194304 | tf_op jit(solution)/shard_map/all_to_all | solution.py:380
  19.2 2.9 %copy-start.4 = (s32[2,8,6,128,128]{4,3,2,1,0:T(8,128)S(1)}, s32[2,8,6,128,128]{4,3,2,1,0:T(8,128)}, u32[]{:S(2)}) copy-start(s32[2,8,6,128,128]{4,3,2,1,0:T(8,128)} %counts) | copy-start | bytes 18874372
  22.1 5.1 %copy-start.9 = (s32[2,32,1]{1,2,0:T(1,128)S(1)}, s32[2,32,1]{1,2,0:T(1,128)}, u32[]{:S(2)}) copy-start(s32[2,32,1]{1,2,0:T(1,128)} %param.13) | copy-start | bytes 772
  25.7 5.4 %collective-permute-start.2 = (bf16[8,128,768]{2,1,0:T(8,128)(2,1)}, bf16[8,128,768]{2,1,0:T(8,128)(2,1)}, u32[]{:S(2)}, u32[]{:S(2)}) collective-permute-start(bf16[8,128,768]{2,1,0:T(8,128)(2,1)} %get-tuple-element.25.refs_1_), channel_id=1, source_target_pairs={{0,1},{1,0},{2,3},{3,2},{4,5},{5,4},{6,7},{7,6},{8,9},{9,8},{10,11... | collective-permute-start | bytes 4718600 | tf_op jit(solution)/shard_map/ppermute | solution.py:363
  25.9 4.3 %collective-permute-start.3 = (f32[8,128,128]{2,1,0:T(8,128)S(1)}, f32[8,128,128]{2,1,0:T(8,128)S(1)}, u32[]{:S(2)}, u32[]{:S(2)}) collective-permute-start(f32[8,128,128]{2,1,0:T(8,128)S(1)} %get-tuple-element.26.refs_2_), channel_id=1, source_target_pairs={{0,1},{1,0},{2,3},{3,2},{4,5},{5,4},{6,7},{7,6},{8,9},{9,8},{10,11... | collective-permute-start | bytes 1572872 | tf_op jit(solution)/shard_map/ppermute | solution.py:363
  26.2 0.8 copy-start.5
  27.3 2.8 %collective-permute-start = (s32[80]{0:T(128)S(1)}, s32[80]{0:T(128)S(1)}, u32[]{:S(2)}, u32[]{:S(2)}) collective-permute-start(s32[80]{0:T(128)S(1)} %pad_add_fusion), channel_id=1, source_target_pairs={{0,1},{1,0},{2,3},{3,2},{4,5},{5,4},{6,7},{7,6},{8,9},{9,8},{10,11... | collective-permute-start | bytes 968 | tf_op jit(solution)/shard_map/ppermute | solution.py:363
  30.2 0.8 copy-start.7
  31.1 1.7 copy-start.3
  32.7 1.1 copy-start.6
  33.8 1.0 copy-start.8
  47.4 2.9 %copy-start.1 = (bf16[4224,512]{1,0:T(8,128)(2,1)S(1)}, bf16[4224,512]{1,0:T(8,128)(2,1)}, u32[]{:S(2)}) copy-start(bf16[4224,512]{1,0:T(8,128)(2,1)} %all-gather.3.cloned.1.call-done) | copy-start | bytes 12976132
  50.0 2.0 collective-permute-start.4
  87.7 2.0 collective-permute-start.5
  125.2 2.0 collective-permute-start.6
  162.7 1.6 collective-permute-start.7
  193.7 2.7 %collective-permute-start.8 = (bf16[2,512,512]{2,1,0:T(8,128)(2,1)S(1)}, bf16[2,512,512]{2,1,0:T(8,128)(2,1)S(1)}, u32[]{:S(2)}, u32[]{:S(2)}) collective-permute-start(bf16[2,512,512]{2,1,0:T(8,128)(2,1)S(1)} %theirs.1), channel_id=1, source_target_pairs={{0,1},{1,0},{2,3},{3,2},{4,5},{5,4},{6,7},{7,6},{8,9},{9,8},{10,11... | collective-permute-start | bytes 3145736 | tf_op jit(solution)/shard_map/ppermute | solution.py:363
Sparse Core Ops, SparseCore 0:
  10.7 32.8 all-gather.2

commit v7 on v6

--- a/solution.py
+++ b/solution.py
@@ -70,12 +70,17 @@
 
 
 def front_kernel(
-    hubs, features, w_self, w_neigh, bias, gain, outgoing, packed_out, held, packed, load_sem, w_sem, out_sem, sems
+    hubs, features, w_self, w_neigh, bias, gain, outgoing, packed_out, held, packed, load_sems, w_sem, out_sem, sems
 ):
     graph, parity, core = lax.axis_index("sm"), lax.axis_index("se"), lax.axis_index("dc")
     width = packed.shape[1]
-    load = pltpu.make_async_copy(features.at[graph], held, load_sem)
-    load.start()
+    n_loads = load_sems.shape[0]
+    step = held.shape[0] // n_loads
+    loads = []
+    for i in range(n_loads):
+        rows = pl.ds(i * step, step)
+        loads.append(pltpu.make_async_copy(features.at[graph, rows], held.at[rows], load_sems.at[i]))
+        loads[-1].start()
     for index, source in enumerate((w_self, w_neigh)):
 
         @pl.when(core == index)
@@ -90,7 +95,8 @@
         values = values - part
     parts.append(jnp.zeros((SPLIT_ROWS - 6, width), jnp.float32))
     packed[width : width + SPLIT_ROWS, :] = jnp.concatenate(parts, axis=0).astype(packed.dtype)
-    load.wait()
+    for load in loads:
+        load.wait()
     half = outgoing.shape[2]
     copies = []
     for j in range(outgoing.shape[0]):
@@ -117,7 +123,7 @@
         [
             pltpu.VMEM((rows, width), features.dtype),
             pltpu.VMEM((width + SPLIT_ROWS, width), w_self.dtype),
-            pltpu.SemaphoreType.DMA,
+            pltpu.SemaphoreType.DMA((4,)),
             pltpu.SemaphoreType.DMA,
             pltpu.SemaphoreType.DMA,
             pltpu.SemaphoreType.DMA((n_hubs,)),

time: 208 us -> 208 us (level)
  no operation moved by 1% of the time
where the time goes in v7:
time: 208 us; the launch traced here: 204 us
  blocking collectives  127 us (61%)
  Pallas kernels  27.2 us (13%)
  waiting for transfers between devices  17.9 us (9%)
  between operations  13.6 us (7%)
  starting transfers between devices  9.64 us (5%)
  local copies, waits for them, and re-layouts  8.8 us (4%)
    all_to_all x3, blocking collectives, body(): received = lax.all_to_all(outgoing, CHIPS, 0, 0, tiled=True)  98.3 us
    all_to_all x1, blocking collectives, body(): straight = lax.all_to_all(leaving, ('se', 'sm'), 0, 0, tiled=True)  28.6 us
    all_to_all x1, waiting for transfers between devices, body(): received = lax.all_to_all(outgoing, CORES, 0, 0, tiled=True)  10.2 us
    unnamed x20, local copies, waits for them, and re-layouts  8.55 us
    all_to_all x1, starting transfers between devices, body(): received = lax.all_to_all(outgoing, CORES, 0, 0, tiled=True)  8.39 us
    ppermute x9, waiting for transfers between devices, swap(): return lax.ppermute(value, 'dc', [(0, 1), (1, 0)])  7.63 us
    pallas_call x4, Pallas kernels, aggregate(): call(functools.partial(aggregate_kernel, last), 'aggregate', (SMEM, VMEM,...  6.04 us
    pallas_call x3, Pallas kernels, dense(): call(functools.partial(dense_kernel, layer), 'dense', (SMEM,) + (VMEM,) *...  4.85 us
  transfers between devices with their start and end apart: 11, of which 7 were waited for; matrix products, arithmetic and copies ran while one was open for 0% of the time, Pallas kernels for 5%

profile of v7, /device:TPU:24, one launch (start us, length us, event | category | flops | bytes accessed | tf_op | source)
XLA Modules:
  0.0 204.3 jit_solution(29090283158431769)
XLA Ops:
  6.5 4.0 %front.1 = (bf16[32,128,256]{2,1,0:T(8,128)(2,1)}, bf16[528,512]{1,0:T(8,128)(2,1)}) custom-call(s32[2,32]{1,0:T(2,128)} %bitcast.20, bf16[2,1024,512]{2,1,0:T(8,128)(2,1)} %refs_0_.1, bf16[1,512,512]{2,1,0:T(8,128)(2,1)} %w_self.1, bf16[1,512,512]{2,1,0:T(8,128)(2,1)} %w_neigh.1, f32[1,512]{1,0:T(1,128)} %bias.1, f32[1,512]{1,0:T(1,128)} %gain.1), custom_call_target="tpu_custom_call" | custom-call | tf_op jit(solution)/shard_map/front/pallas_call | solution.py:117
  10.7 8.4 %all-to-all-start = ((bf16[32,128,256]{2,1,0:T(8,128)(2,1)}), bf16[32,128,256]{2,1,0:T(8,128)(2,1)}, u32[]{:S(2)}, u32[]{:S(2)}) async-start(bf16[32,128,256]{2,1,0:T(8,128)(2,1)} %get-tuple-element.23), calls=%async_computation | async-start | bytes 4194304 | tf_op jit(solution)/shard_map/all_to_all | solution.py:386
  19.2 2.9 %copy-done.4 = s32[2,8,6,128,128]{4,3,2,1,0:T(8,128)S(1)} copy-done((s32[2,8,6,128,128]{4,3,2,1,0:T(8,128)S(1)}, s32[2,8,6,128,128]{4,3,2,1,0:T(8,128)}, u32[]{:S(2)}) %copy-start.4) | copy-done | bytes 6291480
  22.1 3.6 %tally.1 = (bf16[8,128,768]{2,1,0:T(8,128)(2,1)}, f32[8,128,128]{2,1,0:T(8,128)S(1)}) custom-call(s32[3]{0:T(128)S(1)} %pad_add_fusion.1.place, s32[2,8,6,128,128]{4,3,2,1,0:T(8,128)S(1)} %copy-done.4), custom_call_target="tpu_custom_call" | custom-call | tf_op jit(solution)/shard_map/tally/pallas_call | solution.py:172
  27.5 2.6 %collective-permute-done = s32[80]{0:T(128)S(1)} collective-permute-done((s32[80]{0:T(128)S(1)}, s32[80]{0:T(128)S(1)}, u32[]{:S(2)}, u32[]{:S(2)}) %collective-permute-start) | collective-permute-done | bytes 352 | tf_op jit(solution)/shard_map/ppermute | solution.py:369
  31.0 1.7 copy-done.3
  32.7 1.1 copy-done.6
  33.8 1.0 copy-done.8
  34.8 2.4 %ready.1 = (bf16[1024,512]{1,0:T(8,128)(2,1)S(1)}, bf16[8,128,768]{2,1,0:T(8,128)(2,1)S(1)}, f32[8,128,128]{2,1,0:T(8,128)S(1)}) custom-call(s32[3]{0:T(128)S(1)} %pad_add_fusion.1.place, bf16[2,1024,512]{2,1,0:T(8,128)(2,1)S(1)} %copy-done.3, bf16[8,128,768]{2,1,0:T(8,128)(2,1)} %get-tuple-element.25.refs_1_, f32[8,128,128]{2,1,0:T(8,128)S(1)} %copy-done.6, ...), custom_call_target="tpu_custom_call" | custom-call | tf_op jit(solution)/shard_map/ready/pallas_call | solution.py:149
  37.2 10.2 %all-to-all-done.received = bf16[32,128,256]{2,1,0:T(8,128)(2,1)} async-done(((bf16[32,128,256]{2,1,0:T(8,128)(2,1)}), bf16[32,128,256]{2,1,0:T(8,128)(2,1)}, u32[]{:S(2)}, u32[]{:S(2)}) %all-to-all-start) | async-done | bytes 2097184 | tf_op jit(solution)/shard_map/all_to_all | solution.py:386
  47.4 2.5 %aggregate.4.mean_mine = bf16[1024,256]{1,0:T(8,128)(2,1)S(1)} custom-call(s32[48]{0:T(128)S(1)} %slice.7.tile_src, bf16[1024,512]{1,0:T(8,128)(2,1)S(1)} %get-tuple-element.27.h, bf16[32,128,256]{2,1,0:T(8,128)(2,1)} %all-to-all-done.received, bf16[8,128,768]{2,1,0:T(8,128)(2,1)S(1)} %get-tuple-element.30.counts, f32[8,128,128]{2,1,0:T(8,128)S(1)} %get-tuple-element.31.inverse), custom_call_target="tpu_custom_call" | custom-call | tf_op jit(solution)/shard_map/aggregate/pallas_call | solution.py:216
  51.9 1.6 dense.3
  53.5 33.0 %all_to_all.25.received = bf16[32,128,256]{2,1,0:T(8,128)(2,1)S(1)} all-to-all(bf16[32,128,256]{2,1,0:T(8,128)(2,1)S(1)} %get-tuple-element.34), channel_id=1, replica_groups=mesh['sm'=2,'se'=2,'dz'=4,'dx'=4,'dc'=2] {'dx','se','dz'}, dimensions={0} | all-to-all | bytes 4194304 | tf_op jit(solution)/shard_map/all_to_all | solution.py:402
  86.5 1.2 aggregate.5.mean_mine
  89.7 1.6 dense.4
  91.3 32.7 %all_to_all.26.received = bf16[32,128,256]{2,1,0:T(8,128)(2,1)S(1)} all-to-all(bf16[32,128,256]{2,1,0:T(8,128)(2,1)S(1)} %get-tuple-element.36), channel_id=1, replica_groups=mesh['sm'=2,'se'=2,'dz'=4,'dx'=4,'dc'=2] {'dx','se','dz'}, dimensions={0} | all-to-all | bytes 4194304 | tf_op jit(solution)/shard_map/all_to_all | solution.py:402
  124.0 1.2 aggregate.6.mean_mine
  127.2 1.6 dense.5
  128.8 32.7 %all_to_all.27.received = bf16[32,128,256]{2,1,0:T(8,128)(2,1)S(1)} all-to-all(bf16[32,128,256]{2,1,0:T(8,128)(2,1)S(1)} %get-tuple-element.38), channel_id=1, replica_groups=mesh['sm'=2,'se'=2,'dz'=4,'dx'=4,'dc'=2] {'dx','se','dz'}, dimensions={0} | all-to-all | bytes 4194304 | tf_op jit(solution)/shard_map/all_to_all | solution.py:402
  161.5 1.2 aggregate.7
  165.0 28.6 %all_to_all.28.straight.source = bf16[4,512,512]{2,1,0:T(8,128)(2,1)S(1)} all-to-all(bf16[4,512,512]{2,1,0:T(8,128)(2,1)S(1)} %last_dense.1), channel_id=1, replica_groups=mesh['sm'=2,'se'=2,'dz'=4,'dx'=4,'dc'=2] {'se','sm'}, dimensions={0} | all-to-all | bytes 4194304 | tf_op jit(solution)/shard_map/all_to_all | solution.py:414
  193.8 1.0 finish.2.rest_0_
  194.8 1.6 collective-permute-done.8.source
  196.5 1.0 finish.3
  (49 shorter events, 11.4 us)
Async XLA Ops:
  6.5 20.5 %copy-start = (s32[2,8,6]{1,0,2:T(2,128)S(1)}, s32[2,8,6]{1,0,2:T(2,128)}, u32[]{:S(2)}) copy-start(s32[2,8,6]{1,0,2:T(2,128)} %param.14) | copy-start | bytes 1156
  6.5 4.1 %copy-start.2 = (bf16[2,1024,512]{2,1,0:T(8,128)(2,1)S(1)}, bf16[2,1024,512]{2,1,0:T(8,128)(2,1)}, u32[]{:S(2)}) copy-start(bf16[2,1024,512]{2,1,0:T(8,128)(2,1)} %refs_0_.1) | copy-start | bytes 6291460
  6.5 40.9 %all-gather.3.cloned.1.call-start = ((), (), s32[]{:S(2)}) async-start(), calls=%async_computation.5 | async-start | bytes 4866048 | tf_op jit(solution)/shard_map/all_gather | solution.py:385
  10.6 20.4 %collective-permute-start.1 = (bf16[2,1024,512]{2,1,0:T(8,128)(2,1)S(1)}, bf16[2,1024,512]{2,1,0:T(8,128)(2,1)}, u32[]{:S(2)}, u32[]{:S(2)}) collective-permute-start(bf16[2,1024,512]{2,1,0:T(8,128)(2,1)S(1)} %copy-done.2), channel_id=1, source_target_pairs={{0,1},{1,0},{2,3},{3,2},{4,5},{5,4},{6,7},{7,6},{8,9},{9,8},{10,11... | collective-permute-start | bytes 6291464 | tf_op jit(solution)/shard_map/ppermute | solution.py:369
  10.7 36.7 %all-to-all-start = ((bf16[32,128,256]{2,1,0:T(8,128)(2,1)}), bf16[32,128,256]{2,1,0:T(8,128)(2,1)}, u32[]{:S(2)}, u32[]{:S(2)}) async-start(bf16[32,128,256]{2,1,0:T(8,128)(2,1)} %get-tuple-element.23), calls=%async_computation | async-start | bytes 4194304 | tf_op jit(solution)/shard_map/all_to_all | solution.py:386
  19.2 2.9 %copy-start.4 = (s32[2,8,6,128,128]{4,3,2,1,0:T(8,128)S(1)}, s32[2,8,6,128,128]{4,3,2,1,0:T(8,128)}, u32[]{:S(2)}) copy-start(s32[2,8,6,128,128]{4,3,2,1,0:T(8,128)} %counts) | copy-start | bytes 18874372
  22.1 5.1 %copy-start.9 = (s32[2,32,1]{1,2,0:T(1,128)S(1)}, s32[2,32,1]{1,2,0:T(1,128)}, u32[]{:S(2)}) copy-start(s32[2,32,1]{1,2,0:T(1,128)} %param.13) | copy-start | bytes 772
  25.7 5.4 %collective-permute-start.2 = (bf16[8,128,768]{2,1,0:T(8,128)(2,1)}, bf16[8,128,768]{2,1,0:T(8,128)(2,1)}, u32[]{:S(2)}, u32[]{:S(2)}) collective-permute-start(bf16[8,128,768]{2,1,0:T(8,128)(2,1)} %get-tuple-element.25.refs_1_), channel_id=1, source_target_pairs={{0,1},{1,0},{2,3},{3,2},{4,5},{5,4},{6,7},{7,6},{8,9},{9,8},{10,11... | collective-permute-start | bytes 4718600 | tf_op jit(solution)/shard_map/ppermute | solution.py:369
  25.9 4.3 %collective-permute-start.3 = (f32[8,128,128]{2,1,0:T(8,128)S(1)}, f32[8,128,128]{2,1,0:T(8,128)S(1)}, u32[]{:S(2)}, u32[]{:S(2)}) collective-permute-start(f32[8,128,128]{2,1,0:T(8,128)S(1)} %get-tuple-element.26.refs_2_), channel_id=1, source_target_pairs={{0,1},{1,0},{2,3},{3,2},{4,5},{5,4},{6,7},{7,6},{8,9},{9,8},{10,11... | collective-permute-start | bytes 1572872 | tf_op jit(solution)/shard_map/ppermute | solution.py:369
  26.2 0.8 copy-start.5
  27.3 2.8 %collective-permute-start = (s32[80]{0:T(128)S(1)}, s32[80]{0:T(128)S(1)}, u32[]{:S(2)}, u32[]{:S(2)}) collective-permute-start(s32[80]{0:T(128)S(1)} %pad_add_fusion), channel_id=1, source_target_pairs={{0,1},{1,0},{2,3},{3,2},{4,5},{5,4},{6,7},{7,6},{8,9},{9,8},{10,11... | collective-permute-start | bytes 968 | tf_op jit(solution)/shard_map/ppermute | solution.py:369
  30.2 0.8 copy-start.7
  31.0 1.7 copy-start.3
  32.7 1.1 copy-start.6
  33.8 1.0 copy-start.8
  47.4 2.9 %copy-start.1 = (bf16[4224,512]{1,0:T(8,128)(2,1)S(1)}, bf16[4224,512]{1,0:T(8,128)(2,1)}, u32[]{:S(2)}) copy-start(bf16[4224,512]{1,0:T(8,128)(2,1)} %all-gather.3.cloned.1.call-done) | copy-start | bytes 12976132
  49.9 2.0 collective-permute-start.4
  87.7 2.0 collective-permute-start.5
  125.2 2.0 collective-permute-start.6
  162.7 1.6 collective-permute-start.7
  193.7 2.7 %collective-permute-start.8 = (bf16[2,512,512]{2,1,0:T(8,128)(2,1)S(1)}, bf16[2,512,512]{2,1,0:T(8,128)(2,1)S(1)}, u32[]{:S(2)}, u32[]{:S(2)}) collective-permute-start(bf16[2,512,512]{2,1,0:T(8,128)(2,1)S(1)} %theirs.1), channel_id=1, source_target_pairs={{0,1},{1,0},{2,3},{3,2},{4,5},{5,4},{6,7},{7,6},{8,9},{9,8},{10,11... | collective-permute-start | bytes 3145736 | tf_op jit(solution)/shard_map/ppermute | solution.py:369
Sparse Core Ops, SparseCore 0:
  10.7 32.8 all-gather.2
